TPU v7x, 32 devices: a whole 2x2x4 slice. The times are simulated.
32 devices in a mesh: tri: 8 (over z, x), rhs: 2 (over y), split: 2 (over core).
Axes of the slice: x: 2, y: 2, z: 4, core: 2. Of those that a mesh axis runs over, the one named last changes fastest.
Arguments:
- residual: float32 [256, 16384], P('rhs', ('tri', 'split')), may hold values from -6 to 6
- attach: int32 [256], P('rhs'), may hold values from 0 to 16383
- vertices: float32 [3, 8192], replicated, may hold values from -3 to 3
- corners: int32 [3, 16384], replicated, may hold values from 0 to 8191
- layers: int32 [16384], replicated, may hold values from 0 to 2
Outputs:
- solution: float32 [256, 16384], P('rhs', ('tri', 'split'))
- remainder: float32 [256, 16384], P('rhs', ('tri', 'split'))
- direction: float32 [256, 16384], P('rhs', ('tri', 'split'))
All inputs are finite; a program needn't handle non-finite values.
Results may differ from a plain program's by a relative error of at most 0.011.
Values may be sent and summed in bfloat16 or wider, within the bound.
No kernel may reach another device: no remote copies, remote signals or barrier semaphores. Data moves between devices by JAX's collectives and lax.ppermute only.
A program may use at most 192 MiB of HBM per device.

v0:
```python
import math

import jax
import jax.numpy as jnp
from jax import lax
from jax.sharding import PartitionSpec as P

smooth_sq = 0.01
self_term = 1.0
inject = 3.0


def geometry(vertices, corners, layers):
    points = vertices[:, corners]
    centre = (points[:, 0] + points[:, 1] + points[:, 2]) / 3.0
    edge_one = points[:, 1] - points[:, 0]
    edge_two = points[:, 2] - points[:, 0]
    cross_x = edge_one[1] * edge_two[2] - edge_one[2] * edge_two[1]
    cross_y = edge_one[2] * edge_two[0] - edge_one[0] * edge_two[2]
    cross_z = edge_one[0] * edge_two[1] - edge_one[1] * edge_two[0]
    area_sq = cross_x * cross_x + cross_y * cross_y + cross_z * cross_z
    factor = jnp.where(layers == 0, 1.0, jnp.where(layers == 1, 0.3, 0.8)).astype(jnp.float32)
    weight = factor * (0.5 + area_sq / (1.0 + area_sq))
    return (centre, weight)


def kernel_tile(cent_rows, weight_rows, ids_rows, cent_cols, weight_cols, ids_cols, scale):
    delta = cent_rows[0][:, None] - cent_cols[0][None, :]
    dist_sq = delta * delta
    delta = cent_rows[1][:, None] - cent_cols[1][None, :]
    dist_sq = dist_sq + delta * delta
    delta = cent_rows[2][:, None] - cent_cols[2][None, :]
    dist_sq = dist_sq + delta * delta
    inverse = lax.rsqrt(dist_sq + smooth_sq)
    same = jnp.where(ids_rows[:, None] == ids_cols[None, :], self_term, 0.0)
    value = weight_rows[:, None] * weight_cols[None, :] * (inverse * scale + same)
    return value.astype(jnp.bfloat16)


def largest_block(width, limit):
    best = 1
    for cand in range(min(width, limit), 0, -1):
        if width % cand == 0:
            best = cand
            break
    return best


def body(residual, attach, vertices, corners, layers):
    highest = lax.Precision.HIGHEST
    columns, rows = residual.shape
    split_count = lax.axis_size("split")
    tri_pos = lax.axis_index("tri")
    split_pos = lax.axis_index("split")
    rhs_pos = lax.axis_index("rhs")
    first_row = (tri_pos * split_count + split_pos) * rows
    first_col = rhs_pos * columns
    centre, weight = geometry(vertices, corners, layers)
    scale = 1.0 / math.sqrt(centre.shape[1])
    my_ids = first_row + jnp.arange(rows, dtype=jnp.int32)
    my_cent = lax.dynamic_slice_in_dim(centre, first_row, rows, 1)
    my_weight = lax.dynamic_slice_in_dim(weight, first_row, rows, 0)
    current = residual + inject * (attach[:, None] == my_ids[None, :]).astype(jnp.float32)
    packed = current.astype(jnp.bfloat16)
    every_rows = lax.all_gather(current, "rhs", axis=0, tiled=True)

    def tile_for(cent_rows, weight_rows, ids_rows, begin, count):
        cent_cols = lax.dynamic_slice_in_dim(centre, begin, count, 1)
        weight_cols = lax.dynamic_slice_in_dim(weight, begin, count, 0)
        ids_cols = begin + jnp.arange(count, dtype=jnp.int32)
        return kernel_tile(
            cent_rows, weight_rows, ids_rows, cent_cols, weight_cols, ids_cols, scale
        )

    empty = jnp.zeros((columns, rows), jnp.float32)
    piece = jax.tree.map(
        lambda part: lax.all_gather(part, ("tri", "split"), axis=1, tiled=True), packed
    )
    start = jnp.int32(0)
    width = piece.shape[1]
    block = largest_block(width, 2048)

    def one_step(index, acc):
        begin = index * block
        source = lax.dynamic_slice_in_dim(piece, begin, block, 1)
        tile = tile_for(my_cent, my_weight, my_ids, start + begin, block)
        return acc + jnp.dot(source, tile.T, preferred_element_type=jnp.float32)

    image = lax.fori_loop(0, width // block, one_step, empty)
    every_image = lax.all_gather(image, "rhs", axis=0, tiled=True)
    part_gram = 0.5 * (
        jnp.dot(every_rows, image.T, precision=highest)
        + jnp.dot(every_image, current.T, precision=highest)
    )
    part_square = jnp.dot(every_rows, current.T, precision=highest)
    summed = lax.psum((part_gram, part_square), ("tri", "split"))
    gram, square = (
        lax.all_gather(summed[0], "rhs", axis=1, tiled=True),
        lax.all_gather(summed[1], "rhs", axis=1, tiled=True),
    )
    step = jax.scipy.linalg.cho_solve((jnp.linalg.cholesky(gram), True), square)
    step_cols = lax.dynamic_slice_in_dim(step, first_col, columns, 1)
    solution = jnp.dot(step_cols.T, every_rows, precision=highest)
    every_remainder = every_rows - jnp.dot(step.T, every_image, precision=highest)
    remainder = lax.dynamic_slice_in_dim(every_remainder, first_col, columns, 0)
    square_factor = jnp.linalg.cholesky(square)
    part_next = jnp.dot(every_remainder, remainder.T, precision=highest)
    next_cols = lax.psum(part_next, ("tri", "split"))
    turn_cols = jax.scipy.linalg.cho_solve((square_factor, True), next_cols)
    direction = remainder + jnp.dot(turn_cols.T, every_rows, precision=highest)
    return (solution, remainder, direction)


def solution(mesh):
    return jax.shard_map(
        body,
        mesh=mesh,
        in_specs=(P("rhs", ("tri", "split")), P("rhs"), P(), P(), P()),
        out_specs=(
            P("rhs", ("tri", "split")),
            P("rhs", ("tri", "split")),
            P("rhs", ("tri", "split")),
        ),
        check_vma=False,
    )
```

profile of v0, /device:TPU:0, one launch (start us, length us, event | category | flops | bytes accessed | tf_op | source)
XLA Modules:
  0.0 577.2 jit_solution(1117115148797959227)
XLA Ops:
  7.2 2.1 fusion.48
  9.4 0.7 all-gather.4.cloned.1.call-update
  10.1 3.4 copy.8
  13.5 1.0 compare_select_fusion
  14.8 164.1 %gather_fusion = f32[49152,3]{1,0:T(8,128)} fusion(f32[3,8192]{0,1:T(8,128)} %copy.8, s32[49152]{0:T(1024)S(1)} %broadcast_clamp_fusion), kind=kCustom, calls=%fused_computation | custom fusion | bytes 1376256 | tf_op jit(solution)/shard_map/gather | solution.py:14
  178.9 13.9 %copy.9 = f32[3,16384,3]{1,2,0:T(4,128)S(1)} copy(f32[3,16384,3]{2,1,0:T(8,128)} %bitcast.124) | data formatting | bytes 1179648 | tf_op jit(solution)/shard_map/gather | solution.py:14
  193.4 49.5 %while.18 = (s32[]{:T(128)}, f32[128,1024]{1,0:T(8,128)S(1)}, bf16[128,16384]{1,0:T(8,128)(2,1)}, f32[1024]{0:T(1024)S(1)}, f32[16384]{0:T(1024)S(1)}, /*index=5...) while((s32[]{:T(128)}, f32[128,1024]{1,0:T(8,128)S(1)}, ...), condition=%wide.region_1.2_spmd.clone, body=%wide.region_0.1_spmd.clone.sunk | while | flops 570690560 | bytes 1736945 | solution.py:89
  193.6 6.0 %fusion.89 = f32[128,1024]{1,0:T(8,128)S(1)} fusion(s32[2048]{0:T(1024)S(1)} %iota_add_fusion.5, f32[2048]{0:T(1024)S(1)} %bitcast.129, f32[1024]{0:T(1024)S(1)} %bitcast.131, f32[2048]{0:T(1024)S(1)} %bitcast.128, f32[1024]{0:T(1024)S(1)} %bitcast.132, f32[2048]{0:T(1024)S(1)} %bitcast.127, f32[1024]{0:T(1024)S(1)} %bitcast.130, ...), kind=kOutput, calls=%fused_computation.9.clone.1 | convolution fusion | flops 570687488 | bytes 1634309 | tf_op jit(solution)/shard_map/while/body/eval_jaxpr/dot_general | solution.py:87
  199.8 6.0 %fusion.89 = f32[128,1024]{1,0:T(8,128)S(1)} fusion(s32[2048]{0:T(1024)S(1)} %iota_add_fusion.5, f32[2048]{0:T(1024)S(1)} %bitcast.129, f32[1024]{0:T(1024)S(1)} %bitcast.131, f32[2048]{0:T(1024)S(1)} %bitcast.128, f32[1024]{0:T(1024)S(1)} %bitcast.132, f32[2048]{0:T(1024)S(1)} %bitcast.127, f32[1024]{0:T(1024)S(1)} %bitcast.130, ...), kind=kOutput, calls=%fused_computation.9.clone.1 | convolution fusion | flops 570687488 | bytes 1634309 | tf_op jit(solution)/shard_map/while/body/eval_jaxpr/dot_general | solution.py:87
  206.0 6.0 %fusion.89 = f32[128,1024]{1,0:T(8,128)S(1)} fusion(s32[2048]{0:T(1024)S(1)} %iota_add_fusion.5, f32[2048]{0:T(1024)S(1)} %bitcast.129, f32[1024]{0:T(1024)S(1)} %bitcast.131, f32[2048]{0:T(1024)S(1)} %bitcast.128, f32[1024]{0:T(1024)S(1)} %bitcast.132, f32[2048]{0:T(1024)S(1)} %bitcast.127, f32[1024]{0:T(1024)S(1)} %bitcast.130, ...), kind=kOutput, calls=%fused_computation.9.clone.1 | convolution fusion | flops 570687488 | bytes 1634309 | tf_op jit(solution)/shard_map/while/body/eval_jaxpr/dot_general | solution.py:87
  212.2 6.0 %fusion.89 = f32[128,1024]{1,0:T(8,128)S(1)} fusion(s32[2048]{0:T(1024)S(1)} %iota_add_fusion.5, f32[2048]{0:T(1024)S(1)} %bitcast.129, f32[1024]{0:T(1024)S(1)} %bitcast.131, f32[2048]{0:T(1024)S(1)} %bitcast.128, f32[1024]{0:T(1024)S(1)} %bitcast.132, f32[2048]{0:T(1024)S(1)} %bitcast.127, f32[1024]{0:T(1024)S(1)} %bitcast.130, ...), kind=kOutput, calls=%fused_computation.9.clone.1 | convolution fusion | flops 570687488 | bytes 1634309 | tf_op jit(solution)/shard_map/while/body/eval_jaxpr/dot_general | solution.py:87
  218.4 6.0 %fusion.89 = f32[128,1024]{1,0:T(8,128)S(1)} fusion(s32[2048]{0:T(1024)S(1)} %iota_add_fusion.5, f32[2048]{0:T(1024)S(1)} %bitcast.129, f32[1024]{0:T(1024)S(1)} %bitcast.131, f32[2048]{0:T(1024)S(1)} %bitcast.128, f32[1024]{0:T(1024)S(1)} %bitcast.132, f32[2048]{0:T(1024)S(1)} %bitcast.127, f32[1024]{0:T(1024)S(1)} %bitcast.130, ...), kind=kOutput, calls=%fused_computation.9.clone.1 | convolution fusion | flops 570687488 | bytes 1634309 | tf_op jit(solution)/shard_map/while/body/eval_jaxpr/dot_general | solution.py:87
  224.6 6.0 %fusion.89 = f32[128,1024]{1,0:T(8,128)S(1)} fusion(s32[2048]{0:T(1024)S(1)} %iota_add_fusion.5, f32[2048]{0:T(1024)S(1)} %bitcast.129, f32[1024]{0:T(1024)S(1)} %bitcast.131, f32[2048]{0:T(1024)S(1)} %bitcast.128, f32[1024]{0:T(1024)S(1)} %bitcast.132, f32[2048]{0:T(1024)S(1)} %bitcast.127, f32[1024]{0:T(1024)S(1)} %bitcast.130, ...), kind=kOutput, calls=%fused_computation.9.clone.1 | convolution fusion | flops 570687488 | bytes 1634309 | tf_op jit(solution)/shard_map/while/body/eval_jaxpr/dot_general | solution.py:87
  230.8 6.0 %fusion.89 = f32[128,1024]{1,0:T(8,128)S(1)} fusion(s32[2048]{0:T(1024)S(1)} %iota_add_fusion.5, f32[2048]{0:T(1024)S(1)} %bitcast.129, f32[1024]{0:T(1024)S(1)} %bitcast.131, f32[2048]{0:T(1024)S(1)} %bitcast.128, f32[1024]{0:T(1024)S(1)} %bitcast.132, f32[2048]{0:T(1024)S(1)} %bitcast.127, f32[1024]{0:T(1024)S(1)} %bitcast.130, ...), kind=kOutput, calls=%fused_computation.9.clone.1 | convolution fusion | flops 570687488 | bytes 1634309 | tf_op jit(solution)/shard_map/while/body/eval_jaxpr/dot_general | solution.py:87
  237.0 6.0 %fusion.89 = f32[128,1024]{1,0:T(8,128)S(1)} fusion(s32[2048]{0:T(1024)S(1)} %iota_add_fusion.5, f32[2048]{0:T(1024)S(1)} %bitcast.129, f32[1024]{0:T(1024)S(1)} %bitcast.131, f32[2048]{0:T(1024)S(1)} %bitcast.128, f32[1024]{0:T(1024)S(1)} %bitcast.132, f32[2048]{0:T(1024)S(1)} %bitcast.127, f32[1024]{0:T(1024)S(1)} %bitcast.130, ...), kind=kOutput, calls=%fused_computation.9.clone.1 | convolution fusion | flops 570687488 | bytes 1634309 | tf_op jit(solution)/shard_map/while/body/eval_jaxpr/dot_general | solution.py:87
  243.0 0.8 copy-done.4
  243.9 3.1 fusion.53
  247.0 2.5 fusion.52
  249.6 18.4 %all-gather.8.cloned.1.call-done = f32[256,1024]{1,0:T(8,128)} async-done(((f32[128,1024]{1,0:T(8,128)}), f32[256,1024]{1,0:T(8,128)}) %all-gather.8.cloned.1.call-update) | async-done | bytes 1048592 | tf_op jit(solution)/shard_map/all_gather | solution.py:90
  267.9 3.1 fusion.11
  271.2 89.5 %all-reduce.7.cloned.1.call-done = (f32[256,128]{0,1:T(8,128)}, f32[256,128]{0,1:T(8,128)}) async-done(((f32[256,128]{0,1:T(8,128)}, f32[256,128]{0,1:T(8,128)}), (f32[256,128]{0,1:T(8,128)}, f32[256,128]{0,1:T(8,128)})) %all-reduce.7.cloned.1.call-update) | async-done | bytes 262160 | tf_op jit(solution)/shard_map/psum | solution.py:96
  360.7 7.0 %all_gather.19 = f32[256,256]{0,1:T(8,128)S(1)} all-gather(f32[256,128]{0,1:T(8,128)} %get-tuple-element.222), channel_id=1, replica_groups=mesh['tri'=8,'rhs'=2,'split'=2] {'rhs'}, dimensions={1}, use_global_device_ids=true | all-gather | bytes 393216 | tf_op jit(solution)/shard_map/all_gather | solution.py:99
  367.8 11.7 %cholesky.164 = f32[128,128]{1,0:T(8,128)S(1)} custom-call(f32[128,128]{1,0:T(8,128)S(1)} %cholesky.197), custom_call_target="Cholesky" | custom-call | tf_op jit(solution)/shard_map/jit(cholesky)/cholesky | solution.py:106
  379.6 9.8 %custom-call.27 = f32[1,128,128]{1,2,0:T(8,128)S(1)} custom-call(f32[1,128,128]{2,1,0:T(8,128)S(1)} %get-tuple-element.242), custom_call_target="InvertDiagBlocksLowerTriangular" | custom-call | tf_op jit(solution)/shard_map/jit(cholesky)/cholesky | solution.py:106
  389.9 11.7 %cholesky.181 = f32[128,128]{1,0:T(8,128)S(1)} custom-call(f32[128,128]{1,0:T(8,128)S(1)} %convolution_subtract_fusion.5), custom_call_target="Cholesky" | custom-call | tf_op jit(solution)/shard_map/jit(cholesky)/cholesky | solution.py:106
  401.7 0.6 compare_reduce_fusion
  403.7 4.0 while.17
  403.8 0.6 fusion.86
  404.3 1.4 bitcast_dynamic-update-slice_fusion.5
  406.3 1.4 bitcast_dynamic-update-slice_fusion.5
  407.8 6.2 %all_gather.18 = f32[256,256]{0,1:T(8,128)S(1)} all-gather(f32[256,128]{0,1:T(8,128)} %get-tuple-element.223), channel_id=1, replica_groups=mesh['tri'=8,'rhs'=2,'split'=2] {'rhs'}, dimensions={1}, use_global_device_ids=true | all-gather | bytes 393216 | tf_op jit(solution)/shard_map/all_gather | solution.py:98
  414.2 11.7 %cholesky.130 = f32[128,128]{1,0:T(8,128)S(1)} custom-call(f32[128,128]{1,0:T(8,128)S(1)} %cholesky.194), custom_call_target="Cholesky" | custom-call | tf_op jit(solution)/shard_map/jit(cholesky)/cholesky | solution.py:101
  426.0 9.8 %custom-call.26 = f32[1,128,128]{1,2,0:T(8,128)S(1)} custom-call(f32[1,128,128]{2,1,0:T(8,128)S(1)} %get-tuple-element.246), custom_call_target="InvertDiagBlocksLowerTriangular" | custom-call | tf_op jit(solution)/shard_map/jit(cholesky)/cholesky | solution.py:101
  436.3 11.7 %cholesky.147 = f32[128,128]{1,0:T(8,128)S(1)} custom-call(f32[128,128]{1,0:T(8,128)S(1)} %convolution_subtract_fusion.6), custom_call_target="Cholesky" | custom-call | tf_op jit(solution)/shard_map/jit(cholesky)/cholesky | solution.py:101
  448.0 0.6 compare_reduce_fusion.2
  450.0 4.3 while.16
  450.9 1.4 bitcast_dynamic-update-slice_fusion.4
  452.3 0.6 fusion.85
  452.9 1.4 bitcast_dynamic-update-slice_fusion.4
  454.3 19.7 %custom-call.22 = f32[2,128,128]{1,2,0:T(8,128)S(1)} custom-call(f32[2,128,128]{2,1,0:T(8,128)S(1)} %get-tuple-element.151), custom_call_target="InvertDiagBlocksLowerTriangular" | custom-call | tf_op jit(solution)/shard_map/jit(_cho_solve)/triangular_solve | solution.py:101
  475.9 1.0 convolution_subtract_fusion
  477.0 1.6 fusion.54
  478.7 1.5 fusion.17
  480.2 20.5 %custom-call.23 = f32[2,128,128]{1,2,0:T(8,128)S(1)} custom-call(f32[2,128,128]{2,1,0:T(8,128)} %copy-done.5), custom_call_target="InvertDiagBlocksLowerTriangular" | custom-call | tf_op jit(solution)/shard_map/jit(_cho_solve)/triangular_solve | solution.py:109
  500.7 64.9 %all-reduce.5.cloned.1.call-done = f32[256,128]{1,0:T(8,128)} async-done(((f32[256,128]{1,0:T(8,128)}), f32[256,128]{1,0:T(8,128)}) %all-reduce.5.cloned.1.call-update) | async-done | bytes 131088 | tf_op jit(solution)/shard_map/psum | solution.py:108
  565.5 1.1 fusion.26
  566.7 1.0 convolution_subtract_fusion.4
  568.7 1.5 convolution_add_fusion
  (112 shorter events, 7.9 us)
Async XLA Ops:
  7.2 186.2 %all-gather.6.cloned.1.call-start = ((), (), s32[]{:S(2)}) async-start(), calls=%async_computation.1 | async-start | bytes 4456448 | tf_op jit(solution)/shard_map/all_gather | solution.py:77
  9.3 234.6 %all-gather.4.cloned.1.call-start = ((), (), s32[]{:S(2)}) async-start(), calls=%async_computation | async-start | bytes 1572864 | tf_op jit(solution)/shard_map/all_gather | solution.py:65
  10.1 257.9 %all-gather.8.cloned.1.call-start = ((), (), s32[]{:S(2)}) async-start(), calls=%async_computation.2 | async-start | bytes 1572864 | tf_op jit(solution)/shard_map/all_gather | solution.py:90
  178.9 14.4 %copy-start.6 = (s32[16384]{0:T(1024)S(1)}, s32[16384]{0:T(1024)}, u32[]{:S(2)}) copy-start(s32[16384]{0:T(1024)} %param.12) | copy-start | bytes 196612
  193.4 50.5 %copy-start.1 = (f32[128,1024]{1,0:T(8,128)S(1)}, f32[128,1024]{1,0:T(8,128)}, u32[]{:S(2)}) copy-start(f32[128,1024]{1,0:T(8,128)} %get-tuple-element.225) | copy-start | bytes 1572868
  243.0 0.8 copy-start.4
  243.8 116.9 %all-reduce.7.cloned.1.call-start = ((), (), s32[]{:S(2)}) async-start(), calls=%async_computation.4 | async-start | bytes 524288 | tf_op jit(solution)/shard_map/psum | solution.py:96
  243.9 232.0 %copy-start = (f32[256,1024]{1,0:T(8,128)S(1)}, f32[256,1024]{1,0:T(8,128)}, u32[]{:S(2)}) copy-start(f32[256,1024]{1,0:T(8,128)} %all-gather.4.cloned.1.call-done) | copy-start | bytes 3145732
  267.9 207.9 %copy-start.3 = (f32[256,1024]{1,0:T(8,128)S(1)}, f32[256,1024]{1,0:T(8,128)}, u32[]{:S(2)}) copy-start(f32[256,1024]{1,0:T(8,128)} %all-gather.8.cloned.1.call-done) | copy-start | bytes 3145732
  271.1 294.4 %all-reduce.5.cloned.1.call-start = ((), (), s32[]{:S(2)}) async-start(), calls=%async_computation.3 | async-start | bytes 262144 | tf_op jit(solution)/shard_map/psum | solution.py:108
  407.7 6.4 %copy-start.5 = (f32[2,128,128]{2,1,0:T(8,128)}, f32[2,128,128]{2,1,0:T(8,128)S(1)}, u32[]{:S(2)}) copy-start(f32[2,128,128]{2,1,0:T(8,128)S(1)} %get-tuple-element.159) | copy-start | bytes 393220
  477.0 93.3 %copy-start.2 = (f32[128,1024]{1,0:T(8,128)}, f32[128,1024]{1,0:T(8,128)S(1)}, u32[]{:S(2)}) copy-start(f32[128,1024]{1,0:T(8,128)S(1)} %constant_dynamic-slice_fusion.3) | copy-start | bytes 1572868
Sparse Core Ops, SparseCore 0:
  10.8 53.2 all-gather.5
  66.2 19.7 all-gather.3
  243.9 23.9 all-gather.7
  271.8 88.8 all-reduce.6
  478.8 86.7 all-reduce.4
where the time goes:
time: 587 us; the launch traced here: 577 us
  local copies, waits for them, and re-layouts  192 us (33%)
  waiting for transfers between devices  174 us (30%)
  other arithmetic  112 us (19%)
  matrix products  68.4 us (12%)
  between operations  17.3 us (3%)
  blocking collectives  13.2 us (2%)
    gather x2, local copies, waits for them, and re-layouts, geometry(): points = vertices[:, corners]  178 us
    psum x1, waiting for transfers between devices, body(): summed = lax.psum((part_gram, part_square), ('tri', 'split'))  89.5 us
    psum x1, waiting for transfers between devices, body(): next_cols = lax.psum(part_next, ('tri', 'split'))  64.9 us
    another operation x9, other arithmetic, body(): step = jax.scipy.linalg.cho_solve((jnp.linalg.cholesky(gram), True), square)  53.7 us
    dot_general x8, matrix products, one_step(): return acc + jnp.dot(source, tile.T, preferred_element_type=jnp.float32)  47.9 us
    another operation x6, other arithmetic, body(): square_factor = jnp.linalg.cholesky(square)  33.9 us
    another operation x2, other arithmetic, body(): turn_cols = jax.scipy.linalg.cho_solve((square_factor, True), next_cols)  20.5 us
    all_gather x1, waiting for transfers between devices, body(): every_image = lax.all_gather(image, 'rhs', axis=0, tiled=True)  18.4 us
  transfers between devices with their start and end apart: 5, of which 3 were waited for; matrix products, arithmetic and copies ran while one was open for 45% of the time, Pallas kernels for 0%

commit v1 on v0

v1 whole, which is shorter than its diff:
```python
import functools
import math

import jax
import jax.numpy as jnp
from jax import lax
from jax.experimental import pallas as pl
from jax.experimental.pallas import tpu as pltpu
from jax.sharding import PartitionSpec as P

smooth_sq = 0.01
self_term = 1.0
inject = 3.0
f32 = jnp.float32
bf16 = jnp.bfloat16
LANES = 128
FEATURES = 32
PAIRS = ((0, 0), (0, 1), (1, 0), (1, 1), (0, 2), (2, 0))
VMEM = pl.BlockSpec(memory_space=pltpu.VMEM)
SMEM = pl.BlockSpec(memory_space=pltpu.SMEM)


def dot(a, b, ca, cb, precision=None):
    return lax.dot_general(
        a, b, (((ca,), (cb,)), ((), ())), precision=precision, preferred_element_type=f32
    )


def exact_dot(a, b, ca, cb):
    return dot(a, b, ca, cb, lax.Precision.HIGHEST)


def params():
    return pltpu.CompilerParams(vmem_limit_bytes=48 * 1024 * 1024)


def pieces_of(value):
    high = value.astype(bf16).astype(f32)
    rest = value - high
    middle = rest.astype(bf16).astype(f32)
    return (high, middle, rest - middle)


def geometry_kernel(scale, blocks_ref, table_ref, corners_ref, layers_ref, a_ref, b_ref, diag_ref, a_rows, b_rows):
    count = corners_ref.shape[1]
    tops = table_ref.shape[1]
    table = [[part.astype(bf16) for part in pieces_of(table_ref[axis])] for axis in range(3)]
    top_iota = lax.broadcasted_iota(jnp.int32, (tops, count), 0)
    low_iota = lax.broadcasted_iota(jnp.int32, (LANES, count), 0)
    points = []
    for corner in range(3):
        index = corners_ref[corner : corner + 1, :]
        top = jnp.where(top_iota == (index >> 7), 1.0, 0.0).astype(bf16)
        low = low_iota == (index & (LANES - 1))
        point = []
        for axis in range(3):
            high, middle, rest = (dot(part, top, 0, 0) for part in table[axis])
            point.append(jnp.sum(jnp.where(low, (high + middle) + rest, 0.0), axis=0, keepdims=True))
        points.append(point)
    p0, p1, p2 = points
    centre = [(p0[k] + p1[k] + p2[k]) / 3.0 for k in range(3)]
    e1 = [p1[k] - p0[k] for k in range(3)]
    e2 = [p2[k] - p0[k] for k in range(3)]
    cross_x = e1[1] * e2[2] - e1[2] * e2[1]
    cross_y = e1[2] * e2[0] - e1[0] * e2[2]
    cross_z = e1[0] * e2[1] - e1[1] * e2[0]
    area_sq = cross_x * cross_x + cross_y * cross_y + cross_z * cross_z
    layers = layers_ref[...]
    factor = jnp.where(layers == 0, 1.0, jnp.where(layers == 1, 0.3, 0.8)).astype(f32)
    weight = factor * (0.5 + area_sq / (1.0 + area_sq))
    unit = 1.0 / (scale * (weight * weight))
    norm = centre[0] * centre[0] + centre[1] * centre[1] + centre[2] * centre[2]
    a_side = [unit * norm, unit] + [unit * c for c in centre]
    b_side = [unit, unit * (norm + smooth_sq)] + [-2.0 * unit * c for c in centre]
    a_parts = [pieces_of(value) for value in a_side]
    b_parts = [pieces_of(value) for value in b_side]
    row = 0
    for a_piece, b_piece in PAIRS:
        for term in range(5):
            a_rows[row : row + 1, :] = a_parts[term][a_piece]
            b_rows[row : row + 1, :] = b_parts[term][b_piece]
            row += 1
    blank = jnp.zeros((FEATURES - row, count), f32)
    a_rows[row:, :] = blank
    b_rows[row:, :] = blank
    a_ref[...] = a_rows[...].astype(bf16)
    b_ref[...] = b_rows[...].astype(bf16)
    diag_ref[...] = weight * weight * (lax.rsqrt(jnp.full_like(weight, smooth_sq)) * scale + self_term)


def geometry(blocks, table, corners, layers, count, scale):
    n = blocks.shape[0]
    tops = table.shape[1]
    feature = jax.ShapeDtypeStruct((n, FEATURES, count), bf16)
    return pl.pallas_call(
        functools.partial(geometry_kernel, scale),
        grid_spec=pltpu.PrefetchScalarGridSpec(
            num_scalar_prefetch=1,
            grid=(n,),
            in_specs=[
                pl.BlockSpec((3, tops, LANES), lambda g, blk: (0, 0, 0)),
                pl.BlockSpec((3, count), lambda g, blk: (0, blk[g])),
                pl.BlockSpec((1, count), lambda g, blk: (0, blk[g])),
            ],
            out_specs=[
                pl.BlockSpec((None, FEATURES, count), lambda g, blk: (g, 0, 0)),
                pl.BlockSpec((None, FEATURES, count), lambda g, blk: (g, 0, 0)),
                pl.BlockSpec((None, 1, count), lambda g, blk: (g, 0, 0)),
            ],
            scratch_shapes=[pltpu.VMEM((FEATURES, count), f32), pltpu.VMEM((FEATURES, count), f32)],
        ),
        out_shape=(feature, feature, jax.ShapeDtypeStruct((n, 1, count), f32)),
        compiler_params=params(),
        name="geometry",
    )(blocks, table, corners, layers[None, :])


def image_kernel(sources, has_start, has_diag, *refs):
    refs = list(refs)
    densities = [refs.pop(0) for _ in range(sources)]
    a_refs = [refs.pop(0) for _ in range(sources)]
    b_ref = refs.pop(0)
    diag_ref = refs.pop(0) if has_diag else None
    start_ref = refs.pop(0) if has_start else None
    out_ref = refs.pop(0)
    targets, columns, count = out_ref.shape
    chunk = min(512, count)

    def one(target, with_diag):
        b = b_ref[target]
        acc = start_ref[target] if has_start else jnp.zeros((columns, count), f32)
        for density, a_ref in zip(densities, a_refs):
            for begin in range(0, count, chunk):
                tile = lax.rsqrt(dot(a_ref[:, begin : begin + chunk], b, 0, 0))
                if with_diag:
                    rows = begin + lax.broadcasted_iota(jnp.int32, tile.shape, 0)
                    cols = lax.broadcasted_iota(jnp.int32, tile.shape, 1)
                    tile = jnp.where(rows == cols, diag_ref[...], tile)
                acc = acc + dot(density[:, begin : begin + chunk], tile.astype(bf16), 1, 0)
        out_ref[target] = acc

    if has_diag:
        one(0, True)
    if targets > int(has_diag):

        @pl.loop(int(has_diag), targets)
        def _(target):
            one(target, False)


def image_part(densities, a_side, b_side, start=None, diag=None):
    columns, count = densities[0].shape
    targets = b_side.shape[0]
    operands = [*densities, *a_side, b_side]
    if diag is not None:
        operands.append(diag)
    if start is not None:
        operands.append(start)
    entries = len(densities) * count * targets * count
    return pl.pallas_call(
        functools.partial(image_kernel, len(densities), start is not None, diag is not None),
        in_specs=[VMEM] * len(operands),
        out_specs=VMEM,
        out_shape=jax.ShapeDtypeStruct((targets, columns, count), f32),
        compiler_params=params(),
        cost_estimate=pl.CostEstimate(
            flops=2 * entries * (columns + FEATURES), bytes_accessed=8 * targets * columns * count, transcendentals=entries
        ),
        name="image_part",
    )(*operands)


def gram_kernel(ranks, place_ref, *refs):
    currents, images = refs[:ranks], refs[ranks : 2 * ranks]
    current_ref, image_ref, sums_ref = refs[2 * ranks :]
    columns, count = currents[0].shape
    for rank in range(ranks):
        at = pl.ds(pl.multiple_of(place_ref[rank] * columns, columns), columns)
        current_ref[at, :] = currents[rank][...]
        image_ref[at, :] = images[rank][...]
    width = count // ranks
    mine = pl.ds(pl.multiple_of(place_ref[0] * width, width), width)
    current = current_ref[:, mine]
    image = image_ref[:, mine]
    total = ranks * columns
    sums_ref[:total] = exact_dot(current, image, 1, 1)
    sums_ref[total : 2 * total] = exact_dot(current, current, 1, 1)
    sums_ref[2 * total :] = exact_dot(image, image, 1, 1)


def gram_sums(places, currents, images):
    ranks = len(currents)
    columns, count = currents[0].shape
    whole = jax.ShapeDtypeStruct((ranks * columns, count), f32)
    return pl.pallas_call(
        functools.partial(gram_kernel, ranks),
        in_specs=[SMEM] + [VMEM] * (2 * ranks),
        out_specs=[VMEM] * 3,
        out_shape=(whole, whole, jax.ShapeDtypeStruct((3 * ranks * columns, ranks * columns), f32)),
        compiler_params=params(),
        name="gram",
    )(places, *currents, *images)


def invert_small(block):
    size = block.shape[0]
    row_at = lax.broadcasted_iota(jnp.int32, block.shape, 0)
    col_at = lax.broadcasted_iota(jnp.int32, block.shape, 1)
    for step in range(size):
        inverse = 1.0 / block[step : step + 1, step : step + 1]
        row = jnp.where(col_at[:1] == step, 1.0, block[step : step + 1, :]) * inverse
        col = block[:, step : step + 1]
        block = jnp.where(row_at == step, row, jnp.where(col_at == step, 0.0, block) - col * row)
    return block


def sweep(ref, begin, size):
    total = ref.shape[0]
    panel = ref[begin : begin + size, :]
    inverse = invert_small(panel[:, begin : begin + size])
    row_at = lax.broadcasted_iota(jnp.int32, panel.shape, 0)
    col_at = lax.broadcasted_iota(jnp.int32, panel.shape, 1)
    inside = (col_at >= begin) & (col_at < begin + size)
    eye = jnp.where(col_at == row_at + begin, 1.0, 0.0)
    row = exact_dot(inverse, jnp.where(inside, eye, panel), 1, 0)
    signed = jnp.where(col_at < begin, -panel, panel)
    update = exact_dot(signed, row, 0, 0)
    lanes = lax.broadcasted_iota(jnp.int32, (total, total), 1)
    ref[...] = jnp.where((lanes >= begin) & (lanes < begin + size), 0.0, ref[...]) - update
    ref[begin : begin + size, :] = row


def solve_kernel(columns, size, place_ref, sums_ref, step_ref, turn_ref, gram_inv, square_inv, step_all):
    total = sums_ref.shape[1]
    cross = sums_ref[:total]
    gram_inv[...] = 0.5 * (cross + cross.T)
    square_inv[...] = sums_ref[total : 2 * total]
    for begin in range(0, total, size):
        sweep(gram_inv, begin, size)
        sweep(square_inv, begin, size)
    mine = pl.ds(pl.multiple_of(place_ref[0] * columns, columns), columns)
    step_all[...] = exact_dot(sums_ref[total : 2 * total], gram_inv[...], 1, 0)
    step = step_all[mine, :]
    step_ref[...] = step
    square_rows = sums_ref[pl.ds(pl.multiple_of(total + place_ref[0] * columns, columns), columns), :]
    cross_rows = sums_ref[mine, :]
    left = exact_dot(step, sums_ref[2 * total :], 1, 0) - cross_rows
    following = square_rows - exact_dot(step, sums_ref[:total], 1, 1) + exact_dot(left, step_all[...], 1, 1)
    turn_ref[...] = exact_dot(following, square_inv[...], 1, 0)


def solve(places, sums, columns):
    total = sums.shape[1]
    square = pltpu.VMEM((total, total), f32)
    rows = jax.ShapeDtypeStruct((columns, total), f32)
    return pl.pallas_call(
        functools.partial(solve_kernel, columns, 32),
        in_specs=[SMEM, VMEM],
        out_specs=[VMEM] * 2,
        out_shape=(rows, rows),
        scratch_shapes=[square, square, square],
        compiler_params=params(),
        name="solve",
    )(places, sums)


def finish_kernel(mine_ref, current_ref, image_ref, step_ref, turn_ref, solution_ref, remainder_ref, direction_ref):
    current = current_ref[...]
    step = step_ref[...]
    solution_ref[...] = exact_dot(step, current, 1, 0)
    remainder = mine_ref[...] - exact_dot(step, image_ref[...], 1, 0)
    remainder_ref[...] = remainder
    direction_ref[...] = remainder + exact_dot(turn_ref[...], current, 1, 0)


def finish(mine, current, image, step, turn):
    out = jax.ShapeDtypeStruct(mine.shape, f32)
    return pl.pallas_call(
        finish_kernel,
        in_specs=[VMEM] * 5,
        out_specs=[VMEM] * 3,
        out_shape=(out, out, out),
        compiler_params=params(),
        name="finish",
    )(mine, current, image, step, turn)


def swap(value, axis, bits):
    size = lax.axis_size(axis)
    return lax.ppermute(value, axis, [(at, at ^ bits) for at in range(size)])


def in_order(parts, place):
    bit = 1
    while bit < len(parts):
        flip = (place & bit) != 0
        parts = [jnp.where(flip, parts[at ^ bit], parts[at]) for at in range(len(parts))]
        bit *= 2
    return parts


def all_sum(value, ranks, groups, near, core, place):
    rows = value.shape[0]
    half = rows // 2
    keep = lax.dynamic_slice_in_dim(value, core * half, half, 0)
    give = lax.dynamic_slice_in_dim(value, (1 - core) * half, half, 0)
    value = keep + swap(give, "split", 1)
    cuts = 2 * ranks
    share = half // cuts
    got = []
    for bits in range(1, cuts):
        give = lax.dynamic_slice_in_dim(value, (place ^ bits) * share, share, 0)
        got.append(pair_swap(give, bits, ranks))
    value = sum(got, lax.dynamic_slice_in_dim(value, place * share, share, 0))
    value = sum([swap(value, "tri", 2 * k) for k in range(1, groups)], value)
    parts = [value] + [pair_swap(value, bits, ranks) for bits in range(1, cuts)]
    value = jnp.concatenate(in_order(parts, place), axis=0)
    return jnp.concatenate(in_order([value, swap(value, "split", 1)], core), axis=0)


def pair_swap(value, bits, ranks):
    rank_bits, tri_bit = bits % ranks, bits // ranks
    if tri_bit == 0:
        return swap(value, "rhs", rank_bits)
    if rank_bits == 0:
        return swap(value, "tri", 1)
    count = lax.axis_size("tri")
    perm = [
        (tri * ranks + rank, (tri ^ 1) * ranks + (rank ^ rank_bits)) for tri in range(count) for rank in range(ranks)
    ]
    return lax.ppermute(value, ("tri", "rhs"), perm)


def body(residual, attach, vertices, corners, layers):
    columns, count = residual.shape
    tris, ranks, cores = lax.axis_size("tri"), lax.axis_size("rhs"), lax.axis_size("split")
    tri, rank, core = lax.axis_index("tri"), lax.axis_index("rhs"), lax.axis_index("split")
    near = min(4, tris)
    groups = tris // near
    scale = 1.0 / math.sqrt(corners.shape[1])

    my_ids = (tri * cores + core) * count + jnp.arange(count, dtype=jnp.int32)
    current = residual + inject * (attach[:, None] == my_ids[None, :]).astype(f32)
    packed = current.astype(bf16)
    packed_near = [swap(packed, "tri", bits) for bits in range(1, near)]
    currents = [current] + [swap(current, "rhs", bits) for bits in range(1, ranks)]

    sources = [(tri ^ bits) * cores + core for bits in range(near)]
    targets = [(tri ^ (near * far)) * cores + (core ^ other) for far in range(groups) for other in range(cores)]
    blocks = jnp.stack([*sources, *targets]).astype(jnp.int32)
    table = vertices.reshape(3, vertices.shape[1] // LANES, LANES)
    a_all, b_all, diag = geometry(blocks, table, corners, layers, count, scale)
    a_side = [a_all[bits] for bits in range(near)]
    b_side = b_all[near:]

    first = image_part([packed], a_side[:1], b_side, diag=diag[0])
    image_far = []
    if groups > 1:
        far = image_part(packed_near, a_side[1:], b_side[cores:], start=first[cores:])
        far = far.reshape(groups - 1, cores, columns, count)
        for at in range(1, groups):
            part = far[at - 1, 0] + swap(far[at - 1, 1].astype(bf16), "split", 1).astype(f32)
            image_far.append(swap(part.astype(bf16), "tri", near * at))
    own = image_part(packed_near, a_side[1:], b_side[:cores], start=first[:cores])
    image = own[0] + swap(own[1], "split", 1)
    for part in image_far:
        image = image + part.astype(f32)

    images = [image] + [swap(image, "rhs", bits) for bits in range(1, ranks)]
    places = jnp.stack([rank ^ bits for bits in range(ranks)]).astype(jnp.int32)
    every_current, every_image, sums = gram_sums(places, currents, images)
    sums = all_sum(sums, ranks, tris // 2, near, core, (tri & 1) * ranks + rank)
    step, turn = solve(places, sums, columns)
    return finish(current, every_current, every_image, step, turn)


def solution(mesh):
    return jax.shard_map(
        body,
        mesh=mesh,
        in_specs=(P("rhs", ("tri", "split")), P("rhs"), P(), P(), P()),
        out_specs=(
            P("rhs", ("tri", "split")),
            P("rhs", ("tri", "split")),
            P("rhs", ("tri", "split")),
        ),
        check_vma=False,
    )
```

time: 587 us -> 152 us (0.26); the launches traced: 577 us -> 151 us
  local copies, waits for them, and re-layouts: 192 us -> 8.41 us
  waiting for transfers between devices: 174 us -> 41 us
  other arithmetic: 112 us -> 3.66 us
  Pallas kernels: 0 us -> 73.6 us
  matrix products: 68.4 us -> 0 us
  starting transfers between devices: 0.2 us -> 23.6 us
  between operations: 17.3 us -> 0.92 us
  blocking collectives: 13.2 us -> 0 us
    gather x2 -> x0, local copies, waits for them, and re-layouts: 178 us -> none  [geometry(): points = vertices[:, corners]]
    psum x2 -> x0, waiting for transfers between devices: 154 us -> none  [the longest x1 89.5 us: body(): summed = lax.psum((part_gram, part_square), ('tri', 'split'))]
    another operation x17 -> x1, other arithmetic: 108 us -> 0.07 us  [body(): places = jnp.stack([rank ^ bits for bits in range(ranks)]).astype(jnp.int32)]
    pallas_call x0 -> x7, Pallas kernels: none -> 73.6 us  [the longest x1 33.8 us: solve(): pl.pallas_call(functools.partial(solve_kernel, columns, 32), in_specs=[SM...]
    dot_general x15 -> x0, matrix products: 62.4 us -> none  [the longest x8 47.9 us: one_step(): return acc + jnp.dot(source, tile.T, preferred_element_type=jnp.float32)]
    ppermute x0 -> x19, waiting for transfers between devices: none -> 41 us  [the longest x17 36.5 us: swap(): return lax.ppermute(value, axis, [(at, at ^ bits) for at in range(size)])]
    ppermute x0 -> x19, starting transfers between devices: none -> 23.6 us  [the longest x17 20.6 us: swap(): return lax.ppermute(value, axis, [(at, at ^ bits) for at in range(size)])]
    all_gather x3 -> x0, waiting for transfers between devices: 18.4 us -> none  [the longest x1 18.4 us: body(): every_image = lax.all_gather(image, 'rhs', axis=0, tiled=True)]
  transfers between devices with their start and end apart: 5 -> 19, of which waited for: 3 -> 11; matrix products, arithmetic and copies ran while one was open for 45% -> 1% of each run, Pallas kernels for 0% -> 20%
where the time goes in v1:
time: 152 us; the launch traced here: 151 us
  Pallas kernels  73.6 us (48%)
  waiting for transfers between devices  41 us (27%)
  starting transfers between devices  23.6 us (16%)
  local copies, waits for them, and re-layouts  8.41 us (6%)
  other arithmetic  3.66 us (2%)
    ppermute x17, waiting for transfers between devices, swap(): return lax.ppermute(value, axis, [(at, at ^ bits) for at in range(size)])  36.5 us
    pallas_call x1, Pallas kernels, solve(): pl.pallas_call(functools.partial(solve_kernel, columns, 32), in_specs=[SM...  33.8 us
    ppermute x17, starting transfers between devices, swap(): return lax.ppermute(value, axis, [(at, at ^ bits) for at in range(size)])  20.6 us
    pallas_call x1, Pallas kernels, geometry(): pl.pallas_call(functools.partial(geometry_kernel, scale), grid_spec=pltpu...  19.4 us
    pallas_call x3, Pallas kernels, image_part(): pl.pallas_call(functools.partial(image_kernel, len(densities), start is n...  15.8 us
    unnamed x15, local copies, waits for them, and re-layouts  7.26 us
    ppermute x2, waiting for transfers between devices, pair_swap(): return lax.ppermute(value, ('tri', 'rhs'), perm)  4.49 us
  transfers between devices with their start and end apart: 19, of which 11 were waited for; matrix products, arithmetic and copies ran while one was open for 1% of the time, Pallas kernels for 20%

profile of v1, /device:TPU:0, one launch (start us, length us, event | category | flops | bytes accessed | tf_op | source)
XLA Modules:
  0.0 151.2 jit_solution(16134895414788082563)
XLA Ops:
  0.7 1.2 fusion.5
  1.8 3.0 %collective-permute-start.1 = (bf16[128,1024]{1,0:T(8,128)(2,1)S(1)}, bf16[128,1024]{1,0:T(8,128)(2,1)S(1)}, u32[]{:S(2)}, u32[]{:S(2)}) collective-permute-start(bf16[128,1024]{1,0:T(8,128)(2,1)S(1)} %get-tuple-element.19.refs_0_), channel_id=1, source_target_pairs={{0,4},{4,0},{8,12},{12,8},{16,20},{20,16},{24,28},{28,24},{1,5},{5... | collective-permute-start | bytes 786440 | tf_op jit(solution)/shard_map/ppermute | solution.py:290
  4.8 1.6 %collective-permute-start.2 = (bf16[128,1024]{1,0:T(8,128)(2,1)S(1)}, bf16[128,1024]{1,0:T(8,128)(2,1)S(1)}, u32[]{:S(2)}, u32[]{:S(2)}) collective-permute-start(bf16[128,1024]{1,0:T(8,128)(2,1)S(1)} %get-tuple-element.19.refs_0_), channel_id=1, source_target_pairs={{0,8},{4,12},{8,0},{12,4},{16,24},{20,28},{24,16},{28,20},{1,9},{5... | collective-permute-start | bytes 786440 | tf_op jit(solution)/shard_map/ppermute | solution.py:290
  6.4 0.9 copy.10
  7.3 0.1 stack.44.blocks_ref
  7.4 1.0 copy-done.5
  8.4 0.8 copy-done.6
  9.2 19.4 %geometry.1 = (bf16[8,32,1024]{2,1,0:T(8,128)(2,1)S(1)}, bf16[8,32,1024]{2,1,0:T(8,128)(2,1)S(1)}, f32[8,1,1024]{2,1,0:T(1,128)S(1)}) custom-call(s32[8]{0:T(128)S(1)} %stack.44.blocks_ref, f32[3,64,128]{2,1,0:T(8,128)S(1)} %bitcast.43, s32[3,16384]{1,0:T(4,128)S(1)} %copy-done.5, s32[1,16384]{1,0:T(1,128)S(1)} %bitcast.44), custom_call_target="tpu_custom_call" | custom-call | tf_op jit(solution)/shard_map/geometry/pallas_call | solution.py:95
  28.7 4.2 %image_part.3 = f32[4,128,1024]{2,1,0:T(8,128)S(1)} custom-call(bf16[128,1024]{1,0:T(8,128)(2,1)S(1)} %get-tuple-element.19.refs_0_, bf16[32,1024]{1,0:T(8,128)(2,1)S(1)} %get-tuple-element.27.refs_1_, bf16[4,32,1024]{2,1,0:T(8,128)(2,1)S(1)} %slice.50.refs_2_, f32[1,1024]{1,0:T(1,128)S(1)} %slice_bitcast_fusion.7.refs_3_), custom_call_target="tpu_custom_call" | custom-call | flops 1342177280 | bytes 4194304 | tf_op jit(solution)/shard_map/image_part/pallas_call | solution.py:160
  32.9 0.2 fusion.6
  33.2 5.7 %image_part.5 = f32[2,128,1024]{2,1,0:T(8,128)S(1)} custom-call(bf16[128,1024]{1,0:T(8,128)(2,1)S(1)} %collective-permute-done.1.refs_0_, bf16[128,1024]{1,0:T(8,128)(2,1)S(1)} %collective-permute-done.2.refs_1_, bf16[128,1024]{1,0:T(8,128)(2,1)S(1)} %collective-permute-done.3.refs_2_, bf16[32,1024]{1,0:T(8,128)(2,1)S(1)} %get-tuple-element.30.refs_3_, ...), custom_call_target="tpu_custom_call" | custom-call | flops 2013265920 | bytes 2097152 | tf_op jit(solution)/shard_map/image_part/pallas_call | solution.py:160
  39.0 5.9 %image_part.4 = f32[2,128,1024]{2,1,0:T(8,128)S(1)} custom-call(bf16[128,1024]{1,0:T(8,128)(2,1)S(1)} %collective-permute-done.1.refs_0_, bf16[128,1024]{1,0:T(8,128)(2,1)S(1)} %collective-permute-done.2.refs_1_, bf16[128,1024]{1,0:T(8,128)(2,1)S(1)} %collective-permute-done.3.refs_2_, bf16[32,1024]{1,0:T(8,128)(2,1)S(1)} %get-tuple-element.30.refs_3_, ...), custom_call_target="tpu_custom_call" | custom-call | flops 2013265920 | bytes 2097152 | tf_op jit(solution)/shard_map/image_part/pallas_call | solution.py:160
  45.0 0.6 collective-permute-start.4
  45.6 3.1 %collective-permute-start.6 = (bf16[128,1024]{1,0:T(8,128)(2,1)S(1)}, bf16[128,1024]{1,0:T(8,128)(2,1)S(1)}, u32[]{:S(2)}, u32[]{:S(2)}) collective-permute-start(bf16[128,1024]{1,0:T(8,128)(2,1)S(1)} %fusion.1), channel_id=1, source_target_pairs={{0,16},{4,20},{8,24},{12,28},{16,0},{20,4},{24,8},{28,12},{1,17},{... | collective-permute-start | bytes 786440 | tf_op jit(solution)/shard_map/ppermute | solution.py:290
  48.7 1.5 %collective-permute-start = (f32[128,1024]{1,0:T(8,128)S(1)}, f32[128,1024]{1,0:T(8,128)S(1)}, u32[]{:S(2)}, u32[]{:S(2)}) collective-permute-start(f32[128,1024]{1,0:T(8,128)S(1)} %get-tuple-element.20.refs_0_.mine_ref), channel_id=1, source_target_pairs={{0,2},{2,0},{1,3},{3,1},{4,6},{6,4},{5,7},{7,5},{8,10},{10,8},{9,1... | collective-permute-start | bytes 1572872 | tf_op jit(solution)/shard_map/ppermute | solution.py:290
  50.2 10.6 %collective-permute-done.6 = bf16[128,1024]{1,0:T(8,128)(2,1)S(1)} collective-permute-done((bf16[128,1024]{1,0:T(8,128)(2,1)S(1)}, bf16[128,1024]{1,0:T(8,128)(2,1)S(1)}, u32[]{:S(2)}, u32[]{:S(2)}) %collective-permute-start.6) | collective-permute-done | bytes 262176 | tf_op jit(solution)/shard_map/ppermute | solution.py:290
  60.8 0.1 fusion.3.refs_2_
  60.9 1.6 %collective-permute-start.7 = (f32[128,1024]{1,0:T(8,128)S(1)}, f32[128,1024]{1,0:T(8,128)S(1)}, u32[]{:S(2)}, u32[]{:S(2)}) collective-permute-start(f32[128,1024]{1,0:T(8,128)S(1)} %fusion.3.refs_2_), channel_id=1, source_target_pairs={{0,2},{2,0},{1,3},{3,1},{4,6},{6,4},{5,7},{7,5},{8,10},{10,8},{9,1... | collective-permute-start | bytes 1572872 | tf_op jit(solution)/shard_map/ppermute | solution.py:290
  62.5 0.1 pad_add_fusion.place_ref
  62.6 0.8 copy-done.1
  63.4 10.9 %collective-permute-done.7.refs_3_ = f32[128,1024]{1,0:T(8,128)S(1)} collective-permute-done((f32[128,1024]{1,0:T(8,128)S(1)}, f32[128,1024]{1,0:T(8,128)S(1)}, u32[]{:S(2)}, u32[]{:S(2)}) %collective-permute-start.7) | collective-permute-done | bytes 524320 | tf_op jit(solution)/shard_map/ppermute | solution.py:290
  74.3 0.8 copy-done.3
  75.1 1.0 copy-done.2
  76.1 1.0 copy-done.4
  77.2 2.3 %gram.1 = (f32[256,1024]{1,0:T(8,128)S(1)}, f32[256,1024]{1,0:T(8,128)S(1)}, f32[768,256]{1,0:T(8,128)S(1)}) custom-call(s32[2]{0:T(128)S(1)} %pad_add_fusion.place_ref, f32[128,1024]{1,0:T(8,128)S(1)} %get-tuple-element.20.refs_0_.mine_ref, f32[128,1024]{1,0:T(8,128)S(1)} %copy-done.2, f32[128,1024]{1,0:T(8,128)S(1)} %fusion.3.refs_2_, ...), custom_call_target="tpu_custom_call" | custom-call | tf_op jit(solution)/shard_map/gram/pallas_call | solution.py:195
  79.4 0.9 copy-done
  80.5 1.7 %collective-permute-done.8 = f32[384,256]{1,0:T(8,128)S(1)} collective-permute-done((f32[384,256]{1,0:T(8,128)S(1)}, f32[384,256]{1,0:T(8,128)S(1)}, u32[]{:S(2)}, u32[]{:S(2)}) %collective-permute-start.8) | collective-permute-done | bytes 393248 | tf_op jit(solution)/shard_map/ppermute | solution.py:290
  82.1 1.0 dynamic-slice_add_fusion
  83.2 0.7 constant_dynamic-slice_fusion.2
  83.9 1.2 collective-permute-start.10
  85.1 1.5 collective-permute-start.11
  86.6 0.8 collective-permute-start.9
  87.3 2.0 %collective-permute-done.10 = f32[96,256]{1,0:T(8,128)S(1)} collective-permute-done((f32[96,256]{1,0:T(8,128)}, f32[96,256]{1,0:T(8,128)S(1)}, u32[]{:S(2)}, u32[]{:S(2)}) %collective-permute-start.10) | collective-permute-done | bytes 98336 | tf_op jit(solution)/shard_map/ppermute | solution.py:290
  89.4 2.4 %collective-permute-done.11 = f32[96,256]{1,0:T(8,128)S(1)} collective-permute-done((f32[96,256]{1,0:T(8,128)S(1)}, f32[96,256]{1,0:T(8,128)S(1)}, u32[]{:S(2)}, u32[]{:S(2)}) %collective-permute-start.11) | collective-permute-done | bytes 98336 | tf_op jit(solution)/shard_map/ppermute | solution.py:331
  91.8 1.2 collective-permute-done.9
  93.0 1.6 %collective-permute-start.12 = (f32[96,256]{1,0:T(8,128)S(1)}, f32[96,256]{1,0:T(8,128)S(1)}, u32[]{:S(2)}, u32[]{:S(2)}) collective-permute-start(f32[96,256]{1,0:T(8,128)S(1)} %add_add_fusion.1), channel_id=1, source_target_pairs={{0,8},{4,12},{8,0},{12,4},{16,24},{20,28},{24,16},{28,20},{1,9},{5... | collective-permute-start | bytes 294920 | tf_op jit(solution)/shard_map/ppermute | solution.py:290
  94.6 3.4 %collective-permute-start.13 = (f32[96,256]{1,0:T(8,128)S(1)}, f32[96,256]{1,0:T(8,128)S(1)}, u32[]{:S(2)}, u32[]{:S(2)}) collective-permute-start(f32[96,256]{1,0:T(8,128)S(1)} %add_add_fusion.1), channel_id=1, source_target_pairs={{0,16},{4,20},{8,24},{12,28},{16,0},{20,4},{24,8},{28,12},{1,17},{... | collective-permute-start | bytes 294920 | tf_op jit(solution)/shard_map/ppermute | solution.py:290
  98.0 7.3 %collective-permute-done.13 = f32[96,256]{1,0:T(8,128)S(1)} collective-permute-done((f32[96,256]{1,0:T(8,128)S(1)}, f32[96,256]{1,0:T(8,128)S(1)}, u32[]{:S(2)}, u32[]{:S(2)}) %collective-permute-start.13) | collective-permute-done | bytes 98336 | tf_op jit(solution)/shard_map/ppermute | solution.py:290
  105.3 1.5 collective-permute-start.15
  106.8 0.3 collective-permute-start.16
  107.1 1.8 %collective-permute-start.17 = (f32[96,256]{1,0:T(8,128)S(1)}, f32[96,256]{1,0:T(8,128)S(1)}, u32[]{:S(2)}, u32[]{:S(2)}) collective-permute-start(f32[96,256]{1,0:T(8,128)S(1)} %add_add_fusion), channel_id=1, source_target_pairs={{0,2},{2,0},{1,3},{3,1},{4,6},{6,4},{5,7},{7,5},{8,10},{10,8},{9,1... | collective-permute-start | bytes 294920 | tf_op jit(solution)/shard_map/ppermute | solution.py:290
  108.8 2.0 %collective-permute-done.15 = f32[96,256]{1,0:T(8,128)S(1)} collective-permute-done((f32[96,256]{1,0:T(8,128)S(1)}, f32[96,256]{1,0:T(8,128)S(1)}, u32[]{:S(2)}, u32[]{:S(2)}) %collective-permute-start.15) | collective-permute-done | bytes 98336 | tf_op jit(solution)/shard_map/ppermute | solution.py:331
  110.9 0.5 collective-permute-done.16
  111.4 0.5 collective-permute-done.17
  112.1 1.8 %collective-permute-done.18 = f32[384,256]{1,0:T(8,128)} collective-permute-done((f32[384,256]{1,0:T(8,128)S(1)}, f32[384,256]{1,0:T(8,128)}, u32[]{:S(2)}, u32[]{:S(2)}) %collective-permute-start.18) | collective-permute-done | bytes 393248 | tf_op jit(solution)/shard_map/ppermute | solution.py:290
  113.9 1.0 broadcast_select_fusion.1
  115.0 33.8 %solve.1 = (f32[128,256]{1,0:T(8,128)S(1)}, f32[128,256]{1,0:T(8,128)S(1)}) custom-call(s32[2]{0:T(128)S(1)} %pad_add_fusion.place_ref, f32[768,256]{1,0:T(8,128)S(1)} %pad_maximum_fusion.sums_ref), custom_call_target="tpu_custom_call" | custom-call | tf_op jit(solution)/shard_map/solve/pallas_call | solution.py:256
  148.8 2.4 %finish.1 = (f32[128,1024]{1,0:T(8,128)}, f32[128,1024]{1,0:T(8,128)}, f32[128,1024]{1,0:T(8,128)}) custom-call(f32[128,1024]{1,0:T(8,128)S(1)} %get-tuple-element.20.refs_0_.mine_ref, f32[256,1024]{1,0:T(8,128)S(1)} %get-tuple-element.14.current_ref, f32[256,1024]{1,0:T(8,128)S(1)} %get-tuple-element.15.image_ref, ...), custom_call_target="tpu_custom_call" | custom-call | tf_op jit(solution)/shard_map/finish/pallas_call | solution.py:278
  (34 shorter events, 0.6 us)
Async XLA Ops:
  1.8 31.4 %collective-permute-start.1 = (bf16[128,1024]{1,0:T(8,128)(2,1)S(1)}, bf16[128,1024]{1,0:T(8,128)(2,1)S(1)}, u32[]{:S(2)}, u32[]{:S(2)}) collective-permute-start(bf16[128,1024]{1,0:T(8,128)(2,1)S(1)} %get-tuple-element.19.refs_0_), channel_id=1, source_target_pairs={{0,4},{4,0},{8,12},{12,8},{16,20},{20,16},{24,28},{28,24},{1,5},{5... | collective-permute-start | bytes 786440 | tf_op jit(solution)/shard_map/ppermute | solution.py:290
  4.8 28.4 %collective-permute-start.2 = (bf16[128,1024]{1,0:T(8,128)(2,1)S(1)}, bf16[128,1024]{1,0:T(8,128)(2,1)S(1)}, u32[]{:S(2)}, u32[]{:S(2)}) collective-permute-start(bf16[128,1024]{1,0:T(8,128)(2,1)S(1)} %get-tuple-element.19.refs_0_), channel_id=1, source_target_pairs={{0,8},{4,12},{8,0},{12,4},{16,24},{20,28},{24,16},{28,20},{1,9},{5... | collective-permute-start | bytes 786440 | tf_op jit(solution)/shard_map/ppermute | solution.py:290
  6.4 26.8 %collective-permute-start.3 = (bf16[128,1024]{1,0:T(8,128)(2,1)S(1)}, bf16[128,1024]{1,0:T(8,128)(2,1)S(1)}, u32[]{:S(2)}, u32[]{:S(2)}) collective-permute-start(bf16[128,1024]{1,0:T(8,128)(2,1)S(1)} %get-tuple-element.19.refs_0_), channel_id=1, source_target_pairs={{0,12},{4,8},{8,4},{12,0},{16,28},{20,24},{24,20},{28,16},{1,13},{... | collective-permute-start | bytes 786440 | tf_op jit(solution)/shard_map/ppermute | solution.py:290
  7.4 1.0 copy-start.5
  8.4 0.8 copy-start.6
  39.0 6.6 %collective-permute-start.5 = (bf16[128,1024]{1,0:T(8,128)(2,1)S(1)}, bf16[128,1024]{1,0:T(8,128)(2,1)S(1)}, u32[]{:S(2)}, u32[]{:S(2)}) collective-permute-start(bf16[128,1024]{1,0:T(8,128)(2,1)S(1)} %fusion.4), channel_id=1, source_target_pairs={{0,1},{1,0},{2,3},{3,2},{4,5},{5,4},{6,7},{7,6},{8,9},{9,8},{10,11... | collective-permute-start | bytes 786440 | tf_op jit(solution)/shard_map/ppermute | solution.py:290
  45.0 15.8 %collective-permute-start.4 = (f32[128,1024]{1,0:T(8,128)S(1)}, f32[128,1024]{1,0:T(8,128)S(1)}, u32[]{:S(2)}, u32[]{:S(2)}) collective-permute-start(f32[128,1024]{1,0:T(8,128)S(1)} %slice_bitcast_fusion.1), channel_id=1, source_target_pairs={{0,1},{1,0},{2,3},{3,2},{4,5},{5,4},{6,7},{7,6},{8,9},{9,8},{10,11... | collective-permute-start | bytes 1572872 | tf_op jit(solution)/shard_map/ppermute | solution.py:290
  45.6 15.2 %collective-permute-start.6 = (bf16[128,1024]{1,0:T(8,128)(2,1)S(1)}, bf16[128,1024]{1,0:T(8,128)(2,1)S(1)}, u32[]{:S(2)}, u32[]{:S(2)}) collective-permute-start(bf16[128,1024]{1,0:T(8,128)(2,1)S(1)} %fusion.1), channel_id=1, source_target_pairs={{0,16},{4,20},{8,24},{12,28},{16,0},{20,4},{24,8},{28,12},{1,17},{... | collective-permute-start | bytes 786440 | tf_op jit(solution)/shard_map/ppermute | solution.py:290
  48.7 13.9 %collective-permute-start = (f32[128,1024]{1,0:T(8,128)S(1)}, f32[128,1024]{1,0:T(8,128)S(1)}, u32[]{:S(2)}, u32[]{:S(2)}) collective-permute-start(f32[128,1024]{1,0:T(8,128)S(1)} %get-tuple-element.20.refs_0_.mine_ref), channel_id=1, source_target_pairs={{0,2},{2,0},{1,3},{3,1},{4,6},{6,4},{5,7},{7,5},{8,10},{10,8},{9,1... | collective-permute-start | bytes 1572872 | tf_op jit(solution)/shard_map/ppermute | solution.py:290
  60.9 13.4 %collective-permute-start.7 = (f32[128,1024]{1,0:T(8,128)S(1)}, f32[128,1024]{1,0:T(8,128)S(1)}, u32[]{:S(2)}, u32[]{:S(2)}) collective-permute-start(f32[128,1024]{1,0:T(8,128)S(1)} %fusion.3.refs_2_), channel_id=1, source_target_pairs={{0,2},{2,0},{1,3},{3,1},{4,6},{6,4},{5,7},{7,5},{8,10},{10,8},{9,1... | collective-permute-start | bytes 1572872 | tf_op jit(solution)/shard_map/ppermute | solution.py:290
  62.6 0.8 copy-start.1
  74.3 0.8 copy-start.3
  75.1 1.0 copy-start.2
  76.1 1.0 copy-start.4
  79.4 0.9 copy-start
  80.3 1.8 %collective-permute-start.8 = (f32[384,256]{1,0:T(8,128)S(1)}, f32[384,256]{1,0:T(8,128)S(1)}, u32[]{:S(2)}, u32[]{:S(2)}) collective-permute-start(f32[384,256]{1,0:T(8,128)S(1)} %constant_dynamic-slice_fusion.3), channel_id=1, source_target_pairs={{0,1},{1,0},{2,3},{3,2},{4,5},{5,4},{6,7},{7,6},{8,9},{9,8},{10,11... | collective-permute-start | bytes 1179656 | tf_op jit(solution)/shard_map/ppermute | solution.py:290
  83.9 5.5 %collective-permute-start.10 = (f32[96,256]{1,0:T(8,128)}, f32[96,256]{1,0:T(8,128)S(1)}, u32[]{:S(2)}, u32[]{:S(2)}) collective-permute-start(f32[96,256]{1,0:T(8,128)} %get-tuple-element.37), channel_id=1, source_target_pairs={{0,4},{4,0},{8,12},{12,8},{16,20},{20,16},{24,28},{28,24},{1,5},{5... | collective-permute-start | bytes 294920 | tf_op jit(solution)/shard_map/ppermute | solution.py:290
  85.1 6.7 %collective-permute-start.11 = (f32[96,256]{1,0:T(8,128)S(1)}, f32[96,256]{1,0:T(8,128)S(1)}, u32[]{:S(2)}, u32[]{:S(2)}) collective-permute-start(f32[96,256]{1,0:T(8,128)S(1)} %get-tuple-element.36), channel_id=1, source_target_pairs={{0,6},{2,4},{4,2},{6,0},{8,14},{10,12},{12,10},{14,8},{16,22},{18,... | collective-permute-start | bytes 294920 | tf_op jit(solution)/shard_map/ppermute | solution.py:331
  86.6 6.4 %collective-permute-start.9 = (f32[96,256]{1,0:T(8,128)S(1)}, f32[96,256]{1,0:T(8,128)S(1)}, u32[]{:S(2)}, u32[]{:S(2)}) collective-permute-start(f32[96,256]{1,0:T(8,128)S(1)} %get-tuple-element.35), channel_id=1, source_target_pairs={{0,2},{2,0},{1,3},{3,1},{4,6},{6,4},{5,7},{7,5},{8,10},{10,8},{9,1... | collective-permute-start | bytes 294920 | tf_op jit(solution)/shard_map/ppermute | solution.py:290
  93.0 5.0 %collective-permute-start.12 = (f32[96,256]{1,0:T(8,128)S(1)}, f32[96,256]{1,0:T(8,128)S(1)}, u32[]{:S(2)}, u32[]{:S(2)}) collective-permute-start(f32[96,256]{1,0:T(8,128)S(1)} %add_add_fusion.1), channel_id=1, source_target_pairs={{0,8},{4,12},{8,0},{12,4},{16,24},{20,28},{24,16},{28,20},{1,9},{5... | collective-permute-start | bytes 294920 | tf_op jit(solution)/shard_map/ppermute | solution.py:290
  94.6 10.7 %collective-permute-start.13 = (f32[96,256]{1,0:T(8,128)S(1)}, f32[96,256]{1,0:T(8,128)S(1)}, u32[]{:S(2)}, u32[]{:S(2)}) collective-permute-start(f32[96,256]{1,0:T(8,128)S(1)} %add_add_fusion.1), channel_id=1, source_target_pairs={{0,16},{4,20},{8,24},{12,28},{16,0},{20,4},{24,8},{28,12},{1,17},{... | collective-permute-start | bytes 294920 | tf_op jit(solution)/shard_map/ppermute | solution.py:290
  98.0 7.3 %collective-permute-start.14 = (f32[96,256]{1,0:T(8,128)S(1)}, f32[96,256]{1,0:T(8,128)S(1)}, u32[]{:S(2)}, u32[]{:S(2)}) collective-permute-start(f32[96,256]{1,0:T(8,128)S(1)} %add_add_fusion.1), channel_id=1, source_target_pairs={{0,24},{4,28},{8,16},{12,20},{16,8},{20,12},{24,0},{28,4},{1,25},{... | collective-permute-start | bytes 294920 | tf_op jit(solution)/shard_map/ppermute | solution.py:290
  105.3 5.6 %collective-permute-start.15 = (f32[96,256]{1,0:T(8,128)S(1)}, f32[96,256]{1,0:T(8,128)S(1)}, u32[]{:S(2)}, u32[]{:S(2)}) collective-permute-start(f32[96,256]{1,0:T(8,128)S(1)} %add_add_fusion), channel_id=1, source_target_pairs={{0,6},{2,4},{4,2},{6,0},{8,14},{10,12},{12,10},{14,8},{16,22},{18,... | collective-permute-start | bytes 294920 | tf_op jit(solution)/shard_map/ppermute | solution.py:331
  106.8 4.6 %collective-permute-start.16 = (f32[96,256]{1,0:T(8,128)S(1)}, f32[96,256]{1,0:T(8,128)S(1)}, u32[]{:S(2)}, u32[]{:S(2)}) collective-permute-start(f32[96,256]{1,0:T(8,128)S(1)} %add_add_fusion), channel_id=1, source_target_pairs={{0,4},{4,0},{8,12},{12,8},{16,20},{20,16},{24,28},{28,24},{1,5},{5... | collective-permute-start | bytes 294920 | tf_op jit(solution)/shard_map/ppermute | solution.py:290
  107.1 4.8 %collective-permute-start.17 = (f32[96,256]{1,0:T(8,128)S(1)}, f32[96,256]{1,0:T(8,128)S(1)}, u32[]{:S(2)}, u32[]{:S(2)}) collective-permute-start(f32[96,256]{1,0:T(8,128)S(1)} %add_add_fusion), channel_id=1, source_target_pairs={{0,2},{2,0},{1,3},{3,1},{4,6},{6,4},{5,7},{7,5},{8,10},{10,8},{9,1... | collective-permute-start | bytes 294920 | tf_op jit(solution)/shard_map/ppermute | solution.py:290
  112.0 1.9 %collective-permute-start.18 = (f32[384,256]{1,0:T(8,128)S(1)}, f32[384,256]{1,0:T(8,128)}, u32[]{:S(2)}, u32[]{:S(2)}) collective-permute-start(f32[384,256]{1,0:T(8,128)S(1)} %pad_maximum_fusion.1), channel_id=1, source_target_pairs={{0,1},{1,0},{2,3},{3,2},{4,5},{5,4},{6,7},{7,6},{8,9},{9,8},{10,11... | collective-permute-start | bytes 1179656 | tf_op jit(solution)/shard_map/ppermute | solution.py:290

commit v2 on v1

v2 whole, which is shorter than its diff:
```python
import functools
import math

import jax
import jax.numpy as jnp
from jax import lax
from jax.experimental import pallas as pl
from jax.experimental.pallas import tpu as pltpu
from jax.sharding import PartitionSpec as P

smooth_sq = 0.01
self_term = 1.0
inject = 3.0
f32 = jnp.float32
bf16 = jnp.bfloat16
LANES = 128
FEATURES = 32
PAIRS = ((0, 0), (0, 1), (1, 0), (1, 1), (0, 2), (2, 0))
VMEM = pl.BlockSpec(memory_space=pltpu.VMEM)
SMEM = pl.BlockSpec(memory_space=pltpu.SMEM)


def dot(a, b, ca, cb, precision=None):
    return lax.dot_general(
        a, b, (((ca,), (cb,)), ((), ())), precision=precision, preferred_element_type=f32
    )


def exact_dot(a, b, ca, cb):
    return dot(a, b, ca, cb, lax.Precision.HIGHEST)


def close_dot(a, b, ca, cb):
    a_high, b_high = a.astype(bf16), b.astype(bf16)
    a_low = (a - a_high.astype(f32)).astype(bf16)
    b_low = (b - b_high.astype(f32)).astype(bf16)
    return (dot(a_low, b_high, ca, cb) + dot(a_high, b_low, ca, cb)) + dot(a_high, b_high, ca, cb)


def params(mebibytes=16):
    return pltpu.CompilerParams(vmem_limit_bytes=mebibytes * 1024 * 1024)


def pieces_of(value):
    high = value.astype(bf16).astype(f32)
    rest = value - high
    middle = rest.astype(bf16).astype(f32)
    return (high, middle, rest - middle)


def geometry_kernel(
    scale, blocks_ref, vertices_ref, corners_ref, layers_ref, a_ref, b_ref, diag_ref, plain, table, a_rows, b_rows
):
    count = corners_ref.shape[1]
    tops = plain.shape[0]

    @pl.when(pl.program_id(0) == 0)
    def _():
        for axis in range(3):
            for top in range(tops):
                plain[top : top + 1, axis * LANES : (axis + 1) * LANES] = vertices_ref[
                    axis : axis + 1, top * LANES : (top + 1) * LANES
                ]
        for at, part in enumerate(pieces_of(plain[...])):
            table[at * tops : (at + 1) * tops, :] = part.astype(bf16)

    top_iota = lax.broadcasted_iota(jnp.int32, (tops, count), 0)
    low_iota = lax.broadcasted_iota(jnp.int32, (LANES, count), 0)
    points = []
    for corner in range(3):
        index = corners_ref[corner : corner + 1, :]
        top = jnp.where(top_iota == (index >> 7), 1.0, 0.0).astype(bf16)
        low = low_iota == (index & (LANES - 1))
        found = dot(table[...], jnp.concatenate([top, top, top], axis=0), 0, 0)
        points.append(
            [
                jnp.sum(jnp.where(low, found[axis * LANES : (axis + 1) * LANES], 0.0), axis=0, keepdims=True)
                for axis in range(3)
            ]
        )
    p0, p1, p2 = points
    centre = [(p0[k] + p1[k] + p2[k]) / 3.0 for k in range(3)]
    e1 = [p1[k] - p0[k] for k in range(3)]
    e2 = [p2[k] - p0[k] for k in range(3)]
    cross_x = e1[1] * e2[2] - e1[2] * e2[1]
    cross_y = e1[2] * e2[0] - e1[0] * e2[2]
    cross_z = e1[0] * e2[1] - e1[1] * e2[0]
    area_sq = cross_x * cross_x + cross_y * cross_y + cross_z * cross_z
    layers = layers_ref[...]
    factor = jnp.where(layers == 0, 1.0, jnp.where(layers == 1, 0.3, 0.8)).astype(f32)
    weight = factor * (0.5 + area_sq / (1.0 + area_sq))
    unit = 1.0 / (scale * (weight * weight))
    norm = centre[0] * centre[0] + centre[1] * centre[1] + centre[2] * centre[2]
    a_side = [unit * norm, unit] + [unit * c for c in centre]
    b_side = [unit, unit * (norm + smooth_sq)] + [-2.0 * unit * c for c in centre]
    a_parts = [pieces_of(value) for value in a_side]
    b_parts = [pieces_of(value) for value in b_side]
    row = 0
    for a_piece, b_piece in PAIRS:
        for term in range(5):
            a_rows[row : row + 1, :] = a_parts[term][a_piece]
            b_rows[row : row + 1, :] = b_parts[term][b_piece]
            row += 1
    blank = jnp.zeros((FEATURES - row, count), f32)
    a_rows[row:, :] = blank
    b_rows[row:, :] = blank
    a_ref[...] = a_rows[...].astype(bf16)
    b_ref[...] = b_rows[...].astype(bf16)
    diag_ref[...] = weight * weight * (lax.rsqrt(jnp.full_like(weight, smooth_sq)) * scale + self_term)


def geometry(blocks, vertices, corners, layers, count, scale):
    n = blocks.shape[0]
    points = vertices.shape[1]
    tops = points // LANES
    feature = jax.ShapeDtypeStruct((n, FEATURES, count), bf16)
    return pl.pallas_call(
        functools.partial(geometry_kernel, scale),
        grid_spec=pltpu.PrefetchScalarGridSpec(
            num_scalar_prefetch=1,
            grid=(n,),
            in_specs=[
                pl.BlockSpec((3, points), lambda g, blk: (0, 0)),
                pl.BlockSpec((3, count), lambda g, blk: (0, blk[g])),
                pl.BlockSpec((1, count), lambda g, blk: (0, blk[g])),
            ],
            out_specs=[
                pl.BlockSpec((None, FEATURES, count), lambda g, blk: (g, 0, 0)),
                pl.BlockSpec((None, FEATURES, count), lambda g, blk: (g, 0, 0)),
                pl.BlockSpec((None, 1, count), lambda g, blk: (g, 0, 0)),
            ],
            scratch_shapes=[
                pltpu.VMEM((tops, 3 * LANES), f32),
                pltpu.VMEM((3 * tops, 3 * LANES), bf16),
                pltpu.VMEM((FEATURES, count), f32),
                pltpu.VMEM((FEATURES, count), f32),
            ],
        ),
        out_shape=(feature, feature, jax.ShapeDtypeStruct((n, 1, count), f32)),
        compiler_params=params(),
        name="geometry",
    )(blocks, vertices, corners, layers[None, :])


def image_kernel(sources, has_start, has_diag, *refs):
    refs = list(refs)
    densities = [refs.pop(0) for _ in range(sources)]
    a_refs = [refs.pop(0) for _ in range(sources)]
    b_ref = refs.pop(0)
    start_ref = refs.pop(0) if has_start else None
    out_ref = refs.pop(0)
    targets, columns, count = out_ref.shape
    chunk = min(512, count)

    def one(target, with_diag):
        b = b_ref[target]
        acc = start_ref[target] if has_start else jnp.zeros((columns, count), f32)
        for density, a_ref in zip(densities, a_refs):
            for begin in range(0, count, chunk):
                tile = lax.rsqrt(dot(a_ref[:, begin : begin + chunk], b, 0, 0))
                if with_diag:
                    rows = begin + lax.broadcasted_iota(jnp.int32, tile.shape, 0)
                    cols = lax.broadcasted_iota(jnp.int32, tile.shape, 1)
                    tile = jnp.where(rows == cols, 0.0, tile)
                acc = acc + dot(density[:, begin : begin + chunk], tile.astype(bf16), 1, 0)
        out_ref[target] = acc

    if has_diag:
        one(0, True)
    if targets > int(has_diag):

        @pl.loop(int(has_diag), targets)
        def _(target):
            one(target, False)


def image_part(densities, a_side, b_side, start=None, own_first=False):
    columns, count = densities[0].shape
    targets = b_side.shape[0]
    operands = [*densities, *a_side, b_side]
    if start is not None:
        operands.append(start)
    entries = len(densities) * count * targets * count
    return pl.pallas_call(
        functools.partial(image_kernel, len(densities), start is not None, own_first),
        in_specs=[VMEM] * len(operands),
        out_specs=VMEM,
        out_shape=jax.ShapeDtypeStruct((targets, columns, count), f32),
        compiler_params=params(24),
        cost_estimate=pl.CostEstimate(
            flops=2 * entries * (columns + FEATURES), bytes_accessed=8 * targets * columns * count, transcendentals=entries
        ),
        name="image_part",
    )(*operands)


def combine_kernel(ranks, place_ref, *refs):
    parts, smooth_ref = refs[: -2 * ranks + 1], refs[-2 * ranks + 1]
    gives, rests = refs[-2 * ranks + 2 : -ranks + 1], refs[-ranks + 1 :]
    count = smooth_ref.shape[1]
    width = count // ranks
    smooth = parts[0][...].astype(f32)
    for part in parts[1:]:
        smooth = smooth + part[...].astype(f32)
    smooth_ref[...] = smooth
    for at in range(1, ranks):
        place = place_ref[at]
        gives[at - 1][...] = smooth_ref[:, pl.ds(pl.multiple_of(place * width, width), width)].astype(bf16)
        for chunk in range(ranks - 1):
            begin = lax.rem(place + 1 + chunk, ranks) * width
            rests[at - 1][:, chunk * width : (chunk + 1) * width] = smooth_ref[
                :, pl.ds(pl.multiple_of(begin, width), width)
            ].astype(bf16)


def combine(places, parts):
    ranks = places.shape[0]
    columns, count = parts[0].shape
    width = count // ranks
    out_shape = [jax.ShapeDtypeStruct((columns, count), f32)]
    out_shape += [jax.ShapeDtypeStruct((columns, width), bf16)] * (ranks - 1)
    out_shape += [jax.ShapeDtypeStruct((columns, count - width), bf16)] * (ranks - 1)
    outs = pl.pallas_call(
        functools.partial(combine_kernel, ranks),
        in_specs=[SMEM] + [VMEM] * len(parts),
        out_specs=[VMEM] * len(out_shape),
        out_shape=out_shape,
        compiler_params=params(),
        name="combine",
    )(places, *parts)
    return outs[0], outs[1:ranks], outs[ranks:]


def gram_kernel(ranks, place_ref, core_ref, smooth_ref, diag_ref, *refs):
    currents, gots = refs[:ranks], refs[ranks : 2 * ranks - 1]
    keep_ref, give_ref, current_all, image_all, sums = refs[2 * ranks - 1 :]
    columns, count = smooth_ref.shape
    width = count // ranks
    mine = pl.ds(pl.multiple_of(place_ref[0] * width, width), width)
    diag = diag_ref[:, mine].astype(bf16).astype(f32)
    for rank in range(ranks):
        at = pl.ds(pl.multiple_of(place_ref[rank] * columns, columns), columns)
        current = currents[rank][:, mine]
        smooth = smooth_ref[:, mine] if rank == 0 else gots[rank - 1][...].astype(f32)
        current_all[at, :] = current
        image_all[at, :] = smooth + diag * current.astype(bf16).astype(f32)
    current = current_all[...]
    image = image_all[...]
    total = ranks * columns
    sums[:total] = close_dot(current, image, 1, 1)
    sums[total : 2 * total] = close_dot(current, current, 1, 1)
    sums[2 * total :] = close_dot(image, image, 1, 1)
    half = keep_ref.shape[0]
    keep_ref[...] = sums[pl.ds(pl.multiple_of(core_ref[0] * half, half), half), :]
    give_ref[...] = sums[pl.ds(pl.multiple_of((1 - core_ref[0]) * half, half), half), :]


def gram_sums(places, core, smooth, diag, currents, gots):
    ranks = len(currents)
    columns, count = smooth.shape
    total = ranks * columns
    half = jax.ShapeDtypeStruct((3 * total // 2, total), f32)
    return pl.pallas_call(
        functools.partial(gram_kernel, ranks),
        in_specs=[SMEM, SMEM] + [VMEM] * (2 * ranks + 1),
        out_specs=[VMEM] * 2,
        out_shape=(half, half),
        scratch_shapes=[
            pltpu.VMEM((total, count // ranks), f32),
            pltpu.VMEM((total, count // ranks), f32),
            pltpu.VMEM((3 * total, total), f32),
        ],
        compiler_params=params(),
        name="gram",
    )(places, core, smooth, diag, *currents, *gots)


def shares_kernel(place_ref, keep_ref, got_ref, *shares):
    size = shares[0].shape[0]
    for at, share in enumerate(shares):
        rows = pl.ds(pl.multiple_of(place_ref[at] * size, size), size)
        share[...] = keep_ref[rows, :] + got_ref[rows, :]


def cut(places, keep, got):
    rows, lanes = keep.shape
    cuts = places.shape[0]
    return pl.pallas_call(
        shares_kernel,
        in_specs=[SMEM, VMEM, VMEM],
        out_specs=[VMEM] * cuts,
        out_shape=[jax.ShapeDtypeStruct((rows // cuts, lanes), f32)] * cuts,
        compiler_params=params(),
        name="shares",
    )(places, keep, got)


def reciprocal(value):
    guess = pl.reciprocal(value, approx=True)
    return guess * (2.0 - value * guess)


def eliminate(panel, begin, width):
    size, total = panel.shape
    parts = [panel[:, at : at + LANES] for at in range(0, total, LANES)]
    row_at = lax.broadcasted_iota(jnp.int32, (size, LANES), 0)
    col_at = lax.broadcasted_iota(jnp.int32, (size, LANES), 1)
    for group in range(0, size, width):
        own = parts[(begin + group) // LANES]
        first = (begin + group) % LANES
        cols = [jnp.broadcast_to(own[:, first + at : first + at + 1], (size, LANES)) for at in range(width)]
        for at in range(width):
            pivot = group + at
            inverse = reciprocal(cols[at][pivot : pivot + 1, :])
            is_row = row_at == pivot
            col = jnp.where(is_row, -1.0, cols[at])
            for part in range(len(parts)):
                row, gone = parts[part][pivot : pivot + 1, :], is_row
                if part == (begin + pivot) // LANES:
                    is_col = col_at == (begin + pivot) % LANES
                    row, gone = jnp.where(is_col[:1], 1.0, row), is_row | is_col
                parts[part] = jnp.where(gone, 0.0, parts[part]) - col * (row * inverse)
            for later in range(at + 1, width):
                factor = cols[later][pivot : pivot + 1, :] * inverse
                cols[later] = jnp.where(is_row, 0.0, cols[later]) - col * factor
    return jnp.concatenate(parts, axis=1)


def sweep(ref, begin, size):
    total = ref.shape[0]
    panel = ref[begin : begin + size, :]
    row = eliminate(panel, begin, 8)
    col_at = lax.broadcasted_iota(jnp.int32, panel.shape, 1)
    left = [part.astype(bf16) for part in pieces_of(jnp.where(col_at < begin, -panel, panel))]
    right = [part.astype(bf16) for part in pieces_of(row)]
    update = dot(
        jnp.concatenate([left[at] for at, _ in PAIRS], axis=0),
        jnp.concatenate([right[at] for _, at in PAIRS], axis=0),
        0,
        0,
    )
    lanes = lax.broadcasted_iota(jnp.int32, (total, total), 1)
    ref[...] = jnp.where((lanes >= begin) & (lanes < begin + size), 0.0, ref[...]) - update
    ref[begin : begin + size, :] = row


def solve_kernel(columns, size, cuts, place_ref, share_ref, *refs):
    shares = refs[: 2 * cuts]
    step_ref, turn_ref, sums, gram_inv, square_inv, step_all = refs[2 * cuts :]
    rows, total = shares[0].shape
    for at, share in enumerate(shares):
        sums[pl.ds(pl.multiple_of(share_ref[at] * rows, rows), rows), :] = share[...]
    cross = sums[:total]
    gram_inv[...] = 0.5 * (cross + cross.T)
    square_inv[...] = sums[total : 2 * total]
    for begin in range(0, total, size):
        sweep(gram_inv, begin, size)
        sweep(square_inv, begin, size)
    mine = pl.ds(pl.multiple_of(place_ref[0] * columns, columns), columns)
    step_all[...] = close_dot(sums[total : 2 * total], gram_inv[...], 1, 0)
    step = step_all[mine, :]
    step_ref[...] = step
    square_rows = sums[pl.ds(pl.multiple_of(total + place_ref[0] * columns, columns), columns), :]
    cross_rows = sums[mine, :]
    left = close_dot(step, sums[2 * total :], 1, 0) - cross_rows
    following = square_rows - close_dot(step, sums[:total], 1, 1) + close_dot(left, step_all[...], 1, 1)
    turn_ref[...] = close_dot(following, square_inv[...], 1, 0)


def solve(places, share_places, shares, columns):
    total = shares[0].shape[1]
    square = pltpu.VMEM((total, total), f32)
    rows = jax.ShapeDtypeStruct((columns, total), f32)
    return pl.pallas_call(
        functools.partial(solve_kernel, columns, 32, len(shares) // 2),
        in_specs=[SMEM, SMEM] + [VMEM] * len(shares),
        out_specs=[VMEM] * 2,
        out_shape=(rows, rows),
        scratch_shapes=[pltpu.VMEM((3 * total, total), f32), square, square, square],
        compiler_params=params(),
        name="solve",
    )(places, share_places, *shares)


def finish_kernel(ranks, place_ref, smooth_ref, diag_ref, step_ref, turn_ref, *refs):
    currents, gots, rests = refs[:ranks], refs[ranks : 2 * ranks - 1], refs[2 * ranks - 1 : 3 * ranks - 2]
    solution_ref, remainder_ref, direction_ref, current_all, image_all = refs[3 * ranks - 2 :]
    columns, count = smooth_ref.shape
    width = count // ranks
    diag = diag_ref[...].astype(bf16).astype(f32)
    for rank in range(ranks):
        at = pl.ds(pl.multiple_of(place_ref[rank] * columns, columns), columns)
        current = currents[rank][...]
        current_all[at, :] = current
        fixed = diag * current.astype(bf16).astype(f32)
        if rank == 0:
            image_all[at, :] = smooth_ref[...] + fixed
            continue
        for chunk in range(ranks):
            begin = lax.rem(place_ref[0] + chunk, ranks) * width
            lanes = pl.ds(pl.multiple_of(begin, width), width)
            if chunk == 0:
                image_all[at, lanes] = gots[rank - 1][...].astype(f32)
            else:
                image_all[at, lanes] = rests[rank - 1][:, (chunk - 1) * width : chunk * width].astype(f32)
        image_all[at, :] = image_all[at, :] + fixed
    step = step_ref[...]
    solution_ref[...] = close_dot(step, current_all[...], 1, 0)
    remainder = currents[0][...] - close_dot(step, image_all[...], 1, 0)
    remainder_ref[...] = remainder
    direction_ref[...] = remainder + close_dot(turn_ref[...], current_all[...], 1, 0)


def finish(places, smooth, diag, step, turn, currents, gots, rests):
    ranks = len(currents)
    columns, count = smooth.shape
    out = jax.ShapeDtypeStruct((columns, count), f32)
    every = pltpu.VMEM((ranks * columns, count), f32)
    return pl.pallas_call(
        functools.partial(finish_kernel, ranks),
        in_specs=[SMEM] + [VMEM] * (3 * ranks + 2),
        out_specs=[VMEM] * 3,
        out_shape=(out, out, out),
        scratch_shapes=[every, every],
        compiler_params=params(),
        name="finish",
    )(places, smooth, diag, step, turn, *currents, *gots, *rests)


def swap(value, axis, bits):
    size = lax.axis_size(axis)
    return lax.ppermute(value, axis, [(at, at ^ bits) for at in range(size)])


def pair_swap(value, bits, ranks):
    rank_bits, tri_bit = bits % ranks, bits // ranks
    if tri_bit == 0:
        return swap(value, "rhs", rank_bits)
    if rank_bits == 0:
        return swap(value, "tri", 1)
    count = lax.axis_size("tri")
    perm = [
        (tri * ranks + rank, (tri ^ 1) * ranks + (rank ^ rank_bits)) for tri in range(count) for rank in range(ranks)
    ]
    return lax.ppermute(value, ("tri", "rhs"), perm)


def indices(*values):
    return jnp.stack(values).astype(jnp.int32)


def all_sum(keep, give, ranks, tris, place, core):
    cuts = 2 * ranks
    cut_places = indices(*[place ^ bits for bits in range(cuts)])
    value, *gives = cut(cut_places, keep, swap(give, "split", 1))
    value = sum([pair_swap(part, bits, ranks) for bits, part in enumerate(gives, 1)], value)
    value = sum([swap(value, "tri", 2 * far) for far in range(1, tris // 2)], value)
    shares = [value] + [pair_swap(value, bits, ranks) for bits in range(1, cuts)]
    others = [swap(share, "split", 1) for share in shares]
    return shares + others, jnp.concatenate([cut_places + core * cuts, cut_places + (1 - core) * cuts])


def body(residual, attach, vertices, corners, layers):
    columns, count = residual.shape
    tris, ranks, cores = lax.axis_size("tri"), lax.axis_size("rhs"), lax.axis_size("split")
    tri, rank, core = lax.axis_index("tri"), lax.axis_index("rhs"), lax.axis_index("split")
    near = min(4, tris)
    groups = tris // near
    scale = 1.0 / math.sqrt(corners.shape[1])

    my_ids = (tri * cores + core) * count + jnp.arange(count, dtype=jnp.int32)
    current = residual + inject * (attach[:, None] == my_ids[None, :]).astype(f32)
    packed = current.astype(bf16)
    packed_near = [swap(packed, "tri", bits) for bits in range(1, near)]
    currents = [current] + [swap(current, "rhs", bits) for bits in range(1, ranks)]

    own_blocks = [(tri ^ (near * far)) * cores + core for far in range(groups)]
    near_blocks = [(tri ^ bits) * cores + core for bits in range(1, near)]
    a_all, b_all, diag = geometry(indices(*own_blocks, *near_blocks), vertices, corners, layers, count, scale)
    a_near = [a_all[groups + bits] for bits in range(near - 1)]
    b_own, diag = b_all[:groups], diag[0]
    b_other = swap(b_own, "split", 1)

    first_own = image_part([packed], [a_all[0]], b_own, own_first=True)
    first_other = image_part([packed], [a_all[0]], b_other)
    parts_far = []
    if groups > 1:
        far_other = image_part(packed_near, a_near, b_other[1:], start=first_other[1:])
        far_other = swap(far_other.astype(bf16), "split", 1)
        far_own = image_part(packed_near, a_near, b_own[1:], start=first_own[1:])
        far = (far_own + far_other.astype(f32)).astype(bf16)
        parts_far = [swap(far[at - 1], "tri", near * at) for at in range(1, groups)]
    own_other = image_part(packed_near, a_near, b_other[:1], start=first_other[:1])
    own_other = swap(own_other[0], "split", 1)
    own = image_part(packed_near, a_near, b_own[:1], start=first_own[:1])

    places = indices(*[rank ^ bits for bits in range(ranks)])
    smooth, gives, rests = combine(places, [own[0], own_other, *parts_far])
    gots = [swap(give, "rhs", bits) for bits, give in enumerate(gives, 1)]
    keep, give = gram_sums(places, indices(core), smooth, diag, currents, gots)
    keep, give, *rests = lax.optimization_barrier((keep, give, *rests))
    rests = [swap(rest, "rhs", bits) for bits, rest in enumerate(rests, 1)]
    shares, share_places = all_sum(keep, give, ranks, tris, (tri & 1) * ranks + rank, core)
    step, turn = solve(places, share_places, shares, columns)
    return finish(places, smooth, diag, step, turn, currents, gots, rests)


def solution(mesh):
    return jax.shard_map(
        body,
        mesh=mesh,
        in_specs=(P("rhs", ("tri", "split")), P("rhs"), P(), P(), P()),
        out_specs=(
            P("rhs", ("tri", "split")),
            P("rhs", ("tri", "split")),
            P("rhs", ("tri", "split")),
        ),
        check_vma=False,
    )
```

time: 152 us -> 102 us (0.67)
  Pallas kernels: 73.6 us -> 44.1 us
  waiting for transfers between devices: 41 us -> 30.7 us
  local copies, waits for them, and re-layouts: 8.41 us -> 0.94 us
    pallas_call x3 -> x5, Pallas kernels: 38.4 us -> 17.2 us  [the longest x1 11.9 us: solve(): pl.pallas_call(functools.partial(solve_kernel, columns, 32, len(shares) /...]
    pallas_call x1, Pallas kernels: 19.4 us -> 6.39 us  [geometry(): pl.pallas_call(functools.partial(geometry_kernel, scale), grid_spec=pltpu...]
    ppermute x17 -> x22, waiting for transfers between devices: 36.5 us -> 25.2 us  [swap(): return lax.ppermute(value, axis, [(at, at ^ bits) for at in range(size)])]
    unnamed x15 -> x8, local copies, waits for them, and re-layouts: 7.26 us -> 0.65 us
    pallas_call x3 -> x6, Pallas kernels: 15.8 us -> 20.4 us  [image_part(): pl.pallas_call(functools.partial(image_kernel, len(densities), start is n...]
    ppermute x17 -> x22, starting transfers between devices: 20.6 us -> 20.2 us  [swap(): return lax.ppermute(value, axis, [(at, at ^ bits) for at in range(size)])]
  transfers between devices with their start and end apart: 19 -> 24, of which waited for: 11 -> 12; matrix products, arithmetic and copies ran while one was open for 1% -> 1% of each run, Pallas kernels for 20% -> 39%
where the time goes in v2:
time: 102 us
  Pallas kernels  44.1 us (43%)
  waiting for transfers between devices  30.7 us (30%)
  starting transfers between devices  23.2 us (23%)
  other arithmetic  2.3 us (2%)
    ppermute x22, waiting for transfers between devices, swap(): return lax.ppermute(value, axis, [(at, at ^ bits) for at in range(size)])  25.2 us
    pallas_call x6, Pallas kernels, image_part(): pl.pallas_call(functools.partial(image_kernel, len(densities), start is n...  20.4 us
    ppermute x22, starting transfers between devices, swap(): return lax.ppermute(value, axis, [(at, at ^ bits) for at in range(size)])  20.2 us
    pallas_call x1, Pallas kernels, solve(): pl.pallas_call(functools.partial(solve_kernel, columns, 32, len(shares) /...  11.9 us
    pallas_call x1, Pallas kernels, geometry(): pl.pallas_call(functools.partial(geometry_kernel, scale), grid_spec=pltpu...  6.39 us
    ppermute x2, waiting for transfers between devices, pair_swap(): return lax.ppermute(value, ('tri', 'rhs'), perm)  5.54 us
    ppermute x2, starting transfers between devices, pair_swap(): return lax.ppermute(value, ('tri', 'rhs'), perm)  2.94 us
    pallas_call x1, Pallas kernels, finish(): pl.pallas_call(functools.partial(finish_kernel, ranks), in_specs=[SMEM] +...  2.56 us
  transfers between devices with their start and end apart: 24, of which 12 were waited for; matrix products, arithmetic and copies ran while one was open for 1% of the time, Pallas kernels for 39%

profile of v2, /device:TPU:0, one launch (start us, length us, event | category | flops | bytes accessed | tf_op | source)
XLA Modules:
  0.0 102.1 jit_solution(11857119833647139701)
XLA Ops:
  0.7 0.6 copy-done.3
  1.3 1.2 %fusion.1 = (bf16[128,1024]{1,0:T(8,128)(2,1)S(1)}, f32[128,1024]{1,0:T(8,128)S(1)}) fusion(f32[128,1024]{1,0:T(8,128)} %param.5, s32[1024]{0:T(1024)S(1)} %iota_add_fusion, s32[128]{0:T(128)S(1)} %copy-done.3), kind=kLoop, calls=%fused_computation.16 | loop fusion | flops 524288 | bytes 1315328 | tf_op jit(solution)/shard_map/convert_element_type | solution.py:473
  2.5 3.0 %collective-permute-start = (bf16[128,1024]{1,0:T(8,128)(2,1)S(1)}, bf16[128,1024]{1,0:T(8,128)(2,1)S(1)}, u32[]{:S(2)}, u32[]{:S(2)}) collective-permute-start(bf16[128,1024]{1,0:T(8,128)(2,1)S(1)} %get-tuple-element.39.refs_0_), channel_id=1, source_target_pairs={{0,4},{4,0},{8,12},{12,8},{16,20},{20,16},{24,28},{28,24},{1,5},{5... | collective-permute-start | bytes 786440 | tf_op jit(solution)/shard_map/ppermute | solution.py:432
  5.5 1.6 %collective-permute-start.1 = (bf16[128,1024]{1,0:T(8,128)(2,1)S(1)}, bf16[128,1024]{1,0:T(8,128)(2,1)}, u32[]{:S(2)}, u32[]{:S(2)}) collective-permute-start(bf16[128,1024]{1,0:T(8,128)(2,1)S(1)} %get-tuple-element.39.refs_0_), channel_id=1, source_target_pairs={{0,8},{4,12},{8,0},{12,4},{16,24},{20,28},{24,16},{28,20},{1,9},{5... | collective-permute-start | bytes 786440 | tf_op jit(solution)/shard_map/ppermute | solution.py:432
  7.1 0.1 stack.53.blocks_ref
  7.2 6.4 %geometry.1 = (bf16[5,32,1024]{2,1,0:T(8,128)(2,1)S(1)}, bf16[5,32,1024]{2,1,0:T(8,128)(2,1)S(1)}, f32[5,1,1024]{2,1,0:T(1,128)S(1)}) custom-call(s32[5]{0:T(128)S(1)} %stack.53.blocks_ref, f32[3,8192]{1,0:T(4,128)S(1)} %copy-done.1, s32[3,16384]{1,0:T(4,128)S(1)} %copy-done, s32[1,16384]{1,0:T(1,128)S(1)} %bitcast.28), custom_call_target="tpu_custom_call" | custom-call | tf_op jit(solution)/shard_map/geometry/pallas_call | solution.py:117
  13.7 2.0 %collective-permute-start.7 = (f32[128,1024]{1,0:T(8,128)S(1)}, f32[128,1024]{1,0:T(8,128)S(1)}, u32[]{:S(2)}, u32[]{:S(2)}) collective-permute-start(f32[128,1024]{1,0:T(8,128)S(1)} %get-tuple-element.40.refs_0_), channel_id=1, source_target_pairs={{0,2},{2,0},{1,3},{3,1},{4,6},{6,4},{5,7},{7,5},{8,10},{10,8},{9,1... | collective-permute-start | bytes 1572872 | tf_op jit(solution)/shard_map/ppermute | solution.py:432
  15.7 1.9 %image_part.6 = f32[2,128,1024]{2,1,0:T(8,128)S(1)} custom-call(bf16[128,1024]{1,0:T(8,128)(2,1)S(1)} %get-tuple-element.39.refs_0_, bf16[32,1024]{1,0:T(8,128)(2,1)S(1)} %get-tuple-element.47.refs_1_, bf16[2,32,1024]{2,1,0:T(8,128)(2,1)S(1)} %slice.50.refs_2_), custom_call_target="tpu_custom_call" | custom-call | flops 671088640 | bytes 2097152 | tf_op jit(solution)/shard_map/image_part/pallas_call | solution.py:184
  17.7 0.1 fusion.3
  17.8 2.3 %image_part.8 = f32[2,128,1024]{2,1,0:T(8,128)S(1)} custom-call(bf16[128,1024]{1,0:T(8,128)(2,1)S(1)} %get-tuple-element.39.refs_0_, bf16[32,1024]{1,0:T(8,128)(2,1)S(1)} %get-tuple-element.47.refs_1_, bf16[2,32,1024]{2,1,0:T(8,128)(2,1)S(1)} %collective-permute-done.3.refs_2_), custom_call_target="tpu_custom_call" | custom-call | flops 671088640 | bytes 2097152 | tf_op jit(solution)/shard_map/image_part/pallas_call | solution.py:184
  20.2 3.9 %image_part.11 = f32[1,128,1024]{2,1,0:T(8,128)S(1)} custom-call(bf16[128,1024]{1,0:T(8,128)(2,1)S(1)} %collective-permute-done.refs_0_, bf16[128,1024]{1,0:T(8,128)(2,1)} %collective-permute-done.1.refs_1_, bf16[128,1024]{1,0:T(8,128)(2,1)} %collective-permute-done.2.refs_2_, bf16[32,1024]{1,0:T(8,128)(2,1)S(1)} %get-tuple-element.50.refs_3_, ...), custom_call_target="tpu_custom_call" | custom-call | flops 1006632960 | bytes 1048576 | tf_op jit(solution)/shard_map/image_part/pallas_call | solution.py:184
  24.1 0.2 collective-permute-start.5
  24.3 4.7 %image_part.9 = f32[1,128,1024]{2,1,0:T(8,128)} custom-call(bf16[128,1024]{1,0:T(8,128)(2,1)S(1)} %collective-permute-done.refs_0_, bf16[128,1024]{1,0:T(8,128)(2,1)} %collective-permute-done.1.refs_1_, bf16[128,1024]{1,0:T(8,128)(2,1)} %collective-permute-done.2.refs_2_, bf16[32,1024]{1,0:T(8,128)(2,1)S(1)} %get-tuple-element.50.refs_3_, ...), custom_call_target="tpu_custom_call" | custom-call | flops 1006632960 | bytes 1048576 | tf_op jit(solution)/shard_map/image_part/pallas_call | solution.py:184
  29.0 0.3 collective-permute-start.4
  29.3 3.9 %image_part.10 = f32[1,128,1024]{2,1,0:T(8,128)S(1)} custom-call(bf16[128,1024]{1,0:T(8,128)(2,1)S(1)} %collective-permute-done.refs_0_, bf16[128,1024]{1,0:T(8,128)(2,1)} %collective-permute-done.1.refs_1_, bf16[128,1024]{1,0:T(8,128)(2,1)} %collective-permute-done.2.refs_2_, bf16[32,1024]{1,0:T(8,128)(2,1)S(1)} %get-tuple-element.50.refs_3_, ...), custom_call_target="tpu_custom_call" | custom-call | flops 1006632960 | bytes 1048576 | tf_op jit(solution)/shard_map/image_part/pallas_call | solution.py:184
  33.2 0.8 fusion
  34.0 2.6 %collective-permute-start.6 = (bf16[128,1024]{1,0:T(8,128)(2,1)}, bf16[128,1024]{1,0:T(8,128)(2,1)S(1)}, u32[]{:S(2)}, u32[]{:S(2)}) collective-permute-start(bf16[128,1024]{1,0:T(8,128)(2,1)} %fusion), channel_id=1, source_target_pairs={{0,16},{4,20},{8,24},{12,28},{16,0},{20,4},{24,8},{28,12},{1,17},{... | collective-permute-start | bytes 786440 | tf_op jit(solution)/shard_map/ppermute | solution.py:432
  36.6 0.1 pad_add_fusion.place_ref
  36.6 3.9 %image_part.7 = f32[1,128,1024]{2,1,0:T(8,128)S(1)} custom-call(bf16[128,1024]{1,0:T(8,128)(2,1)S(1)} %collective-permute-done.refs_0_, bf16[128,1024]{1,0:T(8,128)(2,1)} %collective-permute-done.1.refs_1_, bf16[128,1024]{1,0:T(8,128)(2,1)} %collective-permute-done.2.refs_2_, bf16[32,1024]{1,0:T(8,128)(2,1)S(1)} %get-tuple-element.50.refs_3_, ...), custom_call_target="tpu_custom_call" | custom-call | flops 1006632960 | bytes 1048576 | tf_op jit(solution)/shard_map/image_part/pallas_call | solution.py:184
  40.5 8.6 %collective-permute-done.6.refs_2_ = bf16[128,1024]{1,0:T(8,128)(2,1)S(1)} collective-permute-done((bf16[128,1024]{1,0:T(8,128)(2,1)}, bf16[128,1024]{1,0:T(8,128)(2,1)S(1)}, u32[]{:S(2)}, u32[]{:S(2)}) %collective-permute-start.6) | collective-permute-done | bytes 262176 | tf_op jit(solution)/shard_map/ppermute | solution.py:432
  49.1 0.7 combine.1
  49.8 0.5 collective-permute-start.8
  50.3 4.5 %collective-permute-done.8.refs_2_ = bf16[128,512]{1,0:T(8,128)(2,1)S(1)} collective-permute-done((bf16[128,512]{1,0:T(8,128)(2,1)S(1)}, bf16[128,512]{1,0:T(8,128)(2,1)S(1)}, u32[]{:S(2)}, u32[]{:S(2)}) %collective-permute-start.8) | collective-permute-done | bytes 131104 | tf_op jit(solution)/shard_map/ppermute | solution.py:432
  54.8 1.5 %gram.1 = (f32[384,256]{1,0:T(8,128)S(1)}, f32[384,256]{1,0:T(8,128)S(1)}) custom-call(s32[2]{0:T(128)S(1)} %pad_add_fusion.place_ref, s32[1]{0:T(128)} %bitcast.20.core_ref, f32[128,1024]{1,0:T(8,128)S(1)} %get-tuple-element.22.smooth_ref, f32[1,1024]{1,0:T(1,128)S(1)} %slice_bitcast_fusion.4.diag_ref, f32[128,1024]{1,0:T(8,128)S(1)} %get-tuple-element.40.refs_0_, ...), custom_call_target="tpu_custom_call" | custom-call | tf_op jit(solution)/shard_map/gram/pallas_call | solution.py:263
  56.4 0.1 broadcast_add_fusion.1
  56.5 1.6 %collective-permute-done.9.got_ref = f32[384,256]{1,0:T(8,128)S(1)} collective-permute-done((f32[384,256]{1,0:T(8,128)S(1)}, f32[384,256]{1,0:T(8,128)S(1)}, u32[]{:S(2)}, u32[]{:S(2)}) %collective-permute-start.9) | collective-permute-done | bytes 393248 | tf_op jit(solution)/shard_map/ppermute | solution.py:432
  58.1 0.6 shares.1
  58.7 0.5 collective-permute-start.10
  59.2 1.5 %collective-permute-start.11 = (f32[96,256]{1,0:T(8,128)S(1)}, f32[96,256]{1,0:T(8,128)S(1)}, u32[]{:S(2)}, u32[]{:S(2)}) collective-permute-start(f32[96,256]{1,0:T(8,128)S(1)} %get-tuple-element.32), channel_id=1, source_target_pairs={{0,4},{4,0},{8,12},{12,8},{16,20},{20,16},{24,28},{28,24},{1,5},{5... | collective-permute-start | bytes 294920 | tf_op jit(solution)/shard_map/ppermute | solution.py:432
  60.8 1.5 %collective-permute-start.12 = (f32[96,256]{1,0:T(8,128)S(1)}, f32[96,256]{1,0:T(8,128)S(1)}, u32[]{:S(2)}, u32[]{:S(2)}) collective-permute-start(f32[96,256]{1,0:T(8,128)S(1)} %get-tuple-element.33), channel_id=1, source_target_pairs={{0,6},{2,4},{4,2},{6,0},{8,14},{10,12},{12,10},{14,8},{16,22},{18,... | collective-permute-start | bytes 294920 | tf_op jit(solution)/shard_map/ppermute | solution.py:445
  62.3 1.3 %collective-permute-done.10 = f32[96,256]{1,0:T(8,128)S(1)} collective-permute-done((f32[96,256]{1,0:T(8,128)S(1)}, f32[96,256]{1,0:T(8,128)S(1)}, u32[]{:S(2)}, u32[]{:S(2)}) %collective-permute-start.10) | collective-permute-done | bytes 98336 | tf_op jit(solution)/shard_map/ppermute | solution.py:432
  63.6 0.2 collective-permute-done.11
  63.9 3.1 %collective-permute-done.12 = f32[96,256]{1,0:T(8,128)S(1)} collective-permute-done((f32[96,256]{1,0:T(8,128)S(1)}, f32[96,256]{1,0:T(8,128)S(1)}, u32[]{:S(2)}, u32[]{:S(2)}) %collective-permute-start.12) | collective-permute-done | bytes 98336 | tf_op jit(solution)/shard_map/ppermute | solution.py:445
  67.0 1.3 %collective-permute-start.13 = (f32[96,256]{1,0:T(8,128)S(1)}, f32[96,256]{1,0:T(8,128)S(1)}, u32[]{:S(2)}, u32[]{:S(2)}) collective-permute-start(f32[96,256]{1,0:T(8,128)S(1)} %add_add_fusion.1), channel_id=1, source_target_pairs={{0,8},{4,12},{8,0},{12,4},{16,24},{20,28},{24,16},{28,20},{1,9},{5... | collective-permute-start | bytes 294920 | tf_op jit(solution)/shard_map/ppermute | solution.py:432
  68.3 3.3 %collective-permute-start.14 = (f32[96,256]{1,0:T(8,128)S(1)}, f32[96,256]{1,0:T(8,128)S(1)}, u32[]{:S(2)}, u32[]{:S(2)}) collective-permute-start(f32[96,256]{1,0:T(8,128)S(1)} %add_add_fusion.1), channel_id=1, source_target_pairs={{0,16},{4,20},{8,24},{12,28},{16,0},{20,4},{24,8},{28,12},{1,17},{... | collective-permute-start | bytes 294920 | tf_op jit(solution)/shard_map/ppermute | solution.py:432
  71.6 0.8 collective-permute-start.23
  72.4 0.1 collective-permute-done.13
  72.6 6.1 %collective-permute-done.14 = f32[96,256]{1,0:T(8,128)S(1)} collective-permute-done((f32[96,256]{1,0:T(8,128)S(1)}, f32[96,256]{1,0:T(8,128)S(1)}, u32[]{:S(2)}, u32[]{:S(2)}) %collective-permute-start.14) | collective-permute-done | bytes 98336 | tf_op jit(solution)/shard_map/ppermute | solution.py:432
  78.7 0.4 collective-permute-start.16
  79.0 1.7 %collective-permute-start.17 = (f32[96,256]{1,0:T(8,128)S(1)}, f32[96,256]{1,0:T(8,128)S(1)}, u32[]{:S(2)}, u32[]{:S(2)}) collective-permute-start(f32[96,256]{1,0:T(8,128)S(1)} %add_add_fusion.refs_0_), channel_id=1, source_target_pairs={{0,4},{4,0},{8,12},{12,8},{16,20},{20,16},{24,28},{28,24},{1,5},{5... | collective-permute-start | bytes 294920 | tf_op jit(solution)/shard_map/ppermute | solution.py:432
  80.8 1.4 %collective-permute-start.18 = (f32[96,256]{1,0:T(8,128)S(1)}, f32[96,256]{1,0:T(8,128)S(1)}, u32[]{:S(2)}, u32[]{:S(2)}) collective-permute-start(f32[96,256]{1,0:T(8,128)S(1)} %add_add_fusion.refs_0_), channel_id=1, source_target_pairs={{0,6},{2,4},{4,2},{6,0},{8,14},{10,12},{12,10},{14,8},{16,22},{18,... | collective-permute-start | bytes 294920 | tf_op jit(solution)/shard_map/ppermute | solution.py:445
  82.2 1.1 %collective-permute-done.16.refs_1_ = f32[96,256]{1,0:T(8,128)S(1)} collective-permute-done((f32[96,256]{1,0:T(8,128)S(1)}, f32[96,256]{1,0:T(8,128)S(1)}, u32[]{:S(2)}, u32[]{:S(2)}) %collective-permute-start.16) | collective-permute-done | bytes 98336 | tf_op jit(solution)/shard_map/ppermute | solution.py:432
  83.4 0.3 collective-permute-done.17.refs_2_
  83.7 0.2 collective-permute-start.21
  83.9 2.4 %collective-permute-done.18.refs_3_ = f32[96,256]{1,0:T(8,128)S(1)} collective-permute-done((f32[96,256]{1,0:T(8,128)S(1)}, f32[96,256]{1,0:T(8,128)S(1)}, u32[]{:S(2)}, u32[]{:S(2)}) %collective-permute-start.18) | collective-permute-done | bytes 98336 | tf_op jit(solution)/shard_map/ppermute | solution.py:445
  86.4 1.2 %collective-permute-done.22.refs_7_ = f32[96,256]{1,0:T(8,128)S(1)} collective-permute-done((f32[96,256]{1,0:T(8,128)S(1)}, f32[96,256]{1,0:T(8,128)S(1)}, u32[]{:S(2)}, u32[]{:S(2)}) %collective-permute-start.22) | collective-permute-done | bytes 98336 | tf_op jit(solution)/shard_map/ppermute | solution.py:432
  87.6 11.9 %solve.1 = (f32[128,256]{1,0:T(8,128)S(1)}, f32[128,256]{1,0:T(8,128)S(1)}) custom-call(s32[2]{0:T(128)S(1)} %pad_add_fusion.place_ref, s32[8]{0:T(128)S(1)} %pad_add_fusion.2.share_ref, f32[96,256]{1,0:T(8,128)S(1)} %add_add_fusion.refs_0_, f32[96,256]{1,0:T(8,128)S(1)} %collective-permute-done.16.refs_1_, f32[96,256]{1,0:T(8,128)S(1)} %collective-permute-done.17.refs_2_, ...), custom_call_target="tpu_custom_call" | custom-call | tf_op jit(solution)/shard_map/solve/pallas_call | solution.py:374
  99.5 2.6 %finish.1 = (f32[128,1024]{1,0:T(8,128)}, f32[128,1024]{1,0:T(8,128)}, f32[128,1024]{1,0:T(8,128)}) custom-call(s32[2]{0:T(128)S(1)} %pad_add_fusion.place_ref, f32[128,1024]{1,0:T(8,128)S(1)} %get-tuple-element.22.smooth_ref, f32[1,1024]{1,0:T(1,128)S(1)} %slice_bitcast_fusion.4.diag_ref, f32[128,256]{1,0:T(8,128)S(1)} %get-tuple-element.34.step_ref, ...), custom_call_target="tpu_custom_call" | custom-call | tf_op jit(solution)/shard_map/finish/pallas_call | solution.py:419
  (38 shorter events, 0.5 us)
Async XLA Ops:
  0.6 0.7 copy-start.3
  1.3 5.9 %copy-start = (s32[3,16384]{1,0:T(4,128)S(1)}, s32[3,16384]{1,0:T(4,128)}, u32[]{:S(2)}) copy-start(s32[3,16384]{1,0:T(4,128)} %corners_ref.1) | copy-start | bytes 589828
  1.3 5.9 %copy-start.1 = (f32[3,8192]{1,0:T(4,128)S(1)}, f32[3,8192]{1,0:T(4,128)}, u32[]{:S(2)}) copy-start(f32[3,8192]{1,0:T(4,128)} %vertices_ref.1) | copy-start | bytes 294916
  1.3 5.9 %copy-start.2 = (s32[16384]{0:T(1024)S(1)}, s32[16384]{0:T(1024)}, u32[]{:S(2)}) copy-start(s32[16384]{0:T(1024)} %param.9) | copy-start | bytes 196612
  2.5 17.6 %collective-permute-start = (bf16[128,1024]{1,0:T(8,128)(2,1)S(1)}, bf16[128,1024]{1,0:T(8,128)(2,1)S(1)}, u32[]{:S(2)}, u32[]{:S(2)}) collective-permute-start(bf16[128,1024]{1,0:T(8,128)(2,1)S(1)} %get-tuple-element.39.refs_0_), channel_id=1, source_target_pairs={{0,4},{4,0},{8,12},{12,8},{16,20},{20,16},{24,28},{28,24},{1,5},{5... | collective-permute-start | bytes 786440 | tf_op jit(solution)/shard_map/ppermute | solution.py:432
  5.5 14.6 %collective-permute-start.1 = (bf16[128,1024]{1,0:T(8,128)(2,1)S(1)}, bf16[128,1024]{1,0:T(8,128)(2,1)}, u32[]{:S(2)}, u32[]{:S(2)}) collective-permute-start(bf16[128,1024]{1,0:T(8,128)(2,1)S(1)} %get-tuple-element.39.refs_0_), channel_id=1, source_target_pairs={{0,8},{4,12},{8,0},{12,4},{16,24},{20,28},{24,16},{28,20},{1,9},{5... | collective-permute-start | bytes 786440 | tf_op jit(solution)/shard_map/ppermute | solution.py:432
  7.1 13.1 %collective-permute-start.2 = (bf16[128,1024]{1,0:T(8,128)(2,1)S(1)}, bf16[128,1024]{1,0:T(8,128)(2,1)}, u32[]{:S(2)}, u32[]{:S(2)}) collective-permute-start(bf16[128,1024]{1,0:T(8,128)(2,1)S(1)} %get-tuple-element.39.refs_0_), channel_id=1, source_target_pairs={{0,12},{4,8},{8,4},{12,0},{16,28},{20,24},{24,20},{28,16},{1,13},{... | collective-permute-start | bytes 786440 | tf_op jit(solution)/shard_map/ppermute | solution.py:432
  13.6 4.1 %collective-permute-start.3 = (bf16[2,32,1024]{2,1,0:T(8,128)(2,1)S(1)}, bf16[2,32,1024]{2,1,0:T(8,128)(2,1)S(1)}, u32[]{:S(2)}, u32[]{:S(2)}) collective-permute-start(bf16[2,32,1024]{2,1,0:T(8,128)(2,1)S(1)} %slice.50.refs_2_), channel_id=1, source_target_pairs={{0,1},{1,0},{2,3},{3,2},{4,5},{5,4},{6,7},{7,6},{8,9},{9,8},{10,11... | collective-permute-start | bytes 393224 | tf_op jit(solution)/shard_map/ppermute | solution.py:432
  13.7 36.6 %collective-permute-start.7 = (f32[128,1024]{1,0:T(8,128)S(1)}, f32[128,1024]{1,0:T(8,128)S(1)}, u32[]{:S(2)}, u32[]{:S(2)}) collective-permute-start(f32[128,1024]{1,0:T(8,128)S(1)} %get-tuple-element.40.refs_0_), channel_id=1, source_target_pairs={{0,2},{2,0},{1,3},{3,1},{4,6},{6,4},{5,7},{7,5},{8,10},{10,8},{9,1... | collective-permute-start | bytes 1572872 | tf_op jit(solution)/shard_map/ppermute | solution.py:432
  24.1 9.1 %collective-permute-start.5 = (bf16[1,128,1024]{2,1,0:T(8,128)(2,1)S(1)}, bf16[1,128,1024]{2,1,0:T(8,128)(2,1)S(1)}, u32[]{:S(2)}, u32[]{:S(2)}) collective-permute-start(bf16[1,128,1024]{2,1,0:T(8,128)(2,1)S(1)} %convert_element_type.14), channel_id=1, source_target_pairs={{0,1},{1,0},{2,3},{3,2},{4,5},{5,4},{6,7},{7,6},{8,9},{9,8},{10,11... | collective-permute-start | bytes 786440 | tf_op jit(solution)/shard_map/ppermute | solution.py:432
  29.0 20.1 %collective-permute-start.4 = (f32[128,1024]{1,0:T(8,128)}, f32[128,1024]{1,0:T(8,128)S(1)}, u32[]{:S(2)}, u32[]{:S(2)}) collective-permute-start(f32[128,1024]{1,0:T(8,128)} %bitcast.13), channel_id=1, source_target_pairs={{0,1},{1,0},{2,3},{3,2},{4,5},{5,4},{6,7},{7,6},{8,9},{9,8},{10,11... | collective-permute-start | bytes 1572872 | tf_op jit(solution)/shard_map/ppermute | solution.py:432
  34.0 15.1 %collective-permute-start.6 = (bf16[128,1024]{1,0:T(8,128)(2,1)}, bf16[128,1024]{1,0:T(8,128)(2,1)S(1)}, u32[]{:S(2)}, u32[]{:S(2)}) collective-permute-start(bf16[128,1024]{1,0:T(8,128)(2,1)} %fusion), channel_id=1, source_target_pairs={{0,16},{4,20},{8,24},{12,28},{16,0},{20,4},{24,8},{28,12},{1,17},{... | collective-permute-start | bytes 786440 | tf_op jit(solution)/shard_map/ppermute | solution.py:432
  49.8 5.0 %collective-permute-start.8 = (bf16[128,512]{1,0:T(8,128)(2,1)S(1)}, bf16[128,512]{1,0:T(8,128)(2,1)S(1)}, u32[]{:S(2)}, u32[]{:S(2)}) collective-permute-start(bf16[128,512]{1,0:T(8,128)(2,1)S(1)} %get-tuple-element.24), channel_id=1, source_target_pairs={{0,2},{2,0},{1,3},{3,1},{4,6},{6,4},{5,7},{7,5},{8,10},{10,8},{9,1... | collective-permute-start | bytes 393224 | tf_op jit(solution)/shard_map/ppermute | solution.py:432
  56.3 1.8 %collective-permute-start.9 = (f32[384,256]{1,0:T(8,128)S(1)}, f32[384,256]{1,0:T(8,128)S(1)}, u32[]{:S(2)}, u32[]{:S(2)}) collective-permute-start(f32[384,256]{1,0:T(8,128)S(1)} %get-tuple-element.29), channel_id=1, source_target_pairs={{0,1},{1,0},{2,3},{3,2},{4,5},{5,4},{6,7},{7,6},{8,9},{9,8},{10,11... | collective-permute-start | bytes 1179656 | tf_op jit(solution)/shard_map/ppermute | solution.py:432
  58.7 4.9 %collective-permute-start.10 = (f32[96,256]{1,0:T(8,128)S(1)}, f32[96,256]{1,0:T(8,128)S(1)}, u32[]{:S(2)}, u32[]{:S(2)}) collective-permute-start(f32[96,256]{1,0:T(8,128)S(1)} %get-tuple-element.31), channel_id=1, source_target_pairs={{0,2},{2,0},{1,3},{3,1},{4,6},{6,4},{5,7},{7,5},{8,10},{10,8},{9,1... | collective-permute-start | bytes 294920 | tf_op jit(solution)/shard_map/ppermute | solution.py:432
  59.2 4.6 %collective-permute-start.11 = (f32[96,256]{1,0:T(8,128)S(1)}, f32[96,256]{1,0:T(8,128)S(1)}, u32[]{:S(2)}, u32[]{:S(2)}) collective-permute-start(f32[96,256]{1,0:T(8,128)S(1)} %get-tuple-element.32), channel_id=1, source_target_pairs={{0,4},{4,0},{8,12},{12,8},{16,20},{20,16},{24,28},{28,24},{1,5},{5... | collective-permute-start | bytes 294920 | tf_op jit(solution)/shard_map/ppermute | solution.py:432
  60.8 6.2 %collective-permute-start.12 = (f32[96,256]{1,0:T(8,128)S(1)}, f32[96,256]{1,0:T(8,128)S(1)}, u32[]{:S(2)}, u32[]{:S(2)}) collective-permute-start(f32[96,256]{1,0:T(8,128)S(1)} %get-tuple-element.33), channel_id=1, source_target_pairs={{0,6},{2,4},{4,2},{6,0},{8,14},{10,12},{12,10},{14,8},{16,22},{18,... | collective-permute-start | bytes 294920 | tf_op jit(solution)/shard_map/ppermute | solution.py:445
  67.0 5.6 %collective-permute-start.13 = (f32[96,256]{1,0:T(8,128)S(1)}, f32[96,256]{1,0:T(8,128)S(1)}, u32[]{:S(2)}, u32[]{:S(2)}) collective-permute-start(f32[96,256]{1,0:T(8,128)S(1)} %add_add_fusion.1), channel_id=1, source_target_pairs={{0,8},{4,12},{8,0},{12,4},{16,24},{20,28},{24,16},{28,20},{1,9},{5... | collective-permute-start | bytes 294920 | tf_op jit(solution)/shard_map/ppermute | solution.py:432
  68.3 10.3 %collective-permute-start.14 = (f32[96,256]{1,0:T(8,128)S(1)}, f32[96,256]{1,0:T(8,128)S(1)}, u32[]{:S(2)}, u32[]{:S(2)}) collective-permute-start(f32[96,256]{1,0:T(8,128)S(1)} %add_add_fusion.1), channel_id=1, source_target_pairs={{0,16},{4,20},{8,24},{12,28},{16,0},{20,4},{24,8},{28,12},{1,17},{... | collective-permute-start | bytes 294920 | tf_op jit(solution)/shard_map/ppermute | solution.py:432
  71.6 7.0 %collective-permute-start.15 = (f32[96,256]{1,0:T(8,128)S(1)}, f32[96,256]{1,0:T(8,128)S(1)}, u32[]{:S(2)}, u32[]{:S(2)}) collective-permute-start(f32[96,256]{1,0:T(8,128)S(1)} %add_add_fusion.1), channel_id=1, source_target_pairs={{0,24},{4,28},{8,16},{12,20},{16,8},{20,12},{24,0},{28,4},{1,25},{... | collective-permute-start | bytes 294920 | tf_op jit(solution)/shard_map/ppermute | solution.py:432
  71.6 27.9 %collective-permute-start.23 = (bf16[128,512]{1,0:T(8,128)(2,1)S(1)}, bf16[128,512]{1,0:T(8,128)(2,1)S(1)}, u32[]{:S(2)}, u32[]{:S(2)}) collective-permute-start(bf16[128,512]{1,0:T(8,128)(2,1)S(1)} %get-tuple-element.36), channel_id=1, source_target_pairs={{0,2},{2,0},{1,3},{3,1},{4,6},{6,4},{5,7},{7,5},{8,10},{10,8},{9,1... | collective-permute-start | bytes 393224 | tf_op jit(solution)/shard_map/ppermute | solution.py:432
  78.7 4.7 %collective-permute-start.16 = (f32[96,256]{1,0:T(8,128)S(1)}, f32[96,256]{1,0:T(8,128)S(1)}, u32[]{:S(2)}, u32[]{:S(2)}) collective-permute-start(f32[96,256]{1,0:T(8,128)S(1)} %add_add_fusion.refs_0_), channel_id=1, source_target_pairs={{0,2},{2,0},{1,3},{3,1},{4,6},{6,4},{5,7},{7,5},{8,10},{10,8},{9,1... | collective-permute-start | bytes 294920 | tf_op jit(solution)/shard_map/ppermute | solution.py:432
  79.0 4.6 %collective-permute-start.17 = (f32[96,256]{1,0:T(8,128)S(1)}, f32[96,256]{1,0:T(8,128)S(1)}, u32[]{:S(2)}, u32[]{:S(2)}) collective-permute-start(f32[96,256]{1,0:T(8,128)S(1)} %add_add_fusion.refs_0_), channel_id=1, source_target_pairs={{0,4},{4,0},{8,12},{12,8},{16,20},{20,16},{24,28},{28,24},{1,5},{5... | collective-permute-start | bytes 294920 | tf_op jit(solution)/shard_map/ppermute | solution.py:432
  80.8 5.5 %collective-permute-start.18 = (f32[96,256]{1,0:T(8,128)S(1)}, f32[96,256]{1,0:T(8,128)S(1)}, u32[]{:S(2)}, u32[]{:S(2)}) collective-permute-start(f32[96,256]{1,0:T(8,128)S(1)} %add_add_fusion.refs_0_), channel_id=1, source_target_pairs={{0,6},{2,4},{4,2},{6,0},{8,14},{10,12},{12,10},{14,8},{16,22},{18,... | collective-permute-start | bytes 294920 | tf_op jit(solution)/shard_map/ppermute | solution.py:445
  82.2 4.2 %collective-permute-start.19 = (f32[96,256]{1,0:T(8,128)S(1)}, f32[96,256]{1,0:T(8,128)S(1)}, u32[]{:S(2)}, u32[]{:S(2)}) collective-permute-start(f32[96,256]{1,0:T(8,128)S(1)} %add_add_fusion.refs_0_), channel_id=1, source_target_pairs={{0,1},{1,0},{2,3},{3,2},{4,5},{5,4},{6,7},{7,6},{8,9},{9,8},{10,11... | collective-permute-start | bytes 294920 | tf_op jit(solution)/shard_map/ppermute | solution.py:432
  83.4 3.0 %collective-permute-start.20 = (f32[96,256]{1,0:T(8,128)S(1)}, f32[96,256]{1,0:T(8,128)S(1)}, u32[]{:S(2)}, u32[]{:S(2)}) collective-permute-start(f32[96,256]{1,0:T(8,128)S(1)} %collective-permute-done.16.refs_1_), channel_id=1, source_target_pairs={{0,1},{1,0},{2,3},{3,2},{4,5},{5,4},{6,7},{7,6},{8,9},{9,8},{10,11... | collective-permute-start | bytes 294920 | tf_op jit(solution)/shard_map/ppermute | solution.py:432
  83.7 2.7 %collective-permute-start.21 = (f32[96,256]{1,0:T(8,128)S(1)}, f32[96,256]{1,0:T(8,128)S(1)}, u32[]{:S(2)}, u32[]{:S(2)}) collective-permute-start(f32[96,256]{1,0:T(8,128)S(1)} %collective-permute-done.17.refs_2_), channel_id=1, source_target_pairs={{0,1},{1,0},{2,3},{3,2},{4,5},{5,4},{6,7},{7,6},{8,9},{9,8},{10,11... | collective-permute-start | bytes 294920 | tf_op jit(solution)/shard_map/ppermute | solution.py:432
  86.3 1.3 %collective-permute-start.22 = (f32[96,256]{1,0:T(8,128)S(1)}, f32[96,256]{1,0:T(8,128)S(1)}, u32[]{:S(2)}, u32[]{:S(2)}) collective-permute-start(f32[96,256]{1,0:T(8,128)S(1)} %collective-permute-done.18.refs_3_), channel_id=1, source_target_pairs={{0,1},{1,0},{2,3},{3,2},{4,5},{5,4},{6,7},{7,6},{8,9},{9,8},{10,11... | collective-permute-start | bytes 294920 | tf_op jit(solution)/shard_map/ppermute | solution.py:432

commit v3 on v2

v3 whole, which is shorter than its diff:
```python
import functools
import math

import jax
import jax.numpy as jnp
from jax import lax
from jax.experimental import pallas as pl
from jax.experimental.pallas import tpu as pltpu
from jax.sharding import PartitionSpec as P

smooth_sq = 0.01
self_term = 1.0
inject = 3.0
f32 = jnp.float32
bf16 = jnp.bfloat16
LANES = 128
FEATURES = 32
PAIRS = ((0, 0), (0, 1), (1, 0), (1, 1), (0, 2), (2, 0))
VMEM = pl.BlockSpec(memory_space=pltpu.VMEM)
SMEM = pl.BlockSpec(memory_space=pltpu.SMEM)
SMALL = pl.CostEstimate(flops=1024, bytes_accessed=1024, transcendentals=0)


def dot(a, b, ca, cb, precision=None):
    return lax.dot_general(
        a, b, (((ca,), (cb,)), ((), ())), precision=precision, preferred_element_type=f32
    )


def exact_dot(a, b, ca, cb):
    return dot(a, b, ca, cb, lax.Precision.HIGHEST)


def close_dot(a, b, ca, cb):
    a_high, b_high = a.astype(bf16), b.astype(bf16)
    a_low = (a - a_high.astype(f32)).astype(bf16)
    b_low = (b - b_high.astype(f32)).astype(bf16)
    return (dot(a_low, b_high, ca, cb) + dot(a_high, b_low, ca, cb)) + dot(a_high, b_high, ca, cb)


def params(mebibytes=16):
    return pltpu.CompilerParams(vmem_limit_bytes=mebibytes * 1024 * 1024)


def pieces_of(value):
    high = value.astype(bf16).astype(f32)
    rest = value - high
    middle = rest.astype(bf16).astype(f32)
    return (high, middle, rest - middle)


def geometry_kernel(
    scale, blocks_ref, vertices_ref, corners_ref, layers_ref, a_ref, b_ref, diag_ref, plain, table, a_rows, b_rows
):
    count = corners_ref.shape[1]
    tops = plain.shape[0]

    @pl.when(pl.program_id(0) == 0)
    def _():
        for axis in range(3):
            for top in range(tops):
                plain[top : top + 1, axis * LANES : (axis + 1) * LANES] = vertices_ref[
                    axis : axis + 1, top * LANES : (top + 1) * LANES
                ]
        for at, part in enumerate(pieces_of(plain[...])):
            table[at * tops : (at + 1) * tops, :] = part.astype(bf16)

    top_iota = lax.broadcasted_iota(jnp.int32, (tops, count), 0)
    low_iota = lax.broadcasted_iota(jnp.int32, (LANES, count), 0)
    points = []
    for corner in range(3):
        index = corners_ref[corner : corner + 1, :]
        top = jnp.where(top_iota == (index >> 7), 1.0, 0.0).astype(bf16)
        low = low_iota == (index & (LANES - 1))
        found = dot(table[...], jnp.concatenate([top, top, top], axis=0), 0, 0)
        points.append(
            [
                jnp.sum(jnp.where(low, found[axis * LANES : (axis + 1) * LANES], 0.0), axis=0, keepdims=True)
                for axis in range(3)
            ]
        )
    p0, p1, p2 = points
    centre = [(p0[k] + p1[k] + p2[k]) / 3.0 for k in range(3)]
    e1 = [p1[k] - p0[k] for k in range(3)]
    e2 = [p2[k] - p0[k] for k in range(3)]
    cross_x = e1[1] * e2[2] - e1[2] * e2[1]
    cross_y = e1[2] * e2[0] - e1[0] * e2[2]
    cross_z = e1[0] * e2[1] - e1[1] * e2[0]
    area_sq = cross_x * cross_x + cross_y * cross_y + cross_z * cross_z
    layers = layers_ref[...]
    factor = jnp.where(layers == 0, 1.0, jnp.where(layers == 1, 0.3, 0.8)).astype(f32)
    weight = factor * (0.5 + area_sq / (1.0 + area_sq))
    unit = 1.0 / (scale * (weight * weight))
    norm = centre[0] * centre[0] + centre[1] * centre[1] + centre[2] * centre[2]
    a_side = [unit * norm, unit] + [unit * c for c in centre]
    b_side = [unit, unit * (norm + smooth_sq)] + [-2.0 * unit * c for c in centre]
    a_parts = [pieces_of(value) for value in a_side]
    b_parts = [pieces_of(value) for value in b_side]
    row = 0
    for a_piece, b_piece in PAIRS:
        for term in range(5):
            a_rows[row : row + 1, :] = a_parts[term][a_piece]
            b_rows[row : row + 1, :] = b_parts[term][b_piece]
            row += 1
    blank = jnp.zeros((FEATURES - row, count), f32)
    a_rows[row:, :] = blank
    b_rows[row:, :] = blank
    a_ref[...] = a_rows[...].astype(bf16)
    b_ref[...] = b_rows[...].astype(bf16)
    diag_ref[...] = weight * weight * (lax.rsqrt(jnp.full_like(weight, smooth_sq)) * scale + self_term)


def geometry(blocks, vertices, corners, layers, count, scale):
    n = blocks.shape[0]
    points = vertices.shape[1]
    tops = points // LANES
    return pl.pallas_call(
        functools.partial(geometry_kernel, scale),
        grid_spec=pltpu.PrefetchScalarGridSpec(
            num_scalar_prefetch=1,
            grid=(n,),
            in_specs=[
                pl.BlockSpec((3, points), lambda g, blk: (0, 0)),
                pl.BlockSpec((3, count), lambda g, blk: (0, blk[g])),
                pl.BlockSpec((1, count), lambda g, blk: (0, blk[g])),
            ],
            out_specs=[
                pl.BlockSpec((None, FEATURES, count), lambda g, blk: (g, 0, 0)),
                pl.BlockSpec((None, FEATURES, count), lambda g, blk: (g, 0, 0)),
                pl.BlockSpec((None, 1, count), lambda g, blk: (g, 0, 0)),
            ],
            scratch_shapes=[
                pltpu.VMEM((tops, 3 * LANES), f32),
                pltpu.VMEM((3 * tops, 3 * LANES), bf16),
                pltpu.VMEM((FEATURES, count), f32),
                pltpu.VMEM((FEATURES, count), f32),
            ],
        ),
        out_shape=(
            jax.ShapeDtypeStruct((n, FEATURES, count), bf16),
            jax.ShapeDtypeStruct((n, FEATURES, count), bf16),
            jax.ShapeDtypeStruct((n, 1, count), f32),
        ),
        compiler_params=params(),
        name="geometry",
    )(blocks, vertices, corners, layers[None, :])


def image_kernel(sources, slots, targets, has_start, extras, first_ref, *refs):
    refs = list(refs)
    densities = [refs.pop(0) for _ in sources]
    sides = [refs.pop(0) for _ in range(1 + max(which for which, _ in [*slots, *[t[:2] for t in targets]]))]
    starts = [refs.pop(0) for _ in targets] if has_start else [None] * len(targets)
    more = [refs.pop(0) for _ in range(extras)]
    count = densities[0].shape[1]
    half = count // 2
    chunk = min(512, count)
    for at, (which, slot, part) in enumerate(targets):
        columns, width = refs[at].shape
        if part is None:
            lanes = slice(None)
        else:
            place = first_ref[0] if part == 0 else 1 - first_ref[0]
            lanes = pl.ds(pl.multiple_of(place * half, half), half)
        b = sides[which][slot, :, lanes]
        acc = starts[at][:, lanes] if has_start else jnp.zeros((columns, width), f32)
        for source, (density, (side, a_slot)) in enumerate(zip(densities, slots)):
            for begin in range(0, count, chunk):
                tile = lax.rsqrt(dot(sides[side][a_slot, :, begin : begin + chunk], b, 0, 0))
                acc = acc + dot(density[:, begin : begin + chunk], tile.astype(bf16), 1, 0)
        if at < extras:
            acc = acc + more[at][...].astype(f32)
        refs[at][...] = acc.astype(refs[at].dtype)


def image_part(first, densities, slots, sides, targets, starts=None, extras=(), kind=f32):
    columns, count = densities[0].shape
    sides = sides[: 1 + max(which for which, _ in [*slots, *[t[:2] for t in targets]])]
    operands = [first, *densities, *sides, *(starts or []), *extras]
    widths = [count if part is None else count // 2 for _, _, part in targets]
    return pl.pallas_call(
        functools.partial(image_kernel, range(len(densities)), slots, targets, bool(starts), len(extras)),
        in_specs=[SMEM] + [VMEM] * (len(operands) - 1),
        out_specs=[VMEM] * len(targets),
        out_shape=[jax.ShapeDtypeStruct((columns, width), kind) for width in widths],
        compiler_params=params(20),
        cost_estimate=SMALL,
        name="image_part",
    )(*operands)


def half_of(mine, other):
    return (mine > other).astype(jnp.int32)


def stack_kernel(near, *refs):
    a_ref, out_ref = refs[near:]
    columns = refs[0].shape[0]
    for source in range(near):
        out_ref[source * columns : (source + 1) * columns, :] = refs[source][...]
        side = near * columns + source * FEATURES
        out_ref[side : side + FEATURES, :] = a_ref[near - 1 - source]


def stack_rows(sources, a_side, near):
    columns, count = sources[0].shape
    return pl.pallas_call(
        functools.partial(stack_kernel, near),
        in_specs=[VMEM] * (near + 1),
        out_specs=VMEM,
        out_shape=jax.ShapeDtypeStruct((near * (columns + FEATURES), count), bf16),
        compiler_params=params(),
        cost_estimate=SMALL,
        name="stack_rows",
    )(*sources, a_side)


def own_kernel(near, mine_ref, theirs_ref, b_ref, out_ref):
    columns, count = out_ref.shape
    chunk = min(512, count)
    b = b_ref[0]
    acc = jnp.zeros((columns, count), f32)
    for ref in (mine_ref, theirs_ref):
        for source in range(near):
            side = near * columns + source * FEATURES
            for begin in range(0, count, chunk):
                lanes = slice(begin, begin + chunk)
                tile = lax.rsqrt(dot(ref[side : side + FEATURES, lanes], b, 0, 0))
                if ref is mine_ref and source == 0:
                    rows = begin + lax.broadcasted_iota(jnp.int32, tile.shape, 0)
                    cols = lax.broadcasted_iota(jnp.int32, tile.shape, 1)
                    tile = jnp.where(rows == cols, 0.0, tile)
                acc = acc + dot(ref[source * columns : (source + 1) * columns, lanes], tile.astype(bf16), 1, 0)
    out_ref[...] = acc


def own_image(mine, theirs, b_side, near):
    rows, count = mine.shape
    columns = rows // near - FEATURES
    return pl.pallas_call(
        functools.partial(own_kernel, near),
        in_specs=[VMEM] * 3,
        out_specs=VMEM,
        out_shape=jax.ShapeDtypeStruct((columns, count), f32),
        compiler_params=params(20),
        cost_estimate=SMALL,
        name="own_image",
    )(mine, theirs, b_side)


def combine_kernel(part, first_ref, own_ref, *refs):
    fars, (smooth_ref, low_ref) = refs[:-2], refs[-2:]
    width = smooth_ref.shape[1]
    place = first_ref[0] if part == 0 else 1 - first_ref[0]
    lanes = pl.ds(pl.multiple_of(place * width, width), width)
    smooth = own_ref[:, lanes]
    for far in fars:
        smooth = smooth + far[...].astype(f32)
    smooth_ref[...] = smooth
    low_ref[...] = smooth.astype(bf16)


def combine(part, first, own, fars):
    columns, count = own.shape
    return pl.pallas_call(
        functools.partial(combine_kernel, part),
        in_specs=[SMEM] + [VMEM] * (1 + len(fars)),
        out_specs=[VMEM] * 2,
        out_shape=[jax.ShapeDtypeStruct((columns, count // 2), kind) for kind in (f32, bf16)],
        compiler_params=params(),
        cost_estimate=SMALL,
        name="combine",
    )(first, own, *fars)


def full_image(first_ref, diag_ref, current_ref, smooth_refs, image_ref):
    half = smooth_refs[0].shape[1]
    for place, smooth in zip((first_ref[0], 1 - first_ref[0]), smooth_refs):
        lanes = pl.ds(pl.multiple_of(place * half, half), half)
        fixed = diag_ref[:, lanes].astype(bf16).astype(f32) * current_ref[:, lanes].astype(bf16).astype(f32)
        image_ref[:, lanes] = smooth[...] + fixed


def gram_kernel(ranks, first_ref, diag_ref, first_half, second_half, *refs):
    currents, (block, image) = refs[:ranks], refs[ranks:]
    columns = currents[0].shape[0]
    full_image(first_ref, diag_ref, currents[0], (first_half, second_half), image)
    for rank in range(ranks):
        current = currents[rank][...]
        block[rank, :columns] = close_dot(image[...], current, 1, 1)
        block[rank, columns : 2 * columns] = close_dot(currents[0][...], current, 1, 1)
    block[0, 2 * columns :] = close_dot(image[...], image[...], 1, 1)


def gram_sums(first, diag, smooths, currents):
    ranks = len(currents)
    columns, count = currents[0].shape
    return pl.pallas_call(
        functools.partial(gram_kernel, ranks),
        in_specs=[SMEM] + [VMEM] * (ranks + 3),
        out_specs=[VMEM] * 2,
        out_shape=(
            jax.ShapeDtypeStruct((ranks, 3 * columns, columns), f32),
            jax.ShapeDtypeStruct((columns, count), f32),
        ),
        compiler_params=params(),
        cost_estimate=SMALL,
        name="gram",
    )(first, diag, *smooths, *currents)


def cross_kernel(ranks, place_ref, core_ref, block_ref, image_ref, diag_ref, *refs):
    currents, gots = refs[: ranks - 1], refs[ranks - 1 : 2 * ranks - 2]
    keep_ref, give_ref, sums, block = refs[2 * ranks - 2 :]
    columns, count = image_ref.shape
    half = count // 2
    block[...] = block_ref[...]
    for rank in range(1, ranks):
        which = half_of(place_ref[0], place_ref[rank])
        lanes = pl.ds(pl.multiple_of(which * half, half), half)
        current = currents[rank - 1][:, lanes].astype(bf16).astype(f32)
        other = gots[rank - 1][...].astype(f32) + diag_ref[:, lanes].astype(bf16).astype(f32) * current
        block[rank, 2 * columns :] = close_dot(image_ref[:, lanes], other, 1, 1)
    for place in range(ranks):
        rank = jnp.bitwise_xor(place_ref[0], place)
        sums[:, place * columns : (place + 1) * columns] = block[rank]
    rows = keep_ref.shape[0]
    keep_ref[...] = sums[pl.ds(pl.multiple_of(core_ref[0] * rows, rows), rows), :]
    give_ref[...] = sums[pl.ds(pl.multiple_of((1 - core_ref[0]) * rows, rows), rows), :]


def cross_sums(places, core, blocks, image, diag, currents, gots):
    ranks = len(currents)
    columns, count = image.shape
    total = ranks * columns
    half = jax.ShapeDtypeStruct((3 * columns // 2, total), f32)
    return pl.pallas_call(
        functools.partial(cross_kernel, ranks),
        in_specs=[SMEM, SMEM] + [VMEM] * (2 * ranks + 1),
        out_specs=[VMEM] * 2,
        out_shape=(half, half),
        scratch_shapes=[
            pltpu.VMEM((3 * columns, total), f32),
            pltpu.VMEM((ranks, 3 * columns, columns), f32),
        ],
        compiler_params=params(),
        cost_estimate=SMALL,
        name="cross",
    )(places, core, blocks, image, diag, *currents[1:], *gots)


def shares_kernel(place_ref, keep_ref, got_ref, *shares):
    size = shares[0].shape[0]
    for at, share in enumerate(shares):
        rows = pl.ds(pl.multiple_of(place_ref[at] * size, size), size)
        share[...] = keep_ref[rows, :] + got_ref[rows, :]


def cut(places, keep, got):
    rows, lanes = keep.shape
    cuts = places.shape[0]
    return pl.pallas_call(
        shares_kernel,
        in_specs=[SMEM, VMEM, VMEM],
        out_specs=[VMEM] * cuts,
        out_shape=[jax.ShapeDtypeStruct((rows // cuts, lanes), f32)] * cuts,
        compiler_params=params(),
        name="shares",
    )(places, keep, got)


def reciprocal(value):
    guess = pl.reciprocal(value, approx=True)
    return guess * (2.0 - value * guess)


def eliminate(panel, begin, width):
    size, total = panel.shape
    parts = [panel[:, at : at + LANES] for at in range(0, total, LANES)]
    row_at = lax.broadcasted_iota(jnp.int32, (size, LANES), 0)
    col_at = lax.broadcasted_iota(jnp.int32, (1, LANES), 1)
    for group in range(0, size, width):
        own = parts[(begin + group) // LANES]
        first = (begin + group) % LANES
        cols = [jnp.broadcast_to(own[:, first + at : first + at + 1], (size, LANES)) for at in range(width)]
        for at in range(width):
            pivot = group + at
            value = cols[at][pivot : pivot + 1, :]
            inverse = reciprocal(value)
            col = jnp.where(row_at == pivot, cols[at] - 1.0, cols[at])
            for part in range(len(parts)):
                row = parts[part][pivot : pivot + 1, :]
                if part == (begin + pivot) // LANES:
                    row = jnp.where(col_at == (begin + pivot) % LANES, value + 1.0, row)
                parts[part] = parts[part] - col * (row * inverse)
            for later in range(at + 1, width):
                cols[later] = cols[later] - col * (cols[later][pivot : pivot + 1, :] * inverse)
    return jnp.concatenate(parts, axis=1)


def sweep(ref, begin, size):
    total = ref.shape[0]
    panel = ref[begin : begin + size, :]
    row = eliminate(panel, begin, 8)
    col_at = lax.broadcasted_iota(jnp.int32, panel.shape, 1)
    left = [part.astype(bf16) for part in pieces_of(jnp.where(col_at < begin, -panel, panel))]
    right = [part.astype(bf16) for part in pieces_of(row)]
    update = dot(
        jnp.concatenate([left[at] for at, _ in PAIRS], axis=0),
        jnp.concatenate([right[at] for _, at in PAIRS], axis=0),
        0,
        0,
    )
    lanes = lax.broadcasted_iota(jnp.int32, (total, total), 1)
    ref[...] = jnp.where((lanes >= begin) & (lanes < begin + size), 0.0, ref[...]) - update
    ref[begin : begin + size, :] = row


def solve_kernel(columns, size, place_ref, share_ref, *refs):
    shares = refs[:-7]
    step_ref, turn_ref, sums, grams, gram_inv, square_inv, step_all = refs[-7:]
    rows, total = shares[0].shape
    for at, share in enumerate(shares):
        sums[pl.ds(pl.multiple_of(share_ref[at] * rows, rows), rows), :] = share[...]
    for rank in range(total // columns):
        for which in range(3):
            begin = (rank * 3 + which) * columns
            grams[which, rank * columns : (rank + 1) * columns, :] = sums[begin : begin + columns, :]
    cross = grams[0]
    gram = 0.5 * (cross + cross.T)
    gram_scale = 1.0 / jnp.max(gram, keepdims=True)
    square_scale = 1.0 / jnp.max(grams[1], keepdims=True)
    gram_inv[...] = gram * gram_scale
    square_inv[...] = grams[1] * square_scale
    for begin in range(0, total, size):
        sweep(gram_inv, begin, size)
        sweep(square_inv, begin, size)
    mine = pl.ds(pl.multiple_of(place_ref[0] * columns, columns), columns)
    step_all[...] = close_dot(grams[1], gram_inv[...] * gram_scale, 1, 0)
    step = step_all[mine, :]
    step_ref[...] = step
    row_at = lax.broadcasted_iota(jnp.int32, (total, total), 0) // columns
    col_at = lax.broadcasted_iota(jnp.int32, (total, total), 1) // columns
    pairs = grams[2]
    images = pairs + jnp.where(row_at == col_at, 0.0, pairs.T)
    left = close_dot(step, images, 1, 0)
    across = close_dot(step, grams[0], 1, 0)
    grams[0] = grams[0].T
    left = left - grams[0, mine, :]
    following = grams[1, mine, :] - across + close_dot(left, step_all[...], 1, 1)
    turn_ref[...] = close_dot(following, square_inv[...] * square_scale, 1, 0)


def solve(places, share_places, shares, columns):
    total = shares[0].shape[1]
    square = pltpu.VMEM((total, total), f32)
    rows = jax.ShapeDtypeStruct((columns, total), f32)
    return pl.pallas_call(
        functools.partial(solve_kernel, columns, 32),
        in_specs=[SMEM, SMEM] + [VMEM] * len(shares),
        out_specs=[VMEM] * 2,
        out_shape=(rows, rows),
        scratch_shapes=[
            pltpu.VMEM((3 * total, total), f32),
            pltpu.VMEM((3, total, total), f32),
            square,
            square,
            square,
        ],
        compiler_params=params(),
        name="solve",
    )(places, share_places, *shares)


def others_kernel(ranks, place_ref, diag_ref, *refs):
    currents, gots, rests, outs = (refs[at * (ranks - 1) : (at + 1) * (ranks - 1)] for at in range(4))
    half = diag_ref.shape[1] // 2
    for at in range(ranks - 1):
        which = half_of(place_ref[0], place_ref[at + 1])
        for place, smooth in ((which, gots[at]), (1 - which, rests[at])):
            lanes = pl.ds(pl.multiple_of(place * half, half), half)
            fixed = diag_ref[:, lanes].astype(bf16).astype(f32) * currents[at][:, lanes].astype(bf16).astype(f32)
            outs[at][:, lanes] = smooth[...].astype(f32) + fixed


def other_images(places, diag, currents, gots, rests):
    ranks = len(currents)
    return pl.pallas_call(
        functools.partial(others_kernel, ranks),
        in_specs=[SMEM] + [VMEM] * (3 * ranks - 2),
        out_specs=[VMEM] * (ranks - 1),
        out_shape=[jax.ShapeDtypeStruct(currents[0].shape, f32)] * (ranks - 1),
        compiler_params=params(),
        cost_estimate=SMALL,
        name="other_images",
    )(places, diag, *currents[1:], *gots, *rests)


def finish_kernel(ranks, place_ref, step_ref, turn_ref, *refs):
    currents, images = refs[:ranks], refs[ranks : 2 * ranks]
    solution_ref, remainder_ref, direction_ref, current_all, image_all = refs[2 * ranks :]
    columns = currents[0].shape[0]
    for rank in range(ranks):
        at = pl.ds(pl.multiple_of(place_ref[rank] * columns, columns), columns)
        current_all[at, :] = currents[rank][...]
        image_all[at, :] = images[rank][...]
    current, step = current_all[...], step_ref[...]
    solution_ref[...] = close_dot(step, current, 1, 0)
    remainder = currents[0][...] - close_dot(step, image_all[...], 1, 0)
    remainder_ref[...] = remainder
    direction_ref[...] = remainder + close_dot(turn_ref[...], current, 1, 0)


def finish(places, step, turn, currents, images):
    ranks = len(currents)
    columns, count = currents[0].shape
    total = ranks * columns
    width = max(count // 4, LANES)
    out = jax.ShapeDtypeStruct((columns, count), f32)
    rows = pl.BlockSpec((columns, width), lambda at: (0, at))
    whole = pl.BlockSpec((columns, total), lambda at: (0, 0))
    return pl.pallas_call(
        functools.partial(finish_kernel, ranks),
        grid=(count // width,),
        in_specs=[SMEM, whole, whole] + [rows] * (2 * ranks),
        out_specs=[rows] * 3,
        out_shape=(out, out, out),
        scratch_shapes=[pltpu.VMEM((total, width), f32)] * 2,
        compiler_params=params(),
        cost_estimate=SMALL,
        name="finish",
    )(places, step, turn, *currents, *images)


def swap(value, axis, bits):
    size = lax.axis_size(axis)
    return lax.ppermute(value, axis, [(at, at ^ bits) for at in range(size)])


def pair_swap(value, bits, ranks):
    rank_bits, tri_bit = bits % ranks, bits // ranks
    if tri_bit == 0:
        return swap(value, "rhs", rank_bits)
    if rank_bits == 0:
        return swap(value, "tri", 1)
    count = lax.axis_size("tri")
    perm = [
        (tri * ranks + rank, (tri ^ 1) * ranks + (rank ^ rank_bits)) for tri in range(count) for rank in range(ranks)
    ]
    return lax.ppermute(value, ("tri", "rhs"), perm)


def indices(*values):
    return jnp.stack(values).astype(jnp.int32)


def all_sum(keep, give, beside, ranks, tris, tri, rank, core):
    low = tri & 1
    value, give = cut(indices(low, 1 - low), keep, swap(give, "split", 1))
    value = value + swap(give, "tri", 1)
    parts = [swap(value, "tri", 2 * far) for far in range(1, tris // 2)]
    parts, beside = lax.optimization_barrier((parts, beside))
    value = sum(parts, value)
    shares = [value] + [pair_swap(value, bits, ranks) for bits in range(1, 2 * ranks)]
    shares += [swap(share, "split", 1) for share in shares]
    places = [
        (rank ^ (bits % ranks)) * 4 + (core ^ other) * 2 + (low ^ (bits // ranks))
        for other in range(2)
        for bits in range(2 * ranks)
    ]
    return shares, indices(*places), beside


def body(residual, attach, vertices, corners, layers):
    columns, count = residual.shape
    tris, ranks, cores = lax.axis_size("tri"), lax.axis_size("rhs"), lax.axis_size("split")
    tri, rank, core = lax.axis_index("tri"), lax.axis_index("rhs"), lax.axis_index("split")
    near = min(4, tris)
    groups = tris // near
    scale = 1.0 / math.sqrt(corners.shape[1])

    my_ids = (tri * cores + core) * count + jnp.arange(count, dtype=jnp.int32)
    current = residual + inject * (attach[:, None] == my_ids[None, :]).astype(f32)
    packed = current.astype(bf16)
    currents = [current] + [swap(current, "rhs", bits) for bits in range(1, ranks)]
    sources = [packed] + [swap(packed, "tri", bits) for bits in range(1, near)]

    own_blocks = [(tri ^ (near * far)) * cores + core for far in range(groups)]
    near_blocks = [(tri ^ bits) * cores + core for bits in range(1, near)]
    vertices, packed = lax.optimization_barrier((vertices, packed))
    blocks = indices(*reversed(near_blocks), *own_blocks)
    a_side, b_side, diag = geometry(blocks, vertices, corners, layers, count, scale)
    diag = diag[near - 1]
    b_side = b_side[near - 1 :]
    slots = list(reversed(range(near)))
    sides = [a_side, b_side, swap(b_side, "split", 1)]
    half_place = half_of(rank ^ 1, rank) if ranks > 1 else jnp.int32(0)
    first = indices(half_place)

    def part(which, targets, starts=None, **more):
        return image_part(
            first, sources[which], [(0, slot) for slot in slots[which]], sides, targets, starts, **more
        )

    fars = range(1, groups)
    arrived = [[], []]
    last = slice(near - 1, near)
    far_sum = []
    if groups > 1:
        own_at, other_at = ([(side, far, None) for far in fars] for side in (1, 2))
        far_own = part(slice(0, 1), own_at)
        sides, far_own = lax.optimization_barrier((sides, far_own))
        far_other = part(slice(0, 1), other_at)
        for at in range(1, near - 1):
            both = part(slice(at, at + 1), other_at + own_at, [*far_other, *far_own])
            far_other, far_own = both[: len(other_at)], both[len(other_at) :]
        ready = []
        sides, currents = lax.optimization_barrier((sides, currents))
        for half in range(2):
            ready.append(part(last, [(*at[:2], half) for at in other_at], far_other, kind=bf16))
            sides, _ = lax.optimization_barrier((sides, ready))
        sent = [[swap(value, "split", 1) for value in values] for values in ready]
        for half in range(2):
            far_sum.append(
                part(last, [(*at[:2], half) for at in own_at], far_own, extras=sent[half], kind=bf16)
            )
            arrived[half] = [swap(value, "tri", near * far) for far, value in zip(fars, far_sum[half])]
            sides, _ = lax.optimization_barrier((sides, far_sum))
        sources, _ = lax.optimization_barrier((sources, sent))
    mine = stack_rows(sources, a_side, near)
    theirs = swap(mine, "split", 1)
    theirs, _ = lax.optimization_barrier((theirs, far_sum))
    own = own_image(mine, theirs, b_side, near)

    places = indices(*[rank ^ bits for bits in range(ranks)])
    smooth_first, low_first = combine(0, first, own, arrived[0])
    smooth_second, low_second = combine(1, first, own, arrived[1])
    gots, rests = [], []
    for bits in range(1, ranks):
        if bits == 1:
            give, rest = low_first, low_second
        else:
            is_first = half_of(rank ^ bits, rank) == half_place
            give = jnp.where(is_first, low_first, low_second)
            rest = jnp.where(is_first, low_second, low_first)
        gots.append(swap(give, "rhs", bits))
        rests.append(rest)
    blocks, image = gram_sums(first, diag, [smooth_first, smooth_second], currents)
    keep, give = cross_sums(places, indices(core), blocks, image, diag, currents, gots)
    rests, _ = lax.optimization_barrier((rests, gots))
    rests = [swap(rest, "rhs", bits) for bits, rest in enumerate(rests, 1)]
    beside = other_images(places, diag, currents, gots, rests)
    shares, share_places, beside = all_sum(keep, give, beside, ranks, tris, tri, rank, core)
    step, turn = solve(places, share_places, shares, columns)
    return finish(places, step, turn, currents, [image, *beside])


def solution(mesh):
    return jax.shard_map(
        body,
        mesh=mesh,
        in_specs=(P("rhs", ("tri", "split")), P("rhs"), P(), P(), P()),
        out_specs=(
            P("rhs", ("tri", "split")),
            P("rhs", ("tri", "split")),
            P("rhs", ("tri", "split")),
        ),
        check_vma=False,
    )
```

time: 102 us -> 87.2 us (0.85)
  waiting for transfers between devices: 30.7 us -> 21.7 us
  Pallas kernels: 44.1 us -> 41.7 us
  starting transfers between devices: 23.2 us -> 21 us
    ppermute x22 -> x23, waiting for transfers between devices: 25.2 us -> 19.4 us  [swap(): return lax.ppermute(value, axis, [(at, at ^ bits) for at in range(size)])]
    ppermute x2 -> x1, waiting for transfers between devices: 5.54 us -> 2.38 us  [pair_swap(): return lax.ppermute(value, ('tri', 'rhs'), perm)]
    pallas_call x10 -> x17, Pallas kernels: 37.1 us -> 34.8 us  [the longest x1 11.9 us: solve(): pl.pallas_call(functools.partial(solve_kernel, columns, 32), in_specs=[SM...]
    ppermute x2 -> x1, starting transfers between devices: 2.94 us -> 1.49 us  [pair_swap(): return lax.ppermute(value, ('tri', 'rhs'), perm)]
    ppermute x22 -> x23, starting transfers between devices: 20.2 us -> 19.5 us  [swap(): return lax.ppermute(value, axis, [(at, at ^ bits) for at in range(size)])]
  transfers between devices with their start and end apart: 24 -> 24, of which waited for: 12 -> 13; matrix products, arithmetic and copies ran while one was open for 1% -> 0% of each run, Pallas kernels for 39% -> 28%
where the time goes in v3:
time: 87.2 us; the launch traced here: 87 us
  Pallas kernels  41.7 us (48%)
  waiting for transfers between devices  21.7 us (25%)
  starting transfers between devices  21 us (24%)
  other arithmetic  1.43 us (2%)
  between operations  0.92 us (1%)
    ppermute x23, starting transfers between devices, swap(): return lax.ppermute(value, axis, [(at, at ^ bits) for at in range(size)])  19.5 us
    ppermute x23, waiting for transfers between devices, swap(): return lax.ppermute(value, axis, [(at, at ^ bits) for at in range(size)])  19.4 us
    pallas_call x1, Pallas kernels, solve(): pl.pallas_call(functools.partial(solve_kernel, columns, 32), in_specs=[SM...  11.9 us
    pallas_call x8, Pallas kernels, image_part(): pl.pallas_call(functools.partial(image_kernel, range(len(densities)), slo...  9.31 us
    pallas_call x1, Pallas kernels, own_image(): pl.pallas_call(functools.partial(own_kernel, near), in_specs=[VMEM] * 3,...  7.43 us
    pallas_call x1, Pallas kernels, geometry(): pl.pallas_call(functools.partial(geometry_kernel, scale), grid_spec=pltpu...  6.39 us
    pallas_call x1, Pallas kernels, finish(): pl.pallas_call(functools.partial(finish_kernel, ranks), grid=(count // wi...  3.21 us
    ppermute x1, waiting for transfers between devices, pair_swap(): return lax.ppermute(value, ('tri', 'rhs'), perm)  2.38 us
  transfers between devices with their start and end apart: 24, of which 13 were waited for; matrix products, arithmetic and copies ran while one was open for 0% of the time, Pallas kernels for 28%

profile of v3, /device:TPU:0, one launch (start us, length us, event | category | flops | bytes accessed | tf_op | source)
XLA Modules:
  0.0 87.0 jit_solution(17202394352676311086)
XLA Ops:
  0.7 1.2 %fusion = (bf16[128,1024]{1,0:T(8,128)(2,1)S(1)}, f32[128,1024]{1,0:T(8,128)S(1)}) fusion(f32[128,1024]{1,0:T(8,128)} %param.5, s32[1024]{0:T(1024)S(1)} %iota_add_fusion, s32[128]{0:T(128)} %param.6), kind=kLoop, calls=%fused_computation.6 | loop fusion | flops 524288 | bytes 1315328 | tf_op jit(solution)/shard_map/convert_element_type | solution.py:584
  1.9 3.0 %collective-permute-start.4 = (f32[128,1024]{1,0:T(8,128)S(1)}, f32[128,1024]{1,0:T(8,128)S(1)}, u32[]{:S(2)}, u32[]{:S(2)}) collective-permute-start(f32[128,1024]{1,0:T(8,128)S(1)} %get-tuple-element.78.refs_0_), channel_id=1, source_target_pairs={{0,2},{2,0},{1,3},{3,1},{4,6},{6,4},{5,7},{7,5},{8,10},{10,8},{9,1... | collective-permute-start | bytes 1572872 | tf_op jit(solution)/shard_map/ppermute | solution.py:537
  5.0 1.5 %collective-permute-start = (bf16[128,1024]{1,0:T(8,128)(2,1)S(1)}, bf16[128,1024]{1,0:T(8,128)(2,1)S(1)}, u32[]{:S(2)}, u32[]{:S(2)}) collective-permute-start(bf16[128,1024]{1,0:T(8,128)(2,1)S(1)} %get-tuple-element.66.refs_0_), channel_id=1, source_target_pairs={{0,4},{4,0},{8,12},{12,8},{16,20},{20,16},{24,28},{28,24},{1,5},{5... | collective-permute-start | bytes 786440 | tf_op jit(solution)/shard_map/ppermute | solution.py:537
  6.4 1.6 %collective-permute-start.1 = (bf16[128,1024]{1,0:T(8,128)(2,1)S(1)}, bf16[128,1024]{1,0:T(8,128)(2,1)S(1)}, u32[]{:S(2)}, u32[]{:S(2)}) collective-permute-start(bf16[128,1024]{1,0:T(8,128)(2,1)S(1)} %get-tuple-element.66.refs_0_), channel_id=1, source_target_pairs={{0,8},{4,12},{8,0},{12,4},{16,24},{20,28},{24,16},{28,20},{1,9},{5... | collective-permute-start | bytes 786440 | tf_op jit(solution)/shard_map/ppermute | solution.py:537
  8.0 0.4 collective-permute-start.2
  8.5 6.4 %geometry.1 = (bf16[5,32,1024]{2,1,0:T(8,128)(2,1)S(1)}, bf16[5,32,1024]{2,1,0:T(8,128)(2,1)S(1)}, f32[5,1,1024]{2,1,0:T(1,128)S(1)}) custom-call(s32[5]{0:T(128)S(1)} %stack.94.blocks_ref, f32[3,8192]{1,0:T(4,128)S(1)} %copy-done.1, s32[3,16384]{1,0:T(4,128)S(1)} %copy-done, s32[1,16384]{1,0:T(1,128)S(1)} %bitcast.22), custom_call_target="tpu_custom_call" | custom-call | tf_op jit(solution)/shard_map/geometry/pallas_call | solution.py:117
  15.0 1.0 %image_part.8.refs_5_ = f32[128,1024]{1,0:T(8,128)S(1)} custom-call(s32[1]{0:T(128)} %bitcast.13.first_ref, bf16[128,1024]{1,0:T(8,128)(2,1)S(1)} %get-tuple-element.66.refs_0_, bf16[5,32,1024]{2,1,0:T(8,128)(2,1)S(1)} %get-tuple-element.73.refs_1_.refs_4_, bf16[2,32,1024]{2,1,0:T(8,128)(2,1)S(1)} %slice.7.refs_2_.b_ref), custom_call_target="tpu_custom_call" | custom-call | flops 1024 | bytes 1024 | tf_op jit(solution)/shard_map/image_part/pallas_call | solution.py:181
  16.1 0.3 collective-permute-done.3.refs_3_
  16.4 1.0 %image_part.9.refs_4_ = f32[128,1024]{1,0:T(8,128)S(1)} custom-call(s32[1]{0:T(128)} %bitcast.13.first_ref, bf16[128,1024]{1,0:T(8,128)(2,1)S(1)} %get-tuple-element.66.refs_0_, bf16[5,32,1024]{2,1,0:T(8,128)(2,1)S(1)} %get-tuple-element.73.refs_1_.refs_4_, bf16[2,32,1024]{2,1,0:T(8,128)(2,1)S(1)} %slice.7.refs_2_.b_ref, ...), custom_call_target="tpu_custom_call" | custom-call | flops 1024 | bytes 1024 | tf_op jit(solution)/shard_map/image_part/pallas_call | solution.py:181
  17.4 2.0 %image_part.10 = (f32[128,1024]{1,0:T(8,128)S(1)}, f32[128,1024]{1,0:T(8,128)S(1)}) custom-call(s32[1]{0:T(128)} %bitcast.13.first_ref, bf16[128,1024]{1,0:T(8,128)(2,1)S(1)} %collective-permute-done.refs_0_.refs_1_, bf16[5,32,1024]{2,1,0:T(8,128)(2,1)S(1)} %get-tuple-element.73.refs_1_.refs_4_, bf16[2,32,1024]{2,1,0:T(8,128)(2,1)S(1)} %slice.7.refs_2_.b_ref, ...), custom_call_target="tpu_custom_call" | custom-call | flops 1024 | bytes 1024 | tf_op jit(solution)/shard_map/image_part/pallas_call | solution.py:181
  19.4 2.0 %image_part.11 = (f32[128,1024]{1,0:T(8,128)S(1)}, f32[128,1024]{1,0:T(8,128)S(1)}) custom-call(s32[1]{0:T(128)} %bitcast.13.first_ref, bf16[128,1024]{1,0:T(8,128)(2,1)S(1)} %collective-permute-done.1.refs_0_.refs_2_, bf16[5,32,1024]{2,1,0:T(8,128)(2,1)S(1)} %get-tuple-element.73.refs_1_.refs_4_, bf16[2,32,1024]{2,1,0:T(8,128)(2,1)S(1)} %slice.7.refs_2_.b_ref, ...), custom_call_target="tpu_custom_call" | custom-call | flops 1024 | bytes 1024 | tf_op jit(solution)/shard_map/image_part/pallas_call | solution.py:181
  21.4 0.8 image_part.12
  22.2 0.3 collective-permute-start.5
  22.5 0.8 image_part.13
  23.3 0.4 collective-permute-start.6
  23.7 1.0 %collective-permute-done.6.refs_4_ = bf16[128,512]{1,0:T(8,128)(2,1)S(1)} collective-permute-done((bf16[128,512]{1,0:T(8,128)(2,1)S(1)}, bf16[128,512]{1,0:T(8,128)(2,1)S(1)}, u32[]{:S(2)}, u32[]{:S(2)}) %collective-permute-start.6) | collective-permute-done | bytes 131104 | tf_op jit(solution)/shard_map/ppermute | solution.py:537
  24.8 0.4 collective-permute-start.7
  25.2 0.8 image_part.14
  26.0 2.7 %collective-permute-start.8 = (bf16[128,512]{1,0:T(8,128)(2,1)S(1)}, bf16[128,512]{1,0:T(8,128)(2,1)S(1)}, u32[]{:S(2)}, u32[]{:S(2)}) collective-permute-start(bf16[128,512]{1,0:T(8,128)(2,1)S(1)} %image_part.14), channel_id=1, source_target_pairs={{0,16},{4,20},{8,24},{12,28},{16,0},{20,4},{24,8},{28,12},{1,17},{... | collective-permute-start | bytes 393224 | tf_op jit(solution)/shard_map/ppermute | solution.py:537
  28.7 0.8 image_part.15
  29.5 0.4 collective-permute-start.9
  29.9 7.4 %own_image.1.own_ref = f32[128,1024]{1,0:T(8,128)S(1)} custom-call(bf16[640,1024]{1,0:T(8,128)(2,1)S(1)} %stack_rows.1.mine_ref, bf16[640,1024]{1,0:T(8,128)(2,1)S(1)} %collective-permute-done.7.theirs_ref, bf16[2,32,1024]{2,1,0:T(8,128)(2,1)S(1)} %slice.7.refs_2_.b_ref), custom_call_target="tpu_custom_call" | custom-call | flops 1024 | bytes 1024 | tf_op jit(solution)/shard_map/own_image/pallas_call | solution.py:240
  37.4 1.6 %collective-permute-done.8.refs_0_ = bf16[128,512]{1,0:T(8,128)(2,1)S(1)} collective-permute-done((bf16[128,512]{1,0:T(8,128)(2,1)S(1)}, bf16[128,512]{1,0:T(8,128)(2,1)S(1)}, u32[]{:S(2)}, u32[]{:S(2)}) %collective-permute-start.8) | collective-permute-done | bytes 131104 | tf_op jit(solution)/shard_map/ppermute | solution.py:537
  39.0 0.2 collective-permute-start.10
  39.3 1.7 %collective-permute-done.9.refs_0_ = bf16[128,512]{1,0:T(8,128)(2,1)S(1)} collective-permute-done((bf16[128,512]{1,0:T(8,128)(2,1)S(1)}, bf16[128,512]{1,0:T(8,128)(2,1)S(1)}, u32[]{:S(2)}, u32[]{:S(2)}) %collective-permute-start.9) | collective-permute-done | bytes 131104 | tf_op jit(solution)/shard_map/ppermute | solution.py:537
  41.1 1.3 %gram.1 = (f32[2,384,128]{2,1,0:T(8,128)S(1)}, f32[128,1024]{1,0:T(8,128)S(1)}) custom-call(s32[1]{0:T(128)} %bitcast.13.first_ref, f32[1,1024]{1,0:T(1,128)S(1)} %slice_bitcast_fusion.diag_ref, f32[128,512]{1,0:T(8,128)S(1)} %get-tuple-element.76.first_half, f32[128,512]{1,0:T(8,128)S(1)} %get-tuple-element.77.second_half, ...), custom_call_target="tpu_custom_call" | custom-call | flops 1024 | bytes 1024 | tf_op jit(solution)/shard_map/gram/pallas_call | solution.py:298
  42.4 1.7 %collective-permute-done.10.refs_1_ = bf16[128,512]{1,0:T(8,128)(2,1)S(1)} collective-permute-done((bf16[128,512]{1,0:T(8,128)(2,1)S(1)}, bf16[128,512]{1,0:T(8,128)(2,1)S(1)}, u32[]{:S(2)}, u32[]{:S(2)}) %collective-permute-start.10) | collective-permute-done | bytes 131104 | tf_op jit(solution)/shard_map/ppermute | solution.py:537
  44.0 0.9 %cross.1 = (f32[192,256]{1,0:T(8,128)S(1)}, f32[192,256]{1,0:T(8,128)S(1)}) custom-call(s32[2]{0:T(128)S(1)} %pad_add_fusion.place_ref, s32[1]{0:T(128)} %bitcast.12.core_ref, f32[2,384,128]{2,1,0:T(8,128)S(1)} %get-tuple-element.80.block_ref, f32[128,1024]{1,0:T(8,128)S(1)} %get-tuple-element.81.image_ref.refs_2_, ...), custom_call_target="tpu_custom_call" | custom-call | flops 1024 | bytes 1024 | tf_op jit(solution)/shard_map/cross/pallas_call | solution.py:337
  45.1 1.3 %collective-permute-done.11.got_ref = f32[192,256]{1,0:T(8,128)S(1)} collective-permute-done((f32[192,256]{1,0:T(8,128)S(1)}, f32[192,256]{1,0:T(8,128)S(1)}, u32[]{:S(2)}, u32[]{:S(2)}) %collective-permute-start.11) | collective-permute-done | bytes 196640 | tf_op jit(solution)/shard_map/ppermute | solution.py:537
  46.5 0.6 shares.1
  47.0 1.6 %collective-permute-start.12 = (f32[96,256]{1,0:T(8,128)S(1)}, f32[96,256]{1,0:T(8,128)S(1)}, u32[]{:S(2)}, u32[]{:S(2)}) collective-permute-start(f32[96,256]{1,0:T(8,128)S(1)} %get-tuple-element.86), channel_id=1, source_target_pairs={{0,4},{4,0},{8,12},{12,8},{16,20},{20,16},{24,28},{28,24},{1,5},{5... | collective-permute-start | bytes 294920 | tf_op jit(solution)/shard_map/ppermute | solution.py:537
  48.6 0.5 collective-permute-start.16
  49.1 2.8 %collective-permute-done.12 = f32[96,256]{1,0:T(8,128)S(1)} collective-permute-done((f32[96,256]{1,0:T(8,128)S(1)}, f32[96,256]{1,0:T(8,128)S(1)}, u32[]{:S(2)}, u32[]{:S(2)}) %collective-permute-start.12) | collective-permute-done | bytes 98336 | tf_op jit(solution)/shard_map/ppermute | solution.py:537
  51.9 0.5 collective-permute-start.13
  52.4 3.4 %collective-permute-start.14 = (f32[96,256]{1,0:T(8,128)S(1)}, f32[96,256]{1,0:T(8,128)S(1)}, u32[]{:S(2)}, u32[]{:S(2)}) collective-permute-start(f32[96,256]{1,0:T(8,128)S(1)} %add.101), channel_id=1, source_target_pairs={{0,16},{4,20},{8,24},{12,28},{16,0},{20,4},{24,8},{28,12},{1,17},{... | collective-permute-start | bytes 294920 | tf_op jit(solution)/shard_map/ppermute | solution.py:537
  55.8 0.6 collective-permute-start.15
  56.4 0.6 other_images.1.refs_3_
  57.0 0.7 collective-permute-done.13
  57.8 5.3 %collective-permute-done.14 = f32[96,256]{1,0:T(8,128)S(1)} collective-permute-done((f32[96,256]{1,0:T(8,128)S(1)}, f32[96,256]{1,0:T(8,128)S(1)}, u32[]{:S(2)}, u32[]{:S(2)}) %collective-permute-start.14) | collective-permute-done | bytes 98336 | tf_op jit(solution)/shard_map/ppermute | solution.py:537
  63.1 0.6 collective-permute-start.17
  63.7 1.5 %collective-permute-start.18 = (f32[96,256]{1,0:T(8,128)S(1)}, f32[96,256]{1,0:T(8,128)S(1)}, u32[]{:S(2)}, u32[]{:S(2)}) collective-permute-start(f32[96,256]{1,0:T(8,128)S(1)} %add_add_fusion.refs_0_), channel_id=1, source_target_pairs={{0,4},{4,0},{8,12},{12,8},{16,20},{20,16},{24,28},{28,24},{1,5},{5... | collective-permute-start | bytes 294920 | tf_op jit(solution)/shard_map/ppermute | solution.py:537
  65.2 1.5 %collective-permute-start.19 = (f32[96,256]{1,0:T(8,128)S(1)}, f32[96,256]{1,0:T(8,128)S(1)}, u32[]{:S(2)}, u32[]{:S(2)}) collective-permute-start(f32[96,256]{1,0:T(8,128)S(1)} %add_add_fusion.refs_0_), channel_id=1, source_target_pairs={{0,6},{2,4},{4,2},{6,0},{8,14},{10,12},{12,10},{14,8},{16,22},{18,... | collective-permute-start | bytes 294920 | tf_op jit(solution)/shard_map/ppermute | solution.py:550
  66.6 1.1 %collective-permute-done.17.refs_1_ = f32[96,256]{1,0:T(8,128)S(1)} collective-permute-done((f32[96,256]{1,0:T(8,128)S(1)}, f32[96,256]{1,0:T(8,128)S(1)}, u32[]{:S(2)}, u32[]{:S(2)}) %collective-permute-start.17) | collective-permute-done | bytes 98336 | tf_op jit(solution)/shard_map/ppermute | solution.py:537
  67.8 0.5 collective-permute-done.18.refs_2_
  68.3 2.4 %collective-permute-done.19.refs_3_ = f32[96,256]{1,0:T(8,128)S(1)} collective-permute-done((f32[96,256]{1,0:T(8,128)S(1)}, f32[96,256]{1,0:T(8,128)S(1)}, u32[]{:S(2)}, u32[]{:S(2)}) %collective-permute-start.19) | collective-permute-done | bytes 98336 | tf_op jit(solution)/shard_map/ppermute | solution.py:550
  70.8 1.2 %collective-permute-done.23.refs_7_ = f32[96,256]{1,0:T(8,128)S(1)} collective-permute-done((f32[96,256]{1,0:T(8,128)S(1)}, f32[96,256]{1,0:T(8,128)S(1)}, u32[]{:S(2)}, u32[]{:S(2)}) %collective-permute-start.23) | collective-permute-done | bytes 98336 | tf_op jit(solution)/shard_map/ppermute | solution.py:537
  72.0 11.9 %solve.1 = (f32[128,256]{1,0:T(8,128)S(1)}, f32[128,256]{1,0:T(8,128)S(1)}) custom-call(s32[2]{0:T(128)S(1)} %pad_add_fusion.place_ref, s32[8]{0:T(128)S(1)} %stack.82.share_ref, f32[96,256]{1,0:T(8,128)S(1)} %add_add_fusion.refs_0_, f32[96,256]{1,0:T(8,128)S(1)} %collective-permute-done.17.refs_1_, f32[96,256]{1,0:T(8,128)S(1)} %collective-permute-done.18.refs_2_, ...), custom_call_target="tpu_custom_call" | custom-call | tf_op jit(solution)/shard_map/solve/pallas_call | solution.py:458
  83.8 3.2 %finish.1 = (f32[128,1024]{1,0:T(8,128)}, f32[128,1024]{1,0:T(8,128)}, f32[128,1024]{1,0:T(8,128)}) custom-call(s32[2]{0:T(128)S(1)} %pad_add_fusion.place_ref, f32[128,256]{1,0:T(8,128)S(1)} %get-tuple-element.92.step_ref, f32[128,256]{1,0:T(8,128)S(1)} %get-tuple-element.93.turn_ref, f32[128,1024]{1,0:T(8,128)S(1)} %get-tuple-element.78.refs_0_, ...), custom_call_target="tpu_custom_call" | custom-call | flops 1024 | bytes 1024 | tf_op jit(solution)/shard_map/finish/pallas_call | solution.py:522
  (35 shorter events, 0.7 us)
Async XLA Ops:
  0.6 7.9 %copy-start.1 = (f32[3,8192]{1,0:T(4,128)S(1)}, f32[3,8192]{1,0:T(4,128)}, u32[]{:S(2)}) copy-start(f32[3,8192]{1,0:T(4,128)} %vertices_ref) | copy-start | bytes 294916
  0.6 7.9 %copy-start.2 = (s32[16384]{0:T(1024)S(1)}, s32[16384]{0:T(1024)}, u32[]{:S(2)}) copy-start(s32[16384]{0:T(1024)} %param.9) | copy-start | bytes 196612
  0.7 7.9 %copy-start = (s32[3,16384]{1,0:T(4,128)S(1)}, s32[3,16384]{1,0:T(4,128)}, u32[]{:S(2)}) copy-start(s32[3,16384]{1,0:T(4,128)} %corners_ref.1) | copy-start | bytes 589828
  1.9 19.4 %collective-permute-start.4 = (f32[128,1024]{1,0:T(8,128)S(1)}, f32[128,1024]{1,0:T(8,128)S(1)}, u32[]{:S(2)}, u32[]{:S(2)}) collective-permute-start(f32[128,1024]{1,0:T(8,128)S(1)} %get-tuple-element.78.refs_0_), channel_id=1, source_target_pairs={{0,2},{2,0},{1,3},{3,1},{4,6},{6,4},{5,7},{7,5},{8,10},{10,8},{9,1... | collective-permute-start | bytes 1572872 | tf_op jit(solution)/shard_map/ppermute | solution.py:537
  5.0 12.5 %collective-permute-start = (bf16[128,1024]{1,0:T(8,128)(2,1)S(1)}, bf16[128,1024]{1,0:T(8,128)(2,1)S(1)}, u32[]{:S(2)}, u32[]{:S(2)}) collective-permute-start(bf16[128,1024]{1,0:T(8,128)(2,1)S(1)} %get-tuple-element.66.refs_0_), channel_id=1, source_target_pairs={{0,4},{4,0},{8,12},{12,8},{16,20},{20,16},{24,28},{28,24},{1,5},{5... | collective-permute-start | bytes 786440 | tf_op jit(solution)/shard_map/ppermute | solution.py:537
  6.4 12.9 %collective-permute-start.1 = (bf16[128,1024]{1,0:T(8,128)(2,1)S(1)}, bf16[128,1024]{1,0:T(8,128)(2,1)S(1)}, u32[]{:S(2)}, u32[]{:S(2)}) collective-permute-start(bf16[128,1024]{1,0:T(8,128)(2,1)S(1)} %get-tuple-element.66.refs_0_), channel_id=1, source_target_pairs={{0,8},{4,12},{8,0},{12,4},{16,24},{20,28},{24,16},{28,20},{1,9},{5... | collective-permute-start | bytes 786440 | tf_op jit(solution)/shard_map/ppermute | solution.py:537
  8.0 13.3 %collective-permute-start.2 = (bf16[128,1024]{1,0:T(8,128)(2,1)S(1)}, bf16[128,1024]{1,0:T(8,128)(2,1)S(1)}, u32[]{:S(2)}, u32[]{:S(2)}) collective-permute-start(bf16[128,1024]{1,0:T(8,128)(2,1)S(1)} %get-tuple-element.66.refs_0_), channel_id=1, source_target_pairs={{0,12},{4,8},{8,4},{12,0},{16,28},{20,24},{24,20},{28,16},{1,13},{... | collective-permute-start | bytes 786440 | tf_op jit(solution)/shard_map/ppermute | solution.py:537
  15.0 1.4 %collective-permute-start.3 = (bf16[2,32,1024]{2,1,0:T(8,128)(2,1)S(1)}, bf16[2,32,1024]{2,1,0:T(8,128)(2,1)S(1)}, u32[]{:S(2)}, u32[]{:S(2)}) collective-permute-start(bf16[2,32,1024]{2,1,0:T(8,128)(2,1)S(1)} %slice.7.refs_2_.b_ref), channel_id=1, source_target_pairs={{0,1},{1,0},{2,3},{3,2},{4,5},{5,4},{6,7},{7,6},{8,9},{9,8},{10,11... | collective-permute-start | bytes 393224 | tf_op jit(solution)/shard_map/ppermute | solution.py:537
  22.2 1.5 %collective-permute-start.5 = (bf16[128,512]{1,0:T(8,128)(2,1)S(1)}, bf16[128,512]{1,0:T(8,128)(2,1)S(1)}, u32[]{:S(2)}, u32[]{:S(2)}) collective-permute-start(bf16[128,512]{1,0:T(8,128)(2,1)S(1)} %image_part.12), channel_id=1, source_target_pairs={{0,1},{1,0},{2,3},{3,2},{4,5},{5,4},{6,7},{7,6},{8,9},{9,8},{10,11... | collective-permute-start | bytes 393224 | tf_op jit(solution)/shard_map/ppermute | solution.py:537
  23.3 1.4 %collective-permute-start.6 = (bf16[128,512]{1,0:T(8,128)(2,1)S(1)}, bf16[128,512]{1,0:T(8,128)(2,1)S(1)}, u32[]{:S(2)}, u32[]{:S(2)}) collective-permute-start(bf16[128,512]{1,0:T(8,128)(2,1)S(1)} %image_part.13), channel_id=1, source_target_pairs={{0,1},{1,0},{2,3},{3,2},{4,5},{5,4},{6,7},{7,6},{8,9},{9,8},{10,11... | collective-permute-start | bytes 393224 | tf_op jit(solution)/shard_map/ppermute | solution.py:537
  24.8 5.1 %collective-permute-start.7 = (bf16[640,1024]{1,0:T(8,128)(2,1)S(1)}, bf16[640,1024]{1,0:T(8,128)(2,1)S(1)}, u32[]{:S(2)}, u32[]{:S(2)}) collective-permute-start(bf16[640,1024]{1,0:T(8,128)(2,1)S(1)} %stack_rows.1.mine_ref), channel_id=1, source_target_pairs={{0,1},{1,0},{2,3},{3,2},{4,5},{5,4},{6,7},{7,6},{8,9},{9,8},{10,11... | collective-permute-start | bytes 3932168 | tf_op jit(solution)/shard_map/ppermute | solution.py:537
  26.0 12.9 %collective-permute-start.8 = (bf16[128,512]{1,0:T(8,128)(2,1)S(1)}, bf16[128,512]{1,0:T(8,128)(2,1)S(1)}, u32[]{:S(2)}, u32[]{:S(2)}) collective-permute-start(bf16[128,512]{1,0:T(8,128)(2,1)S(1)} %image_part.14), channel_id=1, source_target_pairs={{0,16},{4,20},{8,24},{12,28},{16,0},{20,4},{24,8},{28,12},{1,17},{... | collective-permute-start | bytes 393224 | tf_op jit(solution)/shard_map/ppermute | solution.py:537
  29.5 11.5 %collective-permute-start.9 = (bf16[128,512]{1,0:T(8,128)(2,1)S(1)}, bf16[128,512]{1,0:T(8,128)(2,1)S(1)}, u32[]{:S(2)}, u32[]{:S(2)}) collective-permute-start(bf16[128,512]{1,0:T(8,128)(2,1)S(1)} %image_part.15), channel_id=1, source_target_pairs={{0,16},{4,20},{8,24},{12,28},{16,0},{20,4},{24,8},{28,12},{1,17},{... | collective-permute-start | bytes 393224 | tf_op jit(solution)/shard_map/ppermute | solution.py:537
  39.0 5.0 %collective-permute-start.10 = (bf16[128,512]{1,0:T(8,128)(2,1)S(1)}, bf16[128,512]{1,0:T(8,128)(2,1)S(1)}, u32[]{:S(2)}, u32[]{:S(2)}) collective-permute-start(bf16[128,512]{1,0:T(8,128)(2,1)S(1)} %get-tuple-element.82), channel_id=1, source_target_pairs={{0,2},{2,0},{1,3},{3,1},{4,6},{6,4},{5,7},{7,5},{8,10},{10,8},{9,1... | collective-permute-start | bytes 393224 | tf_op jit(solution)/shard_map/ppermute | solution.py:537
  44.9 1.5 %collective-permute-start.11 = (f32[192,256]{1,0:T(8,128)S(1)}, f32[192,256]{1,0:T(8,128)S(1)}, u32[]{:S(2)}, u32[]{:S(2)}) collective-permute-start(f32[192,256]{1,0:T(8,128)S(1)} %get-tuple-element.84), channel_id=1, source_target_pairs={{0,1},{1,0},{2,3},{3,2},{4,5},{5,4},{6,7},{7,6},{8,9},{9,8},{10,11... | collective-permute-start | bytes 589832 | tf_op jit(solution)/shard_map/ppermute | solution.py:537
  47.0 4.9 %collective-permute-start.12 = (f32[96,256]{1,0:T(8,128)S(1)}, f32[96,256]{1,0:T(8,128)S(1)}, u32[]{:S(2)}, u32[]{:S(2)}) collective-permute-start(f32[96,256]{1,0:T(8,128)S(1)} %get-tuple-element.86), channel_id=1, source_target_pairs={{0,4},{4,0},{8,12},{12,8},{16,20},{20,16},{24,28},{28,24},{1,5},{5... | collective-permute-start | bytes 294920 | tf_op jit(solution)/shard_map/ppermute | solution.py:537
  48.6 7.8 %collective-permute-start.16 = (bf16[128,512]{1,0:T(8,128)(2,1)S(1)}, bf16[128,512]{1,0:T(8,128)(2,1)S(1)}, u32[]{:S(2)}, u32[]{:S(2)}) collective-permute-start(bf16[128,512]{1,0:T(8,128)(2,1)S(1)} %get-tuple-element.88), channel_id=1, source_target_pairs={{0,2},{2,0},{1,3},{3,1},{4,6},{6,4},{5,7},{7,5},{8,10},{10,8},{9,1... | collective-permute-start | bytes 393224 | tf_op jit(solution)/shard_map/ppermute | solution.py:537
  51.9 5.8 %collective-permute-start.13 = (f32[96,256]{1,0:T(8,128)S(1)}, f32[96,256]{1,0:T(8,128)S(1)}, u32[]{:S(2)}, u32[]{:S(2)}) collective-permute-start(f32[96,256]{1,0:T(8,128)S(1)} %add.101), channel_id=1, source_target_pairs={{0,8},{4,12},{8,0},{12,4},{16,24},{20,28},{24,16},{28,20},{1,9},{5... | collective-permute-start | bytes 294920 | tf_op jit(solution)/shard_map/ppermute | solution.py:537
  52.4 10.6 %collective-permute-start.14 = (f32[96,256]{1,0:T(8,128)S(1)}, f32[96,256]{1,0:T(8,128)S(1)}, u32[]{:S(2)}, u32[]{:S(2)}) collective-permute-start(f32[96,256]{1,0:T(8,128)S(1)} %add.101), channel_id=1, source_target_pairs={{0,16},{4,20},{8,24},{12,28},{16,0},{20,4},{24,8},{28,12},{1,17},{... | collective-permute-start | bytes 294920 | tf_op jit(solution)/shard_map/ppermute | solution.py:537
  55.8 7.3 %collective-permute-start.15 = (f32[96,256]{1,0:T(8,128)S(1)}, f32[96,256]{1,0:T(8,128)S(1)}, u32[]{:S(2)}, u32[]{:S(2)}) collective-permute-start(f32[96,256]{1,0:T(8,128)S(1)} %add.101), channel_id=1, source_target_pairs={{0,24},{4,28},{8,16},{12,20},{16,8},{20,12},{24,0},{28,4},{1,25},{... | collective-permute-start | bytes 294920 | tf_op jit(solution)/shard_map/ppermute | solution.py:537
  63.1 4.7 %collective-permute-start.17 = (f32[96,256]{1,0:T(8,128)S(1)}, f32[96,256]{1,0:T(8,128)S(1)}, u32[]{:S(2)}, u32[]{:S(2)}) collective-permute-start(f32[96,256]{1,0:T(8,128)S(1)} %add_add_fusion.refs_0_), channel_id=1, source_target_pairs={{0,2},{2,0},{1,3},{3,1},{4,6},{6,4},{5,7},{7,5},{8,10},{10,8},{9,1... | collective-permute-start | bytes 294920 | tf_op jit(solution)/shard_map/ppermute | solution.py:537
  63.7 4.6 %collective-permute-start.18 = (f32[96,256]{1,0:T(8,128)S(1)}, f32[96,256]{1,0:T(8,128)S(1)}, u32[]{:S(2)}, u32[]{:S(2)}) collective-permute-start(f32[96,256]{1,0:T(8,128)S(1)} %add_add_fusion.refs_0_), channel_id=1, source_target_pairs={{0,4},{4,0},{8,12},{12,8},{16,20},{20,16},{24,28},{28,24},{1,5},{5... | collective-permute-start | bytes 294920 | tf_op jit(solution)/shard_map/ppermute | solution.py:537
  65.2 5.5 %collective-permute-start.19 = (f32[96,256]{1,0:T(8,128)S(1)}, f32[96,256]{1,0:T(8,128)S(1)}, u32[]{:S(2)}, u32[]{:S(2)}) collective-permute-start(f32[96,256]{1,0:T(8,128)S(1)} %add_add_fusion.refs_0_), channel_id=1, source_target_pairs={{0,6},{2,4},{4,2},{6,0},{8,14},{10,12},{12,10},{14,8},{16,22},{18,... | collective-permute-start | bytes 294920 | tf_op jit(solution)/shard_map/ppermute | solution.py:550
  66.6 4.1 %collective-permute-start.20 = (f32[96,256]{1,0:T(8,128)S(1)}, f32[96,256]{1,0:T(8,128)S(1)}, u32[]{:S(2)}, u32[]{:S(2)}) collective-permute-start(f32[96,256]{1,0:T(8,128)S(1)} %add_add_fusion.refs_0_), channel_id=1, source_target_pairs={{0,1},{1,0},{2,3},{3,2},{4,5},{5,4},{6,7},{7,6},{8,9},{9,8},{10,11... | collective-permute-start | bytes 294920 | tf_op jit(solution)/shard_map/ppermute | solution.py:537
  67.8 3.0 %collective-permute-start.21 = (f32[96,256]{1,0:T(8,128)S(1)}, f32[96,256]{1,0:T(8,128)S(1)}, u32[]{:S(2)}, u32[]{:S(2)}) collective-permute-start(f32[96,256]{1,0:T(8,128)S(1)} %collective-permute-done.17.refs_1_), channel_id=1, source_target_pairs={{0,1},{1,0},{2,3},{3,2},{4,5},{5,4},{6,7},{7,6},{8,9},{9,8},{10,11... | collective-permute-start | bytes 294920 | tf_op jit(solution)/shard_map/ppermute | solution.py:537
  68.3 2.5 %collective-permute-start.22 = (f32[96,256]{1,0:T(8,128)S(1)}, f32[96,256]{1,0:T(8,128)S(1)}, u32[]{:S(2)}, u32[]{:S(2)}) collective-permute-start(f32[96,256]{1,0:T(8,128)S(1)} %collective-permute-done.18.refs_2_), channel_id=1, source_target_pairs={{0,1},{1,0},{2,3},{3,2},{4,5},{5,4},{6,7},{7,6},{8,9},{9,8},{10,11... | collective-permute-start | bytes 294920 | tf_op jit(solution)/shard_map/ppermute | solution.py:537
  70.7 1.3 %collective-permute-start.23 = (f32[96,256]{1,0:T(8,128)S(1)}, f32[96,256]{1,0:T(8,128)S(1)}, u32[]{:S(2)}, u32[]{:S(2)}) collective-permute-start(f32[96,256]{1,0:T(8,128)S(1)} %collective-permute-done.19.refs_3_), channel_id=1, source_target_pairs={{0,1},{1,0},{2,3},{3,2},{4,5},{5,4},{6,7},{7,6},{8,9},{9,8},{10,11... | collective-permute-start | bytes 294920 | tf_op jit(solution)/shard_map/ppermute | solution.py:537

commit v4 on v3

--- a/solution.py
+++ b/solution.py
@@ -14,6 +14,7 @@
 f32 = jnp.float32
 bf16 = jnp.bfloat16
 LANES = 128
+LOW = 64
 FEATURES = 32
 PAIRS = ((0, 0), (0, 1), (1, 0), (1, 1), (0, 2), (2, 0))
 VMEM = pl.BlockSpec(memory_space=pltpu.VMEM)
@@ -27,14 +28,14 @@
     )
 
 
-def exact_dot(a, b, ca, cb):
-    return dot(a, b, ca, cb, lax.Precision.HIGHEST)
+def split(value):
+    high = value.astype(bf16)
+    return high, (value - high.astype(f32)).astype(bf16)
 
 
 def close_dot(a, b, ca, cb):
-    a_high, b_high = a.astype(bf16), b.astype(bf16)
-    a_low = (a - a_high.astype(f32)).astype(bf16)
-    b_low = (b - b_high.astype(f32)).astype(bf16)
+    a_high, a_low = split(a)
+    b_high, b_low = split(b)
     return (dot(a_low, b_high, ca, cb) + dot(a_high, b_low, ca, cb)) + dot(a_high, b_high, ca, cb)
 
 
@@ -50,7 +51,7 @@
 
 
 def geometry_kernel(
-    scale, blocks_ref, vertices_ref, corners_ref, layers_ref, a_ref, b_ref, diag_ref, plain, table, a_rows, b_rows
+    scale, near, blocks_ref, vertices_ref, corners_ref, layers_ref, a_ref, b_ref, diag_ref, plain, table, a_rows, b_rows
 ):
     count = corners_ref.shape[1]
     tops = plain.shape[0]
@@ -62,20 +63,28 @@
                 plain[top : top + 1, axis * LANES : (axis + 1) * LANES] = vertices_ref[
                     axis : axis + 1, top * LANES : (top + 1) * LANES
                 ]
-        for at, part in enumerate(pieces_of(plain[...])):
-            table[at * tops : (at + 1) * tops, :] = part.astype(bf16)
-
-    top_iota = lax.broadcasted_iota(jnp.int32, (tops, count), 0)
-    low_iota = lax.broadcasted_iota(jnp.int32, (LANES, count), 0)
+        for axis in range(3):
+            for side in range(2):
+                begin = axis * LANES + side * LOW
+                value = plain[:, begin : begin + LOW]
+                high = value.astype(bf16)
+                low = (value - high.astype(f32)).astype(bf16)
+                for at, part in enumerate((high, low)):
+                    row = (2 * at + side) * tops
+                    table[row : row + tops, axis * LOW : (axis + 1) * LOW] = part
+
+    top_iota = lax.broadcasted_iota(jnp.int32, (2 * tops, count), 0)
+    low_iota = lax.broadcasted_iota(jnp.int32, (LOW, count), 0)
     points = []
     for corner in range(3):
         index = corners_ref[corner : corner + 1, :]
-        top = jnp.where(top_iota == (index >> 7), 1.0, 0.0).astype(bf16)
-        low = low_iota == (index & (LANES - 1))
-        found = dot(table[...], jnp.concatenate([top, top, top], axis=0), 0, 0)
+        place = (index >> 7) + tops * ((index >> 6) & 1)
+        top = jnp.where(top_iota == place, 1.0, 0.0).astype(bf16)
+        low = low_iota == (index & (LOW - 1))
+        found = dot(table[...], jnp.concatenate([top, top], axis=0), 0, 0)
         points.append(
             [
-                jnp.sum(jnp.where(low, found[axis * LANES : (axis + 1) * LANES], 0.0), axis=0, keepdims=True)
+                jnp.sum(jnp.where(low, found[axis * LOW : (axis + 1) * LOW], 0.0), axis=0, keepdims=True)
                 for axis in range(3)
             ]
         )
@@ -94,28 +103,35 @@
     norm = centre[0] * centre[0] + centre[1] * centre[1] + centre[2] * centre[2]
     a_side = [unit * norm, unit] + [unit * c for c in centre]
     b_side = [unit, unit * (norm + smooth_sq)] + [-2.0 * unit * c for c in centre]
-    a_parts = [pieces_of(value) for value in a_side]
-    b_parts = [pieces_of(value) for value in b_side]
-    row = 0
-    for a_piece, b_piece in PAIRS:
-        for term in range(5):
-            a_rows[row : row + 1, :] = a_parts[term][a_piece]
-            b_rows[row : row + 1, :] = b_parts[term][b_piece]
-            row += 1
-    blank = jnp.zeros((FEATURES - row, count), f32)
-    a_rows[row:, :] = blank
-    b_rows[row:, :] = blank
-    a_ref[...] = a_rows[...].astype(bf16)
-    b_ref[...] = b_rows[...].astype(bf16)
+    block = pl.program_id(0)
+
+    def store(values, which, rows, out_ref):
+        parts = [pieces_of(value) for value in values]
+        row = 0
+        for pair in PAIRS:
+            for term in range(5):
+                rows[row : row + 1, :] = parts[term][pair[which]]
+                row += 1
+        rows[row:, :] = jnp.zeros((FEATURES - row, count), f32)
+        out_ref[...] = rows[...].astype(bf16)
+
+    @pl.when(block < near)
+    def _():
+        store(a_side, 0, a_rows, a_ref)
+
+    @pl.when(block >= near - 1)
+    def _():
+        store(b_side, 1, b_rows, b_ref)
+
     diag_ref[...] = weight * weight * (lax.rsqrt(jnp.full_like(weight, smooth_sq)) * scale + self_term)
 
 
-def geometry(blocks, vertices, corners, layers, count, scale):
+def geometry(blocks, near, vertices, corners, layers, count, scale):
     n = blocks.shape[0]
     points = vertices.shape[1]
     tops = points // LANES
     return pl.pallas_call(
-        functools.partial(geometry_kernel, scale),
+        functools.partial(geometry_kernel, scale, near),
         grid_spec=pltpu.PrefetchScalarGridSpec(
             num_scalar_prefetch=1,
             grid=(n,),
@@ -125,20 +141,20 @@
                 pl.BlockSpec((1, count), lambda g, blk: (0, blk[g])),
             ],
             out_specs=[
-                pl.BlockSpec((None, FEATURES, count), lambda g, blk: (g, 0, 0)),
-                pl.BlockSpec((None, FEATURES, count), lambda g, blk: (g, 0, 0)),
+                pl.BlockSpec((None, FEATURES, count), lambda g, blk: (jnp.minimum(g, near - 1), 0, 0)),
+                pl.BlockSpec((None, FEATURES, count), lambda g, blk: (jnp.maximum(g - near + 1, 0), 0, 0)),
                 pl.BlockSpec((None, 1, count), lambda g, blk: (g, 0, 0)),
             ],
             scratch_shapes=[
                 pltpu.VMEM((tops, 3 * LANES), f32),
-                pltpu.VMEM((3 * tops, 3 * LANES), bf16),
+                pltpu.VMEM((4 * tops, 3 * LOW), bf16),
                 pltpu.VMEM((FEATURES, count), f32),
                 pltpu.VMEM((FEATURES, count), f32),
             ],
         ),
         out_shape=(
-            jax.ShapeDtypeStruct((n, FEATURES, count), bf16),
-            jax.ShapeDtypeStruct((n, FEATURES, count), bf16),
+            jax.ShapeDtypeStruct((near, FEATURES, count), bf16),
+            jax.ShapeDtypeStruct((n - near + 1, FEATURES, count), bf16),
             jax.ShapeDtypeStruct((n, 1, count), f32),
         ),
         compiler_params=params(),
@@ -374,34 +390,36 @@
     return guess * (2.0 - value * guess)
 
 
-def eliminate(panel, begin, width):
+def eliminate(panel, begin, window):
     size, total = panel.shape
     parts = [panel[:, at : at + LANES] for at in range(0, total, LANES)]
     row_at = lax.broadcasted_iota(jnp.int32, (size, LANES), 0)
     col_at = lax.broadcasted_iota(jnp.int32, (1, LANES), 1)
-    for group in range(0, size, width):
-        own = parts[(begin + group) // LANES]
-        first = (begin + group) % LANES
-        cols = [jnp.broadcast_to(own[:, first + at : first + at + 1], (size, LANES)) for at in range(width)]
-        for at in range(width):
-            pivot = group + at
-            value = cols[at][pivot : pivot + 1, :]
-            inverse = reciprocal(value)
-            col = jnp.where(row_at == pivot, cols[at] - 1.0, cols[at])
-            for part in range(len(parts)):
-                row = parts[part][pivot : pivot + 1, :]
-                if part == (begin + pivot) // LANES:
-                    row = jnp.where(col_at == (begin + pivot) % LANES, value + 1.0, row)
-                parts[part] = parts[part] - col * (row * inverse)
-            for later in range(at + 1, width):
-                cols[later] = cols[later] - col * (cols[later][pivot : pivot + 1, :] * inverse)
+
+    def spread(pivot):
+        place = (begin + pivot) % LANES
+        return jnp.broadcast_to(parts[(begin + pivot) // LANES][:, place : place + 1], (size, LANES))
+
+    cols = [spread(pivot) for pivot in range(window)]
+    for pivot in range(size):
+        col = cols.pop(0)
+        inverse = reciprocal(col[pivot : pivot + 1, :])
+        col = col - jnp.where(row_at == pivot, 1.0, 0.0)
+        for part in range(len(parts)):
+            row = parts[part][pivot : pivot + 1, :]
+            if part == (begin + pivot) // LANES:
+                row = row + jnp.where(col_at == (begin + pivot) % LANES, 1.0, 0.0)
+            parts[part] = parts[part] - col * (row * inverse)
+        cols = [later - col * (later[pivot : pivot + 1, :] * inverse) for later in cols]
+        if pivot + window < size:
+            cols.append(spread(pivot + window))
     return jnp.concatenate(parts, axis=1)
 
 
 def sweep(ref, begin, size):
     total = ref.shape[0]
     panel = ref[begin : begin + size, :]
-    row = eliminate(panel, begin, 8)
+    row = eliminate(panel, begin, 6)
     col_at = lax.broadcasted_iota(jnp.int32, panel.shape, 1)
     left = [part.astype(bf16) for part in pieces_of(jnp.where(col_at < begin, -panel, panel))]
     right = [part.astype(bf16) for part in pieces_of(row)]
@@ -496,36 +514,55 @@
     )(places, diag, *currents[1:], *gots, *rests)
 
 
-def finish_kernel(ranks, place_ref, step_ref, turn_ref, *refs):
-    currents, images = refs[:ranks], refs[ranks : 2 * ranks]
-    solution_ref, remainder_ref, direction_ref, current_all, image_all = refs[2 * ranks :]
-    columns = currents[0].shape[0]
+def finish_kernel(ranks, chunks, place_ref, step_ref, turn_ref, *refs):
+    currents, images, refs = refs[:ranks], refs[ranks : 2 * ranks], refs[2 * ranks :]
+    outs, made, (current_all, image_all, sems) = refs[:3], refs[3:6], refs[6:]
+    columns, count = currents[0].shape
     for rank in range(ranks):
         at = pl.ds(pl.multiple_of(place_ref[rank] * columns, columns), columns)
         current_all[at, :] = currents[rank][...]
         image_all[at, :] = images[rank][...]
-    current, step = current_all[...], step_ref[...]
-    solution_ref[...] = close_dot(step, current, 1, 0)
-    remainder = currents[0][...] - close_dot(step, image_all[...], 1, 0)
-    remainder_ref[...] = remainder
-    direction_ref[...] = remainder + close_dot(turn_ref[...], current, 1, 0)
+    step_high, step_low = split(step_ref[...])
+    turn_high, turn_low = split(turn_ref[...])
+    both = jnp.concatenate([step_high, step_low, turn_high, turn_low], axis=0)
+    highs = jnp.concatenate([step_high, turn_high], axis=0)
+    steps = jnp.concatenate([step_high, step_low], axis=0)
+    width = count // chunks
+    copies = []
+    for chunk in range(chunks):
+        lanes = pl.ds(chunk * width, width)
+        current_high, current_low = split(current_all[:, lanes])
+        image_high, image_low = split(image_all[:, lanes])
+        every = dot(both, current_high, 1, 0)
+        rest = dot(highs, current_low, 1, 0)
+        away = dot(steps, image_high, 1, 0)
+        step_part, step_more, turn_part, turn_more = (every[at * columns : (at + 1) * columns] for at in range(4))
+        away = away[:columns] + (away[columns:] + dot(step_high, image_low, 1, 0))
+        remainder = currents[0][:, lanes] - away
+        made[0][:, lanes] = step_part + (step_more + rest[:columns])
+        made[1][:, lanes] = remainder
+        made[2][:, lanes] = remainder + (turn_part + (turn_more + rest[columns:]))
+        for at in range(3):
+            copy = pltpu.make_async_copy(made[at].at[:, lanes], outs[at].at[:, lanes], sems.at[at, chunk])
+            copy.start()
+            copies.append(copy)
+    for copy in copies:
+        copy.wait()
 
 
 def finish(places, step, turn, currents, images):
     ranks = len(currents)
     columns, count = currents[0].shape
     total = ranks * columns
-    width = max(count // 4, LANES)
-    out = jax.ShapeDtypeStruct((columns, count), f32)
-    rows = pl.BlockSpec((columns, width), lambda at: (0, at))
-    whole = pl.BlockSpec((columns, total), lambda at: (0, 0))
-    return pl.pallas_call(
-        functools.partial(finish_kernel, ranks),
-        grid=(count // width,),
-        in_specs=[SMEM, whole, whole] + [rows] * (2 * ranks),
-        out_specs=[rows] * 3,
-        out_shape=(out, out, out),
-        scratch_shapes=[pltpu.VMEM((total, width), f32)] * 2,
+    chunks = 2
+    return pl.pallas_call(
+        functools.partial(finish_kernel, ranks, chunks),
+        in_specs=[SMEM] + [VMEM] * (2 * ranks + 2),
+        out_specs=[pl.BlockSpec(memory_space=pl.ANY)] * 3,
+        out_shape=[jax.ShapeDtypeStruct((columns, count), f32)] * 3,
+        scratch_shapes=[pltpu.VMEM((columns, count), f32)] * 3
+        + [pltpu.VMEM((total, count), f32)] * 2
+        + [pltpu.SemaphoreType.DMA((3, chunks))],
         compiler_params=params(),
         cost_estimate=SMALL,
         name="finish",
@@ -589,9 +626,8 @@
     near_blocks = [(tri ^ bits) * cores + core for bits in range(1, near)]
     vertices, packed = lax.optimization_barrier((vertices, packed))
     blocks = indices(*reversed(near_blocks), *own_blocks)
-    a_side, b_side, diag = geometry(blocks, vertices, corners, layers, count, scale)
+    a_side, b_side, diag = geometry(blocks, near, vertices, corners, layers, count, scale)
     diag = diag[near - 1]
-    b_side = b_side[near - 1 :]
     slots = list(reversed(range(near)))
     sides = [a_side, b_side, swap(b_side, "split", 1)]
     half_place = half_of(rank ^ 1, rank) if ranks > 1 else jnp.int32(0)
@@ -626,7 +662,7 @@
             )
             arrived[half] = [swap(value, "tri", near * far) for far, value in zip(fars, far_sum[half])]
             sides, _ = lax.optimization_barrier((sides, far_sum))
-        sources, _ = lax.optimization_barrier((sources, sent))
+        sources, _ = lax.optimization_barrier((sources, far_sum[0]))
     mine = stack_rows(sources, a_side, near)
     theirs = swap(mine, "split", 1)
     theirs, _ = lax.optimization_barrier((theirs, far_sum))

time: 87.2 us -> 84.6 us (0.970)
  starting transfers between devices: 21 us -> 23.8 us
  Pallas kernels: 41.7 us -> 39 us
  waiting for transfers between devices: 21.7 us -> 19 us
    ppermute x23, waiting for transfers between devices: 19.4 us -> 16.5 us  [swap(): return lax.ppermute(value, axis, [(at, at ^ bits) for at in range(size)])]
    ppermute x23, starting transfers between devices: 19.5 us -> 22.3 us  [swap(): return lax.ppermute(value, axis, [(at, at ^ bits) for at in range(size)])]
    pallas_call x2, Pallas kernels: 9.59 us -> 7.15 us  [the longest x1 4.88 us: geometry(): pl.pallas_call(functools.partial(geometry_kernel, scale, near), grid_spec...]
  transfers between devices with their start and end apart: 24 -> 24, of which waited for: 13 -> 15; matrix products, arithmetic and copies ran while one was open for 0% -> 0% of each run, Pallas kernels for 28% -> 26%
where the time goes in v4:
time: 84.6 us; the launch traced here: 84.4 us
  Pallas kernels  39 us (46%)
  starting transfers between devices  23.8 us (28%)
  waiting for transfers between devices  19 us (22%)
  other arithmetic  1.43 us (2%)
  between operations  1.07 us (1%)
    ppermute x23, starting transfers between devices, swap(): return lax.ppermute(value, axis, [(at, at ^ bits) for at in range(size)])  22.3 us
    ppermute x23, waiting for transfers between devices, swap(): return lax.ppermute(value, axis, [(at, at ^ bits) for at in range(size)])  16.5 us
    pallas_call x1, Pallas kernels, solve(): pl.pallas_call(functools.partial(solve_kernel, columns, 32), in_specs=[SM...  11.6 us
    pallas_call x8, Pallas kernels, image_part(): pl.pallas_call(functools.partial(image_kernel, range(len(densities)), slo...  9.32 us
    pallas_call x1, Pallas kernels, own_image(): pl.pallas_call(functools.partial(own_kernel, near), in_specs=[VMEM] * 3,...  7.43 us
    pallas_call x1, Pallas kernels, geometry(): pl.pallas_call(functools.partial(geometry_kernel, scale, near), grid_spec...  4.88 us
    ppermute x1, waiting for transfers between devices, pair_swap(): return lax.ppermute(value, ('tri', 'rhs'), perm)  2.53 us
    pallas_call x1, Pallas kernels, finish(): pl.pallas_call(functools.partial(finish_kernel, ranks, chunks), in_specs=...  2.27 us
  transfers between devices with their start and end apart: 24, of which 15 were waited for; matrix products, arithmetic and copies ran while one was open for 0% of the time, Pallas kernels for 26%

profile of v4, /device:TPU:0, one launch (start us, length us, event | category | flops | bytes accessed | tf_op | source)
XLA Modules:
  0.0 84.4 jit_solution(5899224120118163237)
XLA Ops:
  0.7 1.2 %fusion = (bf16[128,1024]{1,0:T(8,128)(2,1)S(1)}, f32[128,1024]{1,0:T(8,128)S(1)}) fusion(f32[128,1024]{1,0:T(8,128)} %param.5, s32[1024]{0:T(1024)S(1)} %iota_add_fusion, s32[128]{0:T(128)} %param.6), kind=kLoop, calls=%fused_computation.6 | loop fusion | flops 524288 | bytes 1315328 | tf_op jit(solution)/shard_map/convert_element_type | solution.py:621
  1.9 3.0 %collective-permute-start.4 = (f32[128,1024]{1,0:T(8,128)S(1)}, f32[128,1024]{1,0:T(8,128)S(1)}, u32[]{:S(2)}, u32[]{:S(2)}) collective-permute-start(f32[128,1024]{1,0:T(8,128)S(1)} %get-tuple-element.78.refs_0_), channel_id=1, source_target_pairs={{0,2},{2,0},{1,3},{3,1},{4,6},{6,4},{5,7},{7,5},{8,10},{10,8},{9,1... | collective-permute-start | bytes 1572872 | tf_op jit(solution)/shard_map/ppermute | solution.py:574
  5.0 1.5 %collective-permute-start = (bf16[128,1024]{1,0:T(8,128)(2,1)S(1)}, bf16[128,1024]{1,0:T(8,128)(2,1)S(1)}, u32[]{:S(2)}, u32[]{:S(2)}) collective-permute-start(bf16[128,1024]{1,0:T(8,128)(2,1)S(1)} %get-tuple-element.69.refs_0_), channel_id=1, source_target_pairs={{0,4},{4,0},{8,12},{12,8},{16,20},{20,16},{24,28},{28,24},{1,5},{5... | collective-permute-start | bytes 786440 | tf_op jit(solution)/shard_map/ppermute | solution.py:574
  6.4 1.6 %collective-permute-start.1 = (bf16[128,1024]{1,0:T(8,128)(2,1)S(1)}, bf16[128,1024]{1,0:T(8,128)(2,1)S(1)}, u32[]{:S(2)}, u32[]{:S(2)}) collective-permute-start(bf16[128,1024]{1,0:T(8,128)(2,1)S(1)} %get-tuple-element.69.refs_0_), channel_id=1, source_target_pairs={{0,8},{4,12},{8,0},{12,4},{16,24},{20,28},{24,16},{28,20},{1,9},{5... | collective-permute-start | bytes 786440 | tf_op jit(solution)/shard_map/ppermute | solution.py:574
  8.0 0.4 collective-permute-start.2
  8.5 4.9 %geometry.1 = (bf16[4,32,1024]{2,1,0:T(8,128)(2,1)S(1)}, bf16[2,32,1024]{2,1,0:T(8,128)(2,1)S(1)}, f32[5,1,1024]{2,1,0:T(1,128)S(1)}) custom-call(s32[5]{0:T(128)S(1)} %stack.94.blocks_ref, f32[3,8192]{1,0:T(4,128)S(1)} %copy-done.1, s32[3,16384]{1,0:T(4,128)S(1)} %copy-done, s32[1,16384]{1,0:T(1,128)S(1)} %bitcast.22), custom_call_target="tpu_custom_call" | custom-call | tf_op jit(solution)/shard_map/geometry/pallas_call | solution.py:133
  13.5 1.0 %image_part.8.refs_5_ = f32[128,1024]{1,0:T(8,128)S(1)} custom-call(s32[1]{0:T(128)} %bitcast.13.first_ref, bf16[128,1024]{1,0:T(8,128)(2,1)S(1)} %get-tuple-element.69.refs_0_, bf16[4,32,1024]{2,1,0:T(8,128)(2,1)S(1)} %get-tuple-element.73.refs_1_.refs_4_, bf16[2,32,1024]{2,1,0:T(8,128)(2,1)S(1)} %get-tuple-element.74.refs_2_.b_ref), custom_call_target="tpu_custom_call" | custom-call | flops 1024 | bytes 1024 | tf_op jit(solution)/shard_map/image_part/pallas_call | solution.py:197
  14.6 0.3 collective-permute-done.3.refs_3_
  14.8 1.0 %image_part.9.refs_4_ = f32[128,1024]{1,0:T(8,128)S(1)} custom-call(s32[1]{0:T(128)} %bitcast.13.first_ref, bf16[128,1024]{1,0:T(8,128)(2,1)S(1)} %get-tuple-element.69.refs_0_, bf16[4,32,1024]{2,1,0:T(8,128)(2,1)S(1)} %get-tuple-element.73.refs_1_.refs_4_, bf16[2,32,1024]{2,1,0:T(8,128)(2,1)S(1)} %get-tuple-element.74.refs_2_.b_ref, ...), custom_call_target="tpu_custom_call" | custom-call | flops 1024 | bytes 1024 | tf_op jit(solution)/shard_map/image_part/pallas_call | solution.py:197
  15.9 2.0 %image_part.10 = (f32[128,1024]{1,0:T(8,128)S(1)}, f32[128,1024]{1,0:T(8,128)S(1)}) custom-call(s32[1]{0:T(128)} %bitcast.13.first_ref, bf16[128,1024]{1,0:T(8,128)(2,1)S(1)} %collective-permute-done.refs_0_.refs_1_, bf16[4,32,1024]{2,1,0:T(8,128)(2,1)S(1)} %get-tuple-element.73.refs_1_.refs_4_, bf16[2,32,1024]{2,1,0:T(8,128)(2,1)S(1)} %get-tuple-element.74.refs_2_.b_ref, ...), custom_call_target="tpu_custom_call" | custom-call | flops 1024 | bytes 1024 | tf_op jit(solution)/shard_map/image_part/pallas_call | solution.py:197
  17.9 2.0 %image_part.11 = (f32[128,1024]{1,0:T(8,128)S(1)}, f32[128,1024]{1,0:T(8,128)S(1)}) custom-call(s32[1]{0:T(128)} %bitcast.13.first_ref, bf16[128,1024]{1,0:T(8,128)(2,1)S(1)} %collective-permute-done.1.refs_0_.refs_2_, bf16[4,32,1024]{2,1,0:T(8,128)(2,1)S(1)} %get-tuple-element.73.refs_1_.refs_4_, bf16[2,32,1024]{2,1,0:T(8,128)(2,1)S(1)} %get-tuple-element.74.refs_2_.b_ref, ...), custom_call_target="tpu_custom_call" | custom-call | flops 1024 | bytes 1024 | tf_op jit(solution)/shard_map/image_part/pallas_call | solution.py:197
  19.9 0.8 image_part.12
  20.7 0.3 collective-permute-start.5
  21.0 0.8 image_part.13
  21.8 0.3 collective-permute-done.5.refs_4_
  22.1 0.8 image_part.14
  23.0 0.3 collective-permute-start.6
  23.3 0.3 collective-permute-start.7
  23.6 2.6 %collective-permute-start.8 = (bf16[128,512]{1,0:T(8,128)(2,1)S(1)}, bf16[128,512]{1,0:T(8,128)(2,1)S(1)}, u32[]{:S(2)}, u32[]{:S(2)}) collective-permute-start(bf16[128,512]{1,0:T(8,128)(2,1)S(1)} %image_part.14), channel_id=1, source_target_pairs={{0,16},{4,20},{8,24},{12,28},{16,0},{20,4},{24,8},{28,12},{1,17},{... | collective-permute-start | bytes 393224 | tf_op jit(solution)/shard_map/ppermute | solution.py:574
  26.3 0.8 image_part.15
  27.2 2.7 %collective-permute-start.9 = (bf16[128,512]{1,0:T(8,128)(2,1)S(1)}, bf16[128,512]{1,0:T(8,128)(2,1)S(1)}, u32[]{:S(2)}, u32[]{:S(2)}) collective-permute-start(bf16[128,512]{1,0:T(8,128)(2,1)S(1)} %image_part.15), channel_id=1, source_target_pairs={{0,16},{4,20},{8,24},{12,28},{16,0},{20,4},{24,8},{28,12},{1,17},{... | collective-permute-start | bytes 393224 | tf_op jit(solution)/shard_map/ppermute | solution.py:574
  29.8 7.4 %own_image.1.own_ref = f32[128,1024]{1,0:T(8,128)S(1)} custom-call(bf16[640,1024]{1,0:T(8,128)(2,1)S(1)} %stack_rows.1.mine_ref, bf16[640,1024]{1,0:T(8,128)(2,1)S(1)} %collective-permute-done.6.theirs_ref, bf16[2,32,1024]{2,1,0:T(8,128)(2,1)S(1)} %get-tuple-element.74.refs_2_.b_ref), custom_call_target="tpu_custom_call" | custom-call | flops 1024 | bytes 1024 | tf_op jit(solution)/shard_map/own_image/pallas_call | solution.py:256
  37.3 0.6 collective-permute-start.10
  38.0 0.6 collective-permute-done.9.refs_0_
  38.6 1.3 %gram.1 = (f32[2,384,128]{2,1,0:T(8,128)S(1)}, f32[128,1024]{1,0:T(8,128)S(1)}) custom-call(s32[1]{0:T(128)} %bitcast.13.first_ref, f32[1,1024]{1,0:T(1,128)S(1)} %slice_bitcast_fusion.diag_ref, f32[128,512]{1,0:T(8,128)S(1)} %get-tuple-element.76.first_half, f32[128,512]{1,0:T(8,128)S(1)} %get-tuple-element.77.second_half, ...), custom_call_target="tpu_custom_call" | custom-call | flops 1024 | bytes 1024 | tf_op jit(solution)/shard_map/gram/pallas_call | solution.py:314
  39.9 2.8 %collective-permute-done.10.refs_1_ = bf16[128,512]{1,0:T(8,128)(2,1)S(1)} collective-permute-done((bf16[128,512]{1,0:T(8,128)(2,1)S(1)}, bf16[128,512]{1,0:T(8,128)(2,1)S(1)}, u32[]{:S(2)}, u32[]{:S(2)}) %collective-permute-start.10) | collective-permute-done | bytes 131104 | tf_op jit(solution)/shard_map/ppermute | solution.py:574
  42.7 0.9 %cross.1 = (f32[192,256]{1,0:T(8,128)S(1)}, f32[192,256]{1,0:T(8,128)S(1)}) custom-call(s32[2]{0:T(128)S(1)} %pad_add_fusion.place_ref, s32[1]{0:T(128)} %bitcast.12.core_ref, f32[2,384,128]{2,1,0:T(8,128)S(1)} %get-tuple-element.80.block_ref, f32[128,1024]{1,0:T(8,128)S(1)} %get-tuple-element.81.image_ref.refs_2_, ...), custom_call_target="tpu_custom_call" | custom-call | flops 1024 | bytes 1024 | tf_op jit(solution)/shard_map/cross/pallas_call | solution.py:353
  43.8 1.3 %collective-permute-done.11.got_ref = f32[192,256]{1,0:T(8,128)S(1)} collective-permute-done((f32[192,256]{1,0:T(8,128)S(1)}, f32[192,256]{1,0:T(8,128)S(1)}, u32[]{:S(2)}, u32[]{:S(2)}) %collective-permute-start.11) | collective-permute-done | bytes 196640 | tf_op jit(solution)/shard_map/ppermute | solution.py:574
  45.2 0.6 shares.1
  45.7 1.5 %collective-permute-start.12 = (f32[96,256]{1,0:T(8,128)S(1)}, f32[96,256]{1,0:T(8,128)S(1)}, u32[]{:S(2)}, u32[]{:S(2)}) collective-permute-start(f32[96,256]{1,0:T(8,128)S(1)} %get-tuple-element.86), channel_id=1, source_target_pairs={{0,4},{4,0},{8,12},{12,8},{16,20},{20,16},{24,28},{28,24},{1,5},{5... | collective-permute-start | bytes 294920 | tf_op jit(solution)/shard_map/ppermute | solution.py:574
  47.3 0.5 collective-permute-start.16
  47.8 2.9 %collective-permute-done.12 = f32[96,256]{1,0:T(8,128)S(1)} collective-permute-done((f32[96,256]{1,0:T(8,128)S(1)}, f32[96,256]{1,0:T(8,128)S(1)}, u32[]{:S(2)}, u32[]{:S(2)}) %collective-permute-start.12) | collective-permute-done | bytes 98336 | tf_op jit(solution)/shard_map/ppermute | solution.py:574
  50.7 2.1 %collective-permute-start.15 = (f32[96,256]{1,0:T(8,128)S(1)}, f32[96,256]{1,0:T(8,128)S(1)}, u32[]{:S(2)}, u32[]{:S(2)}) collective-permute-start(f32[96,256]{1,0:T(8,128)S(1)} %add.101), channel_id=1, source_target_pairs={{0,24},{4,28},{8,16},{12,20},{16,8},{20,12},{24,0},{28,4},{1,25},{... | collective-permute-start | bytes 294920 | tf_op jit(solution)/shard_map/ppermute | solution.py:574
  52.8 0.9 %collective-permute-start.14 = (f32[96,256]{1,0:T(8,128)S(1)}, f32[96,256]{1,0:T(8,128)S(1)}, u32[]{:S(2)}, u32[]{:S(2)}) collective-permute-start(f32[96,256]{1,0:T(8,128)S(1)} %add.101), channel_id=1, source_target_pairs={{0,16},{4,20},{8,24},{12,28},{16,0},{20,4},{24,8},{28,12},{1,17},{... | collective-permute-start | bytes 294920 | tf_op jit(solution)/shard_map/ppermute | solution.py:574
  53.7 1.4 %collective-permute-start.13 = (f32[96,256]{1,0:T(8,128)S(1)}, f32[96,256]{1,0:T(8,128)S(1)}, u32[]{:S(2)}, u32[]{:S(2)}) collective-permute-start(f32[96,256]{1,0:T(8,128)S(1)} %add.101), channel_id=1, source_target_pairs={{0,8},{4,12},{8,0},{12,4},{16,24},{20,28},{24,16},{28,20},{1,9},{5... | collective-permute-start | bytes 294920 | tf_op jit(solution)/shard_map/ppermute | solution.py:574
  55.1 0.6 other_images.1.refs_3_
  55.7 2.5 %collective-permute-done.15 = f32[96,256]{1,0:T(8,128)S(1)} collective-permute-done((f32[96,256]{1,0:T(8,128)S(1)}, f32[96,256]{1,0:T(8,128)S(1)}, u32[]{:S(2)}, u32[]{:S(2)}) %collective-permute-start.15) | collective-permute-done | bytes 98336 | tf_op jit(solution)/shard_map/ppermute | solution.py:574
  58.3 3.8 %collective-permute-done.14 = f32[96,256]{1,0:T(8,128)S(1)} collective-permute-done((f32[96,256]{1,0:T(8,128)S(1)}, f32[96,256]{1,0:T(8,128)S(1)}, u32[]{:S(2)}, u32[]{:S(2)}) %collective-permute-start.14) | collective-permute-done | bytes 98336 | tf_op jit(solution)/shard_map/ppermute | solution.py:574
  62.1 1.5 %collective-permute-start.19 = (f32[96,256]{1,0:T(8,128)S(1)}, f32[96,256]{1,0:T(8,128)S(1)}, u32[]{:S(2)}, u32[]{:S(2)}) collective-permute-start(f32[96,256]{1,0:T(8,128)S(1)} %add_add_fusion.refs_0_), channel_id=1, source_target_pairs={{0,6},{2,4},{4,2},{6,0},{8,14},{10,12},{12,10},{14,8},{16,22},{18,... | collective-permute-start | bytes 294920 | tf_op jit(solution)/shard_map/ppermute | solution.py:587
  63.6 0.5 collective-permute-start.18
  64.1 1.5 %collective-permute-start.17 = (f32[96,256]{1,0:T(8,128)S(1)}, f32[96,256]{1,0:T(8,128)S(1)}, u32[]{:S(2)}, u32[]{:S(2)}) collective-permute-start(f32[96,256]{1,0:T(8,128)S(1)} %add_add_fusion.refs_0_), channel_id=1, source_target_pairs={{0,2},{2,0},{1,3},{3,1},{4,6},{6,4},{5,7},{7,5},{8,10},{10,8},{9,1... | collective-permute-start | bytes 294920 | tf_op jit(solution)/shard_map/ppermute | solution.py:574
  65.6 2.5 %collective-permute-done.19.refs_3_ = f32[96,256]{1,0:T(8,128)S(1)} collective-permute-done((f32[96,256]{1,0:T(8,128)S(1)}, f32[96,256]{1,0:T(8,128)S(1)}, u32[]{:S(2)}, u32[]{:S(2)}) %collective-permute-start.19) | collective-permute-done | bytes 98336 | tf_op jit(solution)/shard_map/ppermute | solution.py:587
  68.3 0.4 collective-permute-start.22
  68.7 0.5 collective-permute-done.17.refs_1_
  69.2 0.2 collective-permute-done.23.refs_7_
  69.6 0.8 %collective-permute-done.21.refs_5_ = f32[96,256]{1,0:T(8,128)S(1)} collective-permute-done((f32[96,256]{1,0:T(8,128)S(1)}, f32[96,256]{1,0:T(8,128)S(1)}, u32[]{:S(2)}, u32[]{:S(2)}) %collective-permute-start.21) | collective-permute-done | bytes 98336 | tf_op jit(solution)/shard_map/ppermute | solution.py:574
  70.5 11.6 %solve.1 = (f32[128,256]{1,0:T(8,128)S(1)}, f32[128,256]{1,0:T(8,128)S(1)}) custom-call(s32[2]{0:T(128)S(1)} %pad_add_fusion.place_ref, s32[8]{0:T(128)S(1)} %stack.82.share_ref, f32[96,256]{1,0:T(8,128)S(1)} %add_add_fusion.refs_0_, f32[96,256]{1,0:T(8,128)S(1)} %collective-permute-done.17.refs_1_, f32[96,256]{1,0:T(8,128)S(1)} %collective-permute-done.18.refs_2_, ...), custom_call_target="tpu_custom_call" | custom-call | tf_op jit(solution)/shard_map/solve/pallas_call | solution.py:476
  82.0 2.3 %finish.1 = (f32[128,1024]{1,0:T(8,128)}, f32[128,1024]{1,0:T(8,128)}, f32[128,1024]{1,0:T(8,128)}) custom-call(s32[2]{0:T(128)S(1)} %pad_add_fusion.place_ref, f32[128,256]{1,0:T(8,128)S(1)} %get-tuple-element.92.step_ref, f32[128,256]{1,0:T(8,128)S(1)} %get-tuple-element.93.turn_ref, f32[128,1024]{1,0:T(8,128)S(1)} %get-tuple-element.78.refs_0_, ...), custom_call_target="tpu_custom_call" | custom-call | flops 1024 | bytes 1024 | tf_op jit(solution)/shard_map/finish/pallas_call | solution.py:558
  (34 shorter events, 1.1 us)
Async XLA Ops:
  0.6 7.9 %copy-start.1 = (f32[3,8192]{1,0:T(4,128)S(1)}, f32[3,8192]{1,0:T(4,128)}, u32[]{:S(2)}) copy-start(f32[3,8192]{1,0:T(4,128)} %vertices_ref) | copy-start | bytes 294916
  0.6 7.9 %copy-start.2 = (s32[16384]{0:T(1024)S(1)}, s32[16384]{0:T(1024)}, u32[]{:S(2)}) copy-start(s32[16384]{0:T(1024)} %param.9) | copy-start | bytes 196612
  0.7 7.9 %copy-start = (s32[3,16384]{1,0:T(4,128)S(1)}, s32[3,16384]{1,0:T(4,128)}, u32[]{:S(2)}) copy-start(s32[3,16384]{1,0:T(4,128)} %corners_ref.1) | copy-start | bytes 589828
  1.9 17.9 %collective-permute-start.4 = (f32[128,1024]{1,0:T(8,128)S(1)}, f32[128,1024]{1,0:T(8,128)S(1)}, u32[]{:S(2)}, u32[]{:S(2)}) collective-permute-start(f32[128,1024]{1,0:T(8,128)S(1)} %get-tuple-element.78.refs_0_), channel_id=1, source_target_pairs={{0,2},{2,0},{1,3},{3,1},{4,6},{6,4},{5,7},{7,5},{8,10},{10,8},{9,1... | collective-permute-start | bytes 1572872 | tf_op jit(solution)/shard_map/ppermute | solution.py:574
  5.0 10.9 %collective-permute-start = (bf16[128,1024]{1,0:T(8,128)(2,1)S(1)}, bf16[128,1024]{1,0:T(8,128)(2,1)S(1)}, u32[]{:S(2)}, u32[]{:S(2)}) collective-permute-start(bf16[128,1024]{1,0:T(8,128)(2,1)S(1)} %get-tuple-element.69.refs_0_), channel_id=1, source_target_pairs={{0,4},{4,0},{8,12},{12,8},{16,20},{20,16},{24,28},{28,24},{1,5},{5... | collective-permute-start | bytes 786440 | tf_op jit(solution)/shard_map/ppermute | solution.py:574
  6.4 11.4 %collective-permute-start.1 = (bf16[128,1024]{1,0:T(8,128)(2,1)S(1)}, bf16[128,1024]{1,0:T(8,128)(2,1)S(1)}, u32[]{:S(2)}, u32[]{:S(2)}) collective-permute-start(bf16[128,1024]{1,0:T(8,128)(2,1)S(1)} %get-tuple-element.69.refs_0_), channel_id=1, source_target_pairs={{0,8},{4,12},{8,0},{12,4},{16,24},{20,28},{24,16},{28,20},{1,9},{5... | collective-permute-start | bytes 786440 | tf_op jit(solution)/shard_map/ppermute | solution.py:574
  8.0 11.8 %collective-permute-start.2 = (bf16[128,1024]{1,0:T(8,128)(2,1)S(1)}, bf16[128,1024]{1,0:T(8,128)(2,1)S(1)}, u32[]{:S(2)}, u32[]{:S(2)}) collective-permute-start(bf16[128,1024]{1,0:T(8,128)(2,1)S(1)} %get-tuple-element.69.refs_0_), channel_id=1, source_target_pairs={{0,12},{4,8},{8,4},{12,0},{16,28},{20,24},{24,20},{28,16},{1,13},{... | collective-permute-start | bytes 786440 | tf_op jit(solution)/shard_map/ppermute | solution.py:574
  13.4 1.4 %collective-permute-start.3 = (bf16[2,32,1024]{2,1,0:T(8,128)(2,1)S(1)}, bf16[2,32,1024]{2,1,0:T(8,128)(2,1)S(1)}, u32[]{:S(2)}, u32[]{:S(2)}) collective-permute-start(bf16[2,32,1024]{2,1,0:T(8,128)(2,1)S(1)} %get-tuple-element.74.refs_2_.b_ref), channel_id=1, source_target_pairs={{0,1},{1,0},{2,3},{3,2},{4,5},{5,4},{6,7},{7,6},{8,9},{9,8},{10,11... | collective-permute-start | bytes 393224 | tf_op jit(solution)/shard_map/ppermute | solution.py:574
  20.7 1.4 %collective-permute-start.5 = (bf16[128,512]{1,0:T(8,128)(2,1)S(1)}, bf16[128,512]{1,0:T(8,128)(2,1)S(1)}, u32[]{:S(2)}, u32[]{:S(2)}) collective-permute-start(bf16[128,512]{1,0:T(8,128)(2,1)S(1)} %image_part.12), channel_id=1, source_target_pairs={{0,1},{1,0},{2,3},{3,2},{4,5},{5,4},{6,7},{7,6},{8,9},{9,8},{10,11... | collective-permute-start | bytes 393224 | tf_op jit(solution)/shard_map/ppermute | solution.py:574
  23.0 6.8 %collective-permute-start.6 = (bf16[640,1024]{1,0:T(8,128)(2,1)S(1)}, bf16[640,1024]{1,0:T(8,128)(2,1)S(1)}, u32[]{:S(2)}, u32[]{:S(2)}) collective-permute-start(bf16[640,1024]{1,0:T(8,128)(2,1)S(1)} %stack_rows.1.mine_ref), channel_id=1, source_target_pairs={{0,1},{1,0},{2,3},{3,2},{4,5},{5,4},{6,7},{7,6},{8,9},{9,8},{10,11... | collective-permute-start | bytes 3932168 | tf_op jit(solution)/shard_map/ppermute | solution.py:574
  23.3 3.0 %collective-permute-start.7 = (bf16[128,512]{1,0:T(8,128)(2,1)S(1)}, bf16[128,512]{1,0:T(8,128)(2,1)S(1)}, u32[]{:S(2)}, u32[]{:S(2)}) collective-permute-start(bf16[128,512]{1,0:T(8,128)(2,1)S(1)} %image_part.13), channel_id=1, source_target_pairs={{0,1},{1,0},{2,3},{3,2},{4,5},{5,4},{6,7},{7,6},{8,9},{9,8},{10,11... | collective-permute-start | bytes 393224 | tf_op jit(solution)/shard_map/ppermute | solution.py:574
  23.6 13.7 %collective-permute-start.8 = (bf16[128,512]{1,0:T(8,128)(2,1)S(1)}, bf16[128,512]{1,0:T(8,128)(2,1)S(1)}, u32[]{:S(2)}, u32[]{:S(2)}) collective-permute-start(bf16[128,512]{1,0:T(8,128)(2,1)S(1)} %image_part.14), channel_id=1, source_target_pairs={{0,16},{4,20},{8,24},{12,28},{16,0},{20,4},{24,8},{28,12},{1,17},{... | collective-permute-start | bytes 393224 | tf_op jit(solution)/shard_map/ppermute | solution.py:574
  27.2 11.4 %collective-permute-start.9 = (bf16[128,512]{1,0:T(8,128)(2,1)S(1)}, bf16[128,512]{1,0:T(8,128)(2,1)S(1)}, u32[]{:S(2)}, u32[]{:S(2)}) collective-permute-start(bf16[128,512]{1,0:T(8,128)(2,1)S(1)} %image_part.15), channel_id=1, source_target_pairs={{0,16},{4,20},{8,24},{12,28},{16,0},{20,4},{24,8},{28,12},{1,17},{... | collective-permute-start | bytes 393224 | tf_op jit(solution)/shard_map/ppermute | solution.py:574
  37.3 5.4 %collective-permute-start.10 = (bf16[128,512]{1,0:T(8,128)(2,1)S(1)}, bf16[128,512]{1,0:T(8,128)(2,1)S(1)}, u32[]{:S(2)}, u32[]{:S(2)}) collective-permute-start(bf16[128,512]{1,0:T(8,128)(2,1)S(1)} %get-tuple-element.82), channel_id=1, source_target_pairs={{0,2},{2,0},{1,3},{3,1},{4,6},{6,4},{5,7},{7,5},{8,10},{10,8},{9,1... | collective-permute-start | bytes 393224 | tf_op jit(solution)/shard_map/ppermute | solution.py:574
  43.6 1.5 %collective-permute-start.11 = (f32[192,256]{1,0:T(8,128)S(1)}, f32[192,256]{1,0:T(8,128)S(1)}, u32[]{:S(2)}, u32[]{:S(2)}) collective-permute-start(f32[192,256]{1,0:T(8,128)S(1)} %get-tuple-element.84), channel_id=1, source_target_pairs={{0,1},{1,0},{2,3},{3,2},{4,5},{5,4},{6,7},{7,6},{8,9},{9,8},{10,11... | collective-permute-start | bytes 589832 | tf_op jit(solution)/shard_map/ppermute | solution.py:574
  45.7 4.9 %collective-permute-start.12 = (f32[96,256]{1,0:T(8,128)S(1)}, f32[96,256]{1,0:T(8,128)S(1)}, u32[]{:S(2)}, u32[]{:S(2)}) collective-permute-start(f32[96,256]{1,0:T(8,128)S(1)} %get-tuple-element.86), channel_id=1, source_target_pairs={{0,4},{4,0},{8,12},{12,8},{16,20},{20,16},{24,28},{28,24},{1,5},{5... | collective-permute-start | bytes 294920 | tf_op jit(solution)/shard_map/ppermute | solution.py:574
  47.3 7.9 %collective-permute-start.16 = (bf16[128,512]{1,0:T(8,128)(2,1)S(1)}, bf16[128,512]{1,0:T(8,128)(2,1)S(1)}, u32[]{:S(2)}, u32[]{:S(2)}) collective-permute-start(bf16[128,512]{1,0:T(8,128)(2,1)S(1)} %get-tuple-element.88), channel_id=1, source_target_pairs={{0,2},{2,0},{1,3},{3,1},{4,6},{6,4},{5,7},{7,5},{8,10},{10,8},{9,1... | collective-permute-start | bytes 393224 | tf_op jit(solution)/shard_map/ppermute | solution.py:574
  50.7 7.6 %collective-permute-start.15 = (f32[96,256]{1,0:T(8,128)S(1)}, f32[96,256]{1,0:T(8,128)S(1)}, u32[]{:S(2)}, u32[]{:S(2)}) collective-permute-start(f32[96,256]{1,0:T(8,128)S(1)} %add.101), channel_id=1, source_target_pairs={{0,24},{4,28},{8,16},{12,20},{16,8},{20,12},{24,0},{28,4},{1,25},{... | collective-permute-start | bytes 294920 | tf_op jit(solution)/shard_map/ppermute | solution.py:574
  52.8 9.2 %collective-permute-start.14 = (f32[96,256]{1,0:T(8,128)S(1)}, f32[96,256]{1,0:T(8,128)S(1)}, u32[]{:S(2)}, u32[]{:S(2)}) collective-permute-start(f32[96,256]{1,0:T(8,128)S(1)} %add.101), channel_id=1, source_target_pairs={{0,16},{4,20},{8,24},{12,28},{16,0},{20,4},{24,8},{28,12},{1,17},{... | collective-permute-start | bytes 294920 | tf_op jit(solution)/shard_map/ppermute | solution.py:574
  53.7 8.3 %collective-permute-start.13 = (f32[96,256]{1,0:T(8,128)S(1)}, f32[96,256]{1,0:T(8,128)S(1)}, u32[]{:S(2)}, u32[]{:S(2)}) collective-permute-start(f32[96,256]{1,0:T(8,128)S(1)} %add.101), channel_id=1, source_target_pairs={{0,8},{4,12},{8,0},{12,4},{16,24},{20,28},{24,16},{28,20},{1,9},{5... | collective-permute-start | bytes 294920 | tf_op jit(solution)/shard_map/ppermute | solution.py:574
  62.1 6.1 %collective-permute-start.19 = (f32[96,256]{1,0:T(8,128)S(1)}, f32[96,256]{1,0:T(8,128)S(1)}, u32[]{:S(2)}, u32[]{:S(2)}) collective-permute-start(f32[96,256]{1,0:T(8,128)S(1)} %add_add_fusion.refs_0_), channel_id=1, source_target_pairs={{0,6},{2,4},{4,2},{6,0},{8,14},{10,12},{12,10},{14,8},{16,22},{18,... | collective-permute-start | bytes 294920 | tf_op jit(solution)/shard_map/ppermute | solution.py:587
  63.6 4.7 %collective-permute-start.18 = (f32[96,256]{1,0:T(8,128)S(1)}, f32[96,256]{1,0:T(8,128)S(1)}, u32[]{:S(2)}, u32[]{:S(2)}) collective-permute-start(f32[96,256]{1,0:T(8,128)S(1)} %add_add_fusion.refs_0_), channel_id=1, source_target_pairs={{0,4},{4,0},{8,12},{12,8},{16,20},{20,16},{24,28},{28,24},{1,5},{5... | collective-permute-start | bytes 294920 | tf_op jit(solution)/shard_map/ppermute | solution.py:574
  64.1 5.1 %collective-permute-start.17 = (f32[96,256]{1,0:T(8,128)S(1)}, f32[96,256]{1,0:T(8,128)S(1)}, u32[]{:S(2)}, u32[]{:S(2)}) collective-permute-start(f32[96,256]{1,0:T(8,128)S(1)} %add_add_fusion.refs_0_), channel_id=1, source_target_pairs={{0,2},{2,0},{1,3},{3,1},{4,6},{6,4},{5,7},{7,5},{8,10},{10,8},{9,1... | collective-permute-start | bytes 294920 | tf_op jit(solution)/shard_map/ppermute | solution.py:574
  65.6 3.6 %collective-permute-start.20 = (f32[96,256]{1,0:T(8,128)S(1)}, f32[96,256]{1,0:T(8,128)S(1)}, u32[]{:S(2)}, u32[]{:S(2)}) collective-permute-start(f32[96,256]{1,0:T(8,128)S(1)} %add_add_fusion.refs_0_), channel_id=1, source_target_pairs={{0,1},{1,0},{2,3},{3,2},{4,5},{5,4},{6,7},{7,6},{8,9},{9,8},{10,11... | collective-permute-start | bytes 294920 | tf_op jit(solution)/shard_map/ppermute | solution.py:574
  68.2 1.3 %collective-permute-start.23 = (f32[96,256]{1,0:T(8,128)S(1)}, f32[96,256]{1,0:T(8,128)S(1)}, u32[]{:S(2)}, u32[]{:S(2)}) collective-permute-start(f32[96,256]{1,0:T(8,128)S(1)} %collective-permute-done.19.refs_3_), channel_id=1, source_target_pairs={{0,1},{1,0},{2,3},{3,2},{4,5},{5,4},{6,7},{7,6},{8,9},{9,8},{10,11... | collective-permute-start | bytes 294920 | tf_op jit(solution)/shard_map/ppermute | solution.py:574
  68.3 1.3 %collective-permute-start.22 = (f32[96,256]{1,0:T(8,128)S(1)}, f32[96,256]{1,0:T(8,128)S(1)}, u32[]{:S(2)}, u32[]{:S(2)}) collective-permute-start(f32[96,256]{1,0:T(8,128)S(1)} %collective-permute-done.18.refs_2_), channel_id=1, source_target_pairs={{0,1},{1,0},{2,3},{3,2},{4,5},{5,4},{6,7},{7,6},{8,9},{9,8},{10,11... | collective-permute-start | bytes 294920 | tf_op jit(solution)/shard_map/ppermute | solution.py:574
  69.2 1.3 %collective-permute-start.21 = (f32[96,256]{1,0:T(8,128)S(1)}, f32[96,256]{1,0:T(8,128)S(1)}, u32[]{:S(2)}, u32[]{:S(2)}) collective-permute-start(f32[96,256]{1,0:T(8,128)S(1)} %collective-permute-done.17.refs_1_), channel_id=1, source_target_pairs={{0,1},{1,0},{2,3},{3,2},{4,5},{5,4},{6,7},{7,6},{8,9},{9,8},{10,11... | collective-permute-start | bytes 294920 | tf_op jit(solution)/shard_map/ppermute | solution.py:574

commit v5 on v4

--- a/solution.py
+++ b/solution.py
@@ -16,6 +16,7 @@
 LANES = 128
 LOW = 64
 FEATURES = 32
+TILE = 512 * 1024
 PAIRS = ((0, 0), (0, 1), (1, 0), (1, 1), (0, 2), (2, 0))
 VMEM = pl.BlockSpec(memory_space=pltpu.VMEM)
 SMEM = pl.BlockSpec(memory_space=pltpu.SMEM)
@@ -39,7 +40,7 @@
     return (dot(a_low, b_high, ca, cb) + dot(a_high, b_low, ca, cb)) + dot(a_high, b_high, ca, cb)
 
 
-def params(mebibytes=16):
+def params(mebibytes=12):
     return pltpu.CompilerParams(vmem_limit_bytes=mebibytes * 1024 * 1024)
 
 
@@ -123,7 +124,9 @@
     def _():
         store(b_side, 1, b_rows, b_ref)
 
-    diag_ref[...] = weight * weight * (lax.rsqrt(jnp.full_like(weight, smooth_sq)) * scale + self_term)
+    @pl.when(block == near - 1)
+    def _():
+        diag_ref[...] = weight * weight * (lax.rsqrt(jnp.full_like(weight, smooth_sq)) * scale + self_term)
 
 
 def geometry(blocks, near, vertices, corners, layers, count, scale):
@@ -143,7 +146,7 @@
             out_specs=[
                 pl.BlockSpec((None, FEATURES, count), lambda g, blk: (jnp.minimum(g, near - 1), 0, 0)),
                 pl.BlockSpec((None, FEATURES, count), lambda g, blk: (jnp.maximum(g - near + 1, 0), 0, 0)),
-                pl.BlockSpec((None, 1, count), lambda g, blk: (g, 0, 0)),
+                pl.BlockSpec((1, count), lambda g, blk: (0, 0)),
             ],
             scratch_shapes=[
                 pltpu.VMEM((tops, 3 * LANES), f32),
@@ -155,7 +158,7 @@
         out_shape=(
             jax.ShapeDtypeStruct((near, FEATURES, count), bf16),
             jax.ShapeDtypeStruct((n - near + 1, FEATURES, count), bf16),
-            jax.ShapeDtypeStruct((n, 1, count), f32),
+            jax.ShapeDtypeStruct((1, count), f32),
         ),
         compiler_params=params(),
         name="geometry",
@@ -170,9 +173,9 @@
     more = [refs.pop(0) for _ in range(extras)]
     count = densities[0].shape[1]
     half = count // 2
-    chunk = min(512, count)
     for at, (which, slot, part) in enumerate(targets):
         columns, width = refs[at].shape
+        chunk = min(TILE // width, count)
         if part is None:
             lanes = slice(None)
         else:
@@ -199,7 +202,7 @@
         in_specs=[SMEM] + [VMEM] * (len(operands) - 1),
         out_specs=[VMEM] * len(targets),
         out_shape=[jax.ShapeDtypeStruct((columns, width), kind) for width in widths],
-        compiler_params=params(20),
+        compiler_params=params(12),
         cost_estimate=SMALL,
         name="image_part",
     )(*operands)
@@ -231,76 +234,82 @@
     )(*sources, a_side)
 
 
-def own_kernel(near, mine_ref, theirs_ref, b_ref, out_ref):
-    columns, count = out_ref.shape
-    chunk = min(512, count)
-    b = b_ref[0]
-    acc = jnp.zeros((columns, count), f32)
-    for ref in (mine_ref, theirs_ref):
+def own_kernel(near, part, diagonal, stacks, first_ref, b_ref, *refs):
+    out_ref = refs[-1]
+    columns, width = out_ref.shape
+    count = b_ref.shape[2]
+    chunk = min(TILE // width, count)
+    place = first_ref[0] if part == 0 else 1 - first_ref[0]
+    b = b_ref[0, :, pl.ds(pl.multiple_of(place * width, width), width)]
+    acc = refs[stacks][...] if len(refs) > stacks + 1 else jnp.zeros((columns, width), f32)
+    for at, ref in enumerate(refs[:stacks]):
         for source in range(near):
             side = near * columns + source * FEATURES
             for begin in range(0, count, chunk):
                 lanes = slice(begin, begin + chunk)
                 tile = lax.rsqrt(dot(ref[side : side + FEATURES, lanes], b, 0, 0))
-                if ref is mine_ref and source == 0:
+                if diagonal and at == 0 and source == 0:
                     rows = begin + lax.broadcasted_iota(jnp.int32, tile.shape, 0)
-                    cols = lax.broadcasted_iota(jnp.int32, tile.shape, 1)
+                    cols = place * width + lax.broadcasted_iota(jnp.int32, tile.shape, 1)
                     tile = jnp.where(rows == cols, 0.0, tile)
                 acc = acc + dot(ref[source * columns : (source + 1) * columns, lanes], tile.astype(bf16), 1, 0)
     out_ref[...] = acc
 
 
-def own_image(mine, theirs, b_side, near):
-    rows, count = mine.shape
+def own_image(part, first, stacks, b_side, near, diagonal, start=()):
+    rows, count = stacks[0].shape
     columns = rows // near - FEATURES
-    return pl.pallas_call(
-        functools.partial(own_kernel, near),
-        in_specs=[VMEM] * 3,
+    operands = [b_side, *stacks, *start]
+    return pl.pallas_call(
+        functools.partial(own_kernel, near, part, diagonal, len(stacks)),
+        in_specs=[SMEM] + [VMEM] * len(operands),
         out_specs=VMEM,
-        out_shape=jax.ShapeDtypeStruct((columns, count), f32),
-        compiler_params=params(20),
+        out_shape=jax.ShapeDtypeStruct((columns, count // 2), f32),
+        compiler_params=params(12),
         cost_estimate=SMALL,
         name="own_image",
-    )(mine, theirs, b_side)
-
-
-def combine_kernel(part, first_ref, own_ref, *refs):
-    fars, (smooth_ref, low_ref) = refs[:-2], refs[-2:]
-    width = smooth_ref.shape[1]
-    place = first_ref[0] if part == 0 else 1 - first_ref[0]
-    lanes = pl.ds(pl.multiple_of(place * width, width), width)
-    smooth = own_ref[:, lanes]
-    for far in fars:
-        smooth = smooth + far[...].astype(f32)
-    smooth_ref[...] = smooth
-    low_ref[...] = smooth.astype(bf16)
-
-
-def combine(part, first, own, fars):
-    columns, count = own.shape
-    return pl.pallas_call(
-        functools.partial(combine_kernel, part),
-        in_specs=[SMEM] + [VMEM] * (1 + len(fars)),
+    )(first, *operands)
+
+
+def add_parts(refs):
+    total = refs[0][...].astype(f32)
+    for ref in refs[1:]:
+        total = total + ref[...].astype(f32)
+    return total
+
+
+def combine_kernel(*refs):
+    smooth = add_parts(refs[:-2])
+    refs[-2][...] = smooth
+    refs[-1][...] = smooth.astype(bf16)
+
+
+def combine(parts):
+    return pl.pallas_call(
+        combine_kernel,
+        in_specs=[VMEM] * len(parts),
         out_specs=[VMEM] * 2,
-        out_shape=[jax.ShapeDtypeStruct((columns, count // 2), kind) for kind in (f32, bf16)],
+        out_shape=[jax.ShapeDtypeStruct(parts[0].shape, kind) for kind in (f32, bf16)],
         compiler_params=params(),
         cost_estimate=SMALL,
         name="combine",
-    )(first, own, *fars)
-
-
-def full_image(first_ref, diag_ref, current_ref, smooth_refs, image_ref):
-    half = smooth_refs[0].shape[1]
-    for place, smooth in zip((first_ref[0], 1 - first_ref[0]), smooth_refs):
+    )(*parts)
+
+
+def full_image(first_ref, diag_ref, current_ref, smooths, image_ref):
+    half = smooths[0].shape[1]
+    for place, smooth in zip((first_ref[0], 1 - first_ref[0]), smooths):
         lanes = pl.ds(pl.multiple_of(place * half, half), half)
         fixed = diag_ref[:, lanes].astype(bf16).astype(f32) * current_ref[:, lanes].astype(bf16).astype(f32)
-        image_ref[:, lanes] = smooth[...] + fixed
-
-
-def gram_kernel(ranks, first_ref, diag_ref, first_half, second_half, *refs):
-    currents, (block, image) = refs[:ranks], refs[ranks:]
+        image_ref[:, lanes] = smooth + fixed
+
+
+def gram_kernel(ranks, first_ref, diag_ref, first_half, *refs):
+    currents, parts, (block, image, low) = refs[:ranks], refs[ranks:-3], refs[-3:]
     columns = currents[0].shape[0]
-    full_image(first_ref, diag_ref, currents[0], (first_half, second_half), image)
+    second_half = add_parts(parts)
+    low[...] = second_half.astype(bf16)
+    full_image(first_ref, diag_ref, currents[0], (first_half[...], second_half), image)
     for rank in range(ranks):
         current = currents[rank][...]
         block[rank, :columns] = close_dot(image[...], current, 1, 1)
@@ -308,24 +317,25 @@
     block[0, 2 * columns :] = close_dot(image[...], image[...], 1, 1)
 
 
-def gram_sums(first, diag, smooths, currents):
+def gram_sums(first, diag, smooth, parts, currents):
     ranks = len(currents)
     columns, count = currents[0].shape
     return pl.pallas_call(
         functools.partial(gram_kernel, ranks),
-        in_specs=[SMEM] + [VMEM] * (ranks + 3),
-        out_specs=[VMEM] * 2,
+        in_specs=[SMEM] + [VMEM] * (ranks + len(parts) + 2),
+        out_specs=[VMEM] * 3,
         out_shape=(
             jax.ShapeDtypeStruct((ranks, 3 * columns, columns), f32),
             jax.ShapeDtypeStruct((columns, count), f32),
+            jax.ShapeDtypeStruct((columns, count // 2), bf16),
         ),
         compiler_params=params(),
         cost_estimate=SMALL,
         name="gram",
-    )(first, diag, *smooths, *currents)
-
-
-def cross_kernel(ranks, place_ref, core_ref, block_ref, image_ref, diag_ref, *refs):
+    )(first, diag, smooth, *currents, *parts)
+
+
+def cross_kernel(ranks, place_ref, cut_ref, block_ref, image_ref, diag_ref, *refs):
     currents, gots = refs[: ranks - 1], refs[ranks - 1 : 2 * ranks - 2]
     keep_ref, give_ref, sums, block = refs[2 * ranks - 2 :]
     columns, count = image_ref.shape
@@ -340,12 +350,13 @@
     for place in range(ranks):
         rank = jnp.bitwise_xor(place_ref[0], place)
         sums[:, place * columns : (place + 1) * columns] = block[rank]
-    rows = keep_ref.shape[0]
-    keep_ref[...] = sums[pl.ds(pl.multiple_of(core_ref[0] * rows, rows), rows), :]
-    give_ref[...] = sums[pl.ds(pl.multiple_of((1 - core_ref[0]) * rows, rows), rows), :]
-
-
-def cross_sums(places, core, blocks, image, diag, currents, gots):
+    rows = keep_ref.shape[0] // 2
+    for at, ref in enumerate((keep_ref, keep_ref, give_ref, give_ref)):
+        begin = pl.multiple_of(cut_ref[at] * rows, rows)
+        ref[at % 2 * rows : (at % 2 + 1) * rows, :] = sums[pl.ds(begin, rows), :]
+
+
+def cross_sums(places, cuts, blocks, image, diag, currents, gots):
     ranks = len(currents)
     columns, count = image.shape
     total = ranks * columns
@@ -362,27 +373,7 @@
         compiler_params=params(),
         cost_estimate=SMALL,
         name="cross",
-    )(places, core, blocks, image, diag, *currents[1:], *gots)
-
-
-def shares_kernel(place_ref, keep_ref, got_ref, *shares):
-    size = shares[0].shape[0]
-    for at, share in enumerate(shares):
-        rows = pl.ds(pl.multiple_of(place_ref[at] * size, size), size)
-        share[...] = keep_ref[rows, :] + got_ref[rows, :]
-
-
-def cut(places, keep, got):
-    rows, lanes = keep.shape
-    cuts = places.shape[0]
-    return pl.pallas_call(
-        shares_kernel,
-        in_specs=[SMEM, VMEM, VMEM],
-        out_specs=[VMEM] * cuts,
-        out_shape=[jax.ShapeDtypeStruct((rows // cuts, lanes), f32)] * cuts,
-        compiler_params=params(),
-        name="shares",
-    )(places, keep, got)
+    )(places, cuts, blocks, image, diag, *currents[1:], *gots)
 
 
 def reciprocal(value):
@@ -591,21 +582,16 @@
     return jnp.stack(values).astype(jnp.int32)
 
 
-def all_sum(keep, give, beside, ranks, tris, tri, rank, core):
-    low = tri & 1
-    value, give = cut(indices(low, 1 - low), keep, swap(give, "split", 1))
+def all_sum(keep, give, beside, ranks, tris):
+    value = keep + swap(give, "split", 1)
+    value, give = jnp.split(value, 2)
     value = value + swap(give, "tri", 1)
     parts = [swap(value, "tri", 2 * far) for far in range(1, tris // 2)]
     parts, beside = lax.optimization_barrier((parts, beside))
     value = sum(parts, value)
     shares = [value] + [pair_swap(value, bits, ranks) for bits in range(1, 2 * ranks)]
     shares += [swap(share, "split", 1) for share in shares]
-    places = [
-        (rank ^ (bits % ranks)) * 4 + (core ^ other) * 2 + (low ^ (bits // ranks))
-        for other in range(2)
-        for bits in range(2 * ranks)
-    ]
-    return shares, indices(*places), beside
+    return shares, beside
 
 
 def body(residual, attach, vertices, corners, layers):
@@ -624,14 +610,25 @@
 
     own_blocks = [(tri ^ (near * far)) * cores + core for far in range(groups)]
     near_blocks = [(tri ^ bits) * cores + core for bits in range(1, near)]
-    vertices, packed = lax.optimization_barrier((vertices, packed))
     blocks = indices(*reversed(near_blocks), *own_blocks)
+    half_place = half_of(rank ^ 1, rank) if ranks > 1 else jnp.int32(0)
+    first = indices(half_place)
+    places = indices(*[rank ^ bits for bits in range(ranks)])
+    low = tri & 1
+    cuts = indices(2 * core + low, 2 * core + 1 - low, 2 - 2 * core + low, 3 - 2 * core - low)
+    share_places = indices(
+        *[
+            (rank ^ (bits % ranks)) * 4 + (core ^ other) * 2 + (low ^ (bits // ranks))
+            for other in range(2)
+            for bits in range(2 * ranks)
+        ]
+    )
+    vertices, packed, blocks, first, places, cuts, share_places = lax.optimization_barrier(
+        (vertices, packed, blocks, first, places, cuts, share_places)
+    )
     a_side, b_side, diag = geometry(blocks, near, vertices, corners, layers, count, scale)
-    diag = diag[near - 1]
     slots = list(reversed(range(near)))
     sides = [a_side, b_side, swap(b_side, "split", 1)]
-    half_place = half_of(rank ^ 1, rank) if ranks > 1 else jnp.int32(0)
-    first = indices(half_place)
 
     def part(which, targets, starts=None, **more):
         return image_part(
@@ -665,12 +662,15 @@
         sources, _ = lax.optimization_barrier((sources, far_sum[0]))
     mine = stack_rows(sources, a_side, near)
     theirs = swap(mine, "split", 1)
-    theirs, _ = lax.optimization_barrier((theirs, far_sum))
-    own = own_image(mine, theirs, b_side, near)
-
-    places = indices(*[rank ^ bits for bits in range(ranks)])
-    smooth_first, low_first = combine(0, first, own, arrived[0])
-    smooth_second, low_second = combine(1, first, own, arrived[1])
+    after, _ = lax.optimization_barrier((first, far_sum))
+    own_first = own_image(0, after, [mine, theirs], b_side, near, True)
+    after, _ = lax.optimization_barrier((first, own_first))
+    own_second = own_image(1, after, [mine], b_side, near, True)
+    own_first, own_second = lax.optimization_barrier((own_first, own_second))
+    smooth, low_first = combine([own_first, *arrived[0]])
+    after, _ = lax.optimization_barrier((first, low_first))
+    own_second = own_image(1, after, [theirs], b_side, near, False, [own_second])
+    blocks, image, low_second = gram_sums(first, diag, smooth, [own_second, *arrived[1]], currents)
     gots, rests = [], []
     for bits in range(1, ranks):
         if bits == 1:
@@ -681,12 +681,11 @@
             rest = jnp.where(is_first, low_second, low_first)
         gots.append(swap(give, "rhs", bits))
         rests.append(rest)
-    blocks, image = gram_sums(first, diag, [smooth_first, smooth_second], currents)
-    keep, give = cross_sums(places, indices(core), blocks, image, diag, currents, gots)
+    keep, give = cross_sums(places, cuts, blocks, image, diag, currents, gots)
     rests, _ = lax.optimization_barrier((rests, gots))
     rests = [swap(rest, "rhs", bits) for bits, rest in enumerate(rests, 1)]
     beside = other_images(places, diag, currents, gots, rests)
-    shares, share_places, beside = all_sum(keep, give, beside, ranks, tris, tri, rank, core)
+    shares, beside = all_sum(keep, give, beside, ranks, tris)
     step, turn = solve(places, share_places, shares, columns)
     return finish(places, step, turn, currents, [image, *beside])
 

time: 84.6 us -> 82.5 us (0.975)
  waiting for transfers between devices: 19 us -> 17.8 us
    ppermute x23, waiting for transfers between devices: 16.5 us -> 15.3 us  [swap(): return lax.ppermute(value, axis, [(at, at ^ bits) for at in range(size)])]
  transfers between devices with their start and end apart: 24 -> 24, of which waited for: 15 -> 15; matrix products, arithmetic and copies ran while one was open for 0% -> 0% of each run, Pallas kernels for 26% -> 27%
where the time goes in v5:
time: 82.5 us; the launch traced here: 82.3 us
  Pallas kernels  38.3 us (46%)
  starting transfers between devices  23.5 us (28%)
  waiting for transfers between devices  17.8 us (22%)
  other arithmetic  1.45 us (2%)
  between operations  1.08 us (1%)
    ppermute x23, starting transfers between devices, swap(): return lax.ppermute(value, axis, [(at, at ^ bits) for at in range(size)])  21.8 us
    ppermute x23, waiting for transfers between devices, swap(): return lax.ppermute(value, axis, [(at, at ^ bits) for at in range(size)])  15.3 us
    pallas_call x1, Pallas kernels, solve(): pl.pallas_call(functools.partial(solve_kernel, columns, 32), in_specs=[SM...  11.5 us
    pallas_call x8, Pallas kernels, image_part(): pl.pallas_call(functools.partial(image_kernel, range(len(densities)), slo...  8.5 us
    pallas_call x3, Pallas kernels, own_image(): pl.pallas_call(functools.partial(own_kernel, near, part, diagonal, len(st...  8.05 us
    pallas_call x1, Pallas kernels, geometry(): pl.pallas_call(functools.partial(geometry_kernel, scale, near), grid_spec...  4.88 us
    ppermute x1, waiting for transfers between devices, pair_swap(): return lax.ppermute(value, ('tri', 'rhs'), perm)  2.5 us
    pallas_call x1, Pallas kernels, finish(): pl.pallas_call(functools.partial(finish_kernel, ranks, chunks), in_specs=...  2.27 us
  transfers between devices with their start and end apart: 24, of which 15 were waited for; matrix products, arithmetic and copies ran while one was open for 0% of the time, Pallas kernels for 27%

profile of v5, /device:TPU:0, one launch (start us, length us, event | category | flops | bytes accessed | tf_op | source)
XLA Modules:
  0.0 82.3 jit_solution(5349743840282472570)
XLA Ops:
  0.7 1.2 %fusion = (bf16[128,1024]{1,0:T(8,128)(2,1)S(1)}, f32[128,1024]{1,0:T(8,128)S(1)}) fusion(f32[128,1024]{1,0:T(8,128)} %param.5, s32[1024]{0:T(1024)S(1)} %iota_add_fusion, s32[128]{0:T(128)} %param.6), kind=kLoop, calls=%fused_computation.6 | loop fusion | flops 524288 | bytes 1315328 | tf_op jit(solution)/shard_map/convert_element_type | solution.py:607
  1.9 3.0 %collective-permute-start.2 = (f32[128,1024]{1,0:T(8,128)S(1)}, f32[128,1024]{1,0:T(8,128)S(1)}, u32[]{:S(2)}, u32[]{:S(2)}) collective-permute-start(f32[128,1024]{1,0:T(8,128)S(1)} %get-tuple-element.90.refs_0_), channel_id=1, source_target_pairs={{0,2},{2,0},{1,3},{3,1},{4,6},{6,4},{5,7},{7,5},{8,10},{10,8},{9,1... | collective-permute-start | bytes 1572872 | tf_op jit(solution)/shard_map/ppermute | solution.py:565
  5.0 1.5 %collective-permute-start.4 = (bf16[128,1024]{1,0:T(8,128)(2,1)S(1)}, bf16[128,1024]{1,0:T(8,128)(2,1)S(1)}, u32[]{:S(2)}, u32[]{:S(2)}) collective-permute-start(bf16[128,1024]{1,0:T(8,128)(2,1)S(1)} %get-tuple-element.83.refs_0_), channel_id=1, source_target_pairs={{0,4},{4,0},{8,12},{12,8},{16,20},{20,16},{24,28},{28,24},{1,5},{5... | collective-permute-start | bytes 786440 | tf_op jit(solution)/shard_map/ppermute | solution.py:565
  6.4 1.6 %collective-permute-start.3 = (bf16[128,1024]{1,0:T(8,128)(2,1)S(1)}, bf16[128,1024]{1,0:T(8,128)(2,1)S(1)}, u32[]{:S(2)}, u32[]{:S(2)}) collective-permute-start(bf16[128,1024]{1,0:T(8,128)(2,1)S(1)} %get-tuple-element.83.refs_0_), channel_id=1, source_target_pairs={{0,8},{4,12},{8,0},{12,4},{16,24},{20,28},{24,16},{28,20},{1,9},{5... | collective-permute-start | bytes 786440 | tf_op jit(solution)/shard_map/ppermute | solution.py:565
  8.0 0.4 collective-permute-start
  8.8 4.9 %geometry.1 = (bf16[4,32,1024]{2,1,0:T(8,128)(2,1)S(1)}, bf16[2,32,1024]{2,1,0:T(8,128)(2,1)S(1)}, f32[1,1024]{1,0:T(1,128)S(1)}) custom-call(s32[5]{0:T(128)S(1)} %stack.80.blocks_ref, f32[3,8192]{1,0:T(4,128)S(1)} %copy-done.1, s32[3,16384]{1,0:T(4,128)S(1)} %copy-done, s32[1,16384]{1,0:T(1,128)S(1)} %bitcast.21), custom_call_target="tpu_custom_call" | custom-call | tf_op jit(solution)/shard_map/geometry/pallas_call | solution.py:136
  13.7 1.1 %image_part.8.refs_5_ = f32[128,1024]{1,0:T(8,128)S(1)} custom-call(s32[1]{0:T(128)} %bitcast.5.first_ref, bf16[128,1024]{1,0:T(8,128)(2,1)S(1)} %get-tuple-element.83.refs_0_, bf16[4,32,1024]{2,1,0:T(8,128)(2,1)S(1)} %get-tuple-element.80.refs_1_.refs_4_, bf16[2,32,1024]{2,1,0:T(8,128)(2,1)S(1)} %get-tuple-element.81.refs_2_.b_ref), custom_call_target="tpu_custom_call" | custom-call | flops 1024 | bytes 1024 | tf_op jit(solution)/shard_map/image_part/pallas_call | solution.py:200
  14.8 0.3 collective-permute-done.1.refs_3_
  15.1 1.0 %image_part.9.refs_4_ = f32[128,1024]{1,0:T(8,128)S(1)} custom-call(s32[1]{0:T(128)} %bitcast.5.first_ref, bf16[128,1024]{1,0:T(8,128)(2,1)S(1)} %get-tuple-element.83.refs_0_, bf16[4,32,1024]{2,1,0:T(8,128)(2,1)S(1)} %get-tuple-element.80.refs_1_.refs_4_, bf16[2,32,1024]{2,1,0:T(8,128)(2,1)S(1)} %get-tuple-element.81.refs_2_.b_ref, ...), custom_call_target="tpu_custom_call" | custom-call | flops 1024 | bytes 1024 | tf_op jit(solution)/shard_map/image_part/pallas_call | solution.py:200
  16.1 2.0 %image_part.10 = (f32[128,1024]{1,0:T(8,128)S(1)}, f32[128,1024]{1,0:T(8,128)S(1)}) custom-call(s32[1]{0:T(128)} %bitcast.5.first_ref, bf16[128,1024]{1,0:T(8,128)(2,1)S(1)} %collective-permute-done.4.refs_0_.refs_1_, bf16[4,32,1024]{2,1,0:T(8,128)(2,1)S(1)} %get-tuple-element.80.refs_1_.refs_4_, bf16[2,32,1024]{2,1,0:T(8,128)(2,1)S(1)} %get-tuple-element.81.refs_2_.b_ref, ...), custom_call_target="tpu_custom_call" | custom-call | flops 1024 | bytes 1024 | tf_op jit(solution)/shard_map/image_part/pallas_call | solution.py:200
  18.1 1.9 %image_part.11 = (f32[128,1024]{1,0:T(8,128)S(1)}, f32[128,1024]{1,0:T(8,128)S(1)}) custom-call(s32[1]{0:T(128)} %bitcast.5.first_ref, bf16[128,1024]{1,0:T(8,128)(2,1)S(1)} %collective-permute-done.3.refs_0_.refs_2_, bf16[4,32,1024]{2,1,0:T(8,128)(2,1)S(1)} %get-tuple-element.80.refs_1_.refs_4_, bf16[2,32,1024]{2,1,0:T(8,128)(2,1)S(1)} %get-tuple-element.81.refs_2_.b_ref, ...), custom_call_target="tpu_custom_call" | custom-call | flops 1024 | bytes 1024 | tf_op jit(solution)/shard_map/image_part/pallas_call | solution.py:200
  20.1 0.6 image_part.12
  20.7 0.3 collective-permute-start.5
  21.0 0.6 image_part.13
  21.7 0.5 collective-permute-done.5.refs_4_
  22.1 0.6 image_part.14
  22.9 0.3 collective-permute-start.7
  23.2 0.3 collective-permute-start.6
  23.4 2.6 %collective-permute-start.8 = (bf16[128,512]{1,0:T(8,128)(2,1)S(1)}, bf16[128,512]{1,0:T(8,128)(2,1)S(1)}, u32[]{:S(2)}, u32[]{:S(2)}) collective-permute-start(bf16[128,512]{1,0:T(8,128)(2,1)S(1)} %image_part.14), channel_id=1, source_target_pairs={{0,16},{4,20},{8,24},{12,28},{16,0},{20,4},{24,8},{28,12},{1,17},{... | collective-permute-start | bytes 393224 | tf_op jit(solution)/shard_map/ppermute | solution.py:565
  26.2 0.6 image_part.15
  26.8 2.7 %collective-permute-start.9 = (bf16[128,512]{1,0:T(8,128)(2,1)S(1)}, bf16[128,512]{1,0:T(8,128)(2,1)S(1)}, u32[]{:S(2)}, u32[]{:S(2)}) collective-permute-start(bf16[128,512]{1,0:T(8,128)(2,1)S(1)} %image_part.15), channel_id=1, source_target_pairs={{0,16},{4,20},{8,24},{12,28},{16,0},{20,4},{24,8},{28,12},{1,17},{... | collective-permute-start | bytes 393224 | tf_op jit(solution)/shard_map/ppermute | solution.py:565
  29.5 3.8 %own_image.3.refs_0_ = f32[128,512]{1,0:T(8,128)S(1)} custom-call(s32[1]{0:T(128)} %bitcast.5.first_ref, bf16[2,32,1024]{2,1,0:T(8,128)(2,1)S(1)} %get-tuple-element.81.refs_2_.b_ref, bf16[640,1024]{1,0:T(8,128)(2,1)S(1)} %stack_rows.1.refs_0_, bf16[640,1024]{1,0:T(8,128)(2,1)S(1)} %collective-permute-done.7.refs_1_.refs_0_), custom_call_target="tpu_custom_call" | custom-call | flops 1024 | bytes 1024 | tf_op jit(solution)/shard_map/own_image/pallas_call | solution.py:263
  33.3 2.0 %own_image.4.refs_1_ = f32[128,512]{1,0:T(8,128)S(1)} custom-call(s32[1]{0:T(128)} %bitcast.5.first_ref, bf16[2,32,1024]{2,1,0:T(8,128)(2,1)S(1)} %get-tuple-element.81.refs_2_.b_ref, bf16[640,1024]{1,0:T(8,128)(2,1)S(1)} %stack_rows.1.refs_0_), custom_call_target="tpu_custom_call" | custom-call | flops 1024 | bytes 1024 | tf_op jit(solution)/shard_map/own_image/pallas_call | solution.py:263
  35.3 1.0 %collective-permute-done.8.refs_1_ = bf16[128,512]{1,0:T(8,128)(2,1)S(1)} collective-permute-done((bf16[128,512]{1,0:T(8,128)(2,1)S(1)}, bf16[128,512]{1,0:T(8,128)(2,1)S(1)}, u32[]{:S(2)}, u32[]{:S(2)}) %collective-permute-start.8) | collective-permute-done | bytes 131104 | tf_op jit(solution)/shard_map/ppermute | solution.py:565
  36.5 2.2 %own_image.5.refs_2_ = f32[128,512]{1,0:T(8,128)S(1)} custom-call(s32[1]{0:T(128)} %bitcast.5.first_ref, bf16[2,32,1024]{2,1,0:T(8,128)(2,1)S(1)} %get-tuple-element.81.refs_2_.b_ref, bf16[640,1024]{1,0:T(8,128)(2,1)S(1)} %collective-permute-done.7.refs_1_.refs_0_, f32[128,512]{1,0:T(8,128)S(1)} %own_image.4.refs_1_), custom_call_target="tpu_custom_call" | custom-call | flops 1024 | bytes 1024 | tf_op jit(solution)/shard_map/own_image/pallas_call | solution.py:263
  38.8 1.4 %gram.1 = (f32[2,384,128]{2,1,0:T(8,128)S(1)}, f32[128,1024]{1,0:T(8,128)S(1)}, bf16[128,512]{1,0:T(8,128)(2,1)S(1)}) custom-call(s32[1]{0:T(128)} %bitcast.5.first_ref, f32[1,1024]{1,0:T(1,128)S(1)} %get-tuple-element.61.diag_ref, f32[128,512]{1,0:T(8,128)S(1)} %get-tuple-element.89.first_half, f32[128,1024]{1,0:T(8,128)S(1)} %get-tuple-element.90.refs_0_, ...), custom_call_target="tpu_custom_call" | custom-call | flops 1024 | bytes 1024 | tf_op jit(solution)/shard_map/gram/pallas_call | solution.py:323
  40.1 1.2 %collective-permute-done.10.refs_1_ = bf16[128,512]{1,0:T(8,128)(2,1)S(1)} collective-permute-done((bf16[128,512]{1,0:T(8,128)(2,1)S(1)}, bf16[128,512]{1,0:T(8,128)(2,1)S(1)}, u32[]{:S(2)}, u32[]{:S(2)}) %collective-permute-start.10) | collective-permute-done | bytes 131104 | tf_op jit(solution)/shard_map/ppermute | solution.py:565
  41.4 0.9 %cross.1 = (f32[192,256]{1,0:T(8,128)S(1)}, f32[192,256]{1,0:T(8,128)S(1)}) custom-call(s32[2]{0:T(128)S(1)} %pad_add_fusion.place_ref, s32[4]{0:T(128)S(1)} %pad_add_fusion.1.cut_ref, f32[2,384,128]{2,1,0:T(8,128)S(1)} %get-tuple-element.95.block_ref, f32[128,1024]{1,0:T(8,128)S(1)} %get-tuple-element.96.image_ref.refs_2_, ...), custom_call_target="tpu_custom_call" | custom-call | flops 1024 | bytes 1024 | tf_op jit(solution)/shard_map/cross/pallas_call | solution.py:364
  42.4 1.4 %collective-permute-done.11 = f32[192,256]{1,0:T(8,128)S(1)} collective-permute-done((f32[192,256]{1,0:T(8,128)S(1)}, f32[192,256]{1,0:T(8,128)S(1)}, u32[]{:S(2)}, u32[]{:S(2)}) %collective-permute-start.11) | collective-permute-done | bytes 196640 | tf_op jit(solution)/shard_map/ppermute | solution.py:565
  43.8 1.6 %collective-permute-start.12 = (f32[96,256]{1,0:T(8,128)S(1)}, f32[96,256]{1,0:T(8,128)S(1)}, u32[]{:S(2)}, u32[]{:S(2)}) collective-permute-start(f32[96,256]{1,0:T(8,128)S(1)} %split.9), channel_id=1, source_target_pairs={{0,4},{4,0},{8,12},{12,8},{16,20},{20,16},{24,28},{28,24},{1,5},{5... | collective-permute-start | bytes 294920 | tf_op jit(solution)/shard_map/ppermute | solution.py:565
  45.4 0.7 collective-permute-start.16
  46.1 2.7 %collective-permute-done.12 = f32[96,256]{1,0:T(8,128)S(1)} collective-permute-done((f32[96,256]{1,0:T(8,128)S(1)}, f32[96,256]{1,0:T(8,128)S(1)}, u32[]{:S(2)}, u32[]{:S(2)}) %collective-permute-start.12) | collective-permute-done | bytes 98336 | tf_op jit(solution)/shard_map/ppermute | solution.py:565
  48.8 3.3 %collective-permute-start.15 = (f32[96,256]{1,0:T(8,128)S(1)}, f32[96,256]{1,0:T(8,128)S(1)}, u32[]{:S(2)}, u32[]{:S(2)}) collective-permute-start(f32[96,256]{1,0:T(8,128)S(1)} %slice_add_fusion), channel_id=1, source_target_pairs={{0,24},{4,28},{8,16},{12,20},{16,8},{20,12},{24,0},{28,4},{1,25},{... | collective-permute-start | bytes 294920 | tf_op jit(solution)/shard_map/ppermute | solution.py:565
  52.1 1.1 %collective-permute-start.13 = (f32[96,256]{1,0:T(8,128)S(1)}, f32[96,256]{1,0:T(8,128)S(1)}, u32[]{:S(2)}, u32[]{:S(2)}) collective-permute-start(f32[96,256]{1,0:T(8,128)S(1)} %slice_add_fusion), channel_id=1, source_target_pairs={{0,8},{4,12},{8,0},{12,4},{16,24},{20,28},{24,16},{28,20},{1,9},{5... | collective-permute-start | bytes 294920 | tf_op jit(solution)/shard_map/ppermute | solution.py:565
  53.2 0.6 other_images.1.refs_3_
  53.9 2.0 %collective-permute-done.15 = f32[96,256]{1,0:T(8,128)S(1)} collective-permute-done((f32[96,256]{1,0:T(8,128)S(1)}, f32[96,256]{1,0:T(8,128)S(1)}, u32[]{:S(2)}, u32[]{:S(2)}) %collective-permute-start.15) | collective-permute-done | bytes 98336 | tf_op jit(solution)/shard_map/ppermute | solution.py:565
  55.9 4.0 %collective-permute-done.14 = f32[96,256]{1,0:T(8,128)S(1)} collective-permute-done((f32[96,256]{1,0:T(8,128)S(1)}, f32[96,256]{1,0:T(8,128)S(1)}, u32[]{:S(2)}, u32[]{:S(2)}) %collective-permute-start.14) | collective-permute-done | bytes 98336 | tf_op jit(solution)/shard_map/ppermute | solution.py:565
  59.9 1.7 %collective-permute-start.19 = (f32[96,256]{1,0:T(8,128)S(1)}, f32[96,256]{1,0:T(8,128)S(1)}, u32[]{:S(2)}, u32[]{:S(2)}) collective-permute-start(f32[96,256]{1,0:T(8,128)S(1)} %add_add_fusion.refs_0_), channel_id=1, source_target_pairs={{0,6},{2,4},{4,2},{6,0},{8,14},{10,12},{12,10},{14,8},{16,22},{18,... | collective-permute-start | bytes 294920 | tf_op jit(solution)/shard_map/ppermute | solution.py:578
  61.6 0.5 collective-permute-start.18
  62.1 1.4 %collective-permute-start.17 = (f32[96,256]{1,0:T(8,128)S(1)}, f32[96,256]{1,0:T(8,128)S(1)}, u32[]{:S(2)}, u32[]{:S(2)}) collective-permute-start(f32[96,256]{1,0:T(8,128)S(1)} %add_add_fusion.refs_0_), channel_id=1, source_target_pairs={{0,2},{2,0},{1,3},{3,1},{4,6},{6,4},{5,7},{7,5},{8,10},{10,8},{9,1... | collective-permute-start | bytes 294920 | tf_op jit(solution)/shard_map/ppermute | solution.py:565
  63.5 2.5 %collective-permute-done.19.refs_3_ = f32[96,256]{1,0:T(8,128)S(1)} collective-permute-done((f32[96,256]{1,0:T(8,128)S(1)}, f32[96,256]{1,0:T(8,128)S(1)}, u32[]{:S(2)}, u32[]{:S(2)}) %collective-permute-start.19) | collective-permute-done | bytes 98336 | tf_op jit(solution)/shard_map/ppermute | solution.py:578
  66.2 0.3 collective-permute-start.22
  66.5 0.5 collective-permute-done.17.refs_1_
  67.0 0.3 collective-permute-done.23.refs_7_
  67.3 0.2 collective-permute-done.22.refs_6_
  67.5 0.8 collective-permute-done.21.refs_5_
  68.3 11.5 %solve.1 = (f32[128,256]{1,0:T(8,128)S(1)}, f32[128,256]{1,0:T(8,128)S(1)}) custom-call(s32[2]{0:T(128)S(1)} %pad_add_fusion.place_ref, s32[8]{0:T(128)S(1)} %stack.99.share_ref, f32[96,256]{1,0:T(8,128)S(1)} %add_add_fusion.refs_0_, f32[96,256]{1,0:T(8,128)S(1)} %collective-permute-done.17.refs_1_, f32[96,256]{1,0:T(8,128)S(1)} %collective-permute-done.18.refs_2_, ...), custom_call_target="tpu_custom_call" | custom-call | tf_op jit(solution)/shard_map/solve/pallas_call | solution.py:467
  79.9 2.3 %finish.1 = (f32[128,1024]{1,0:T(8,128)}, f32[128,1024]{1,0:T(8,128)}, f32[128,1024]{1,0:T(8,128)}) custom-call(s32[2]{0:T(128)S(1)} %pad_add_fusion.place_ref, f32[128,256]{1,0:T(8,128)S(1)} %get-tuple-element.104.step_ref, f32[128,256]{1,0:T(8,128)S(1)} %get-tuple-element.105.turn_ref, f32[128,1024]{1,0:T(8,128)S(1)} %get-tuple-element.90.refs_0_, ...), custom_call_target="tpu_custom_call" | custom-call | flops 1024 | bytes 1024 | tf_op jit(solution)/shard_map/finish/pallas_call | solution.py:549
  (35 shorter events, 1.3 us)
Async XLA Ops:
  0.6 8.1 %copy-start.1 = (f32[3,8192]{1,0:T(4,128)S(1)}, f32[3,8192]{1,0:T(4,128)}, u32[]{:S(2)}) copy-start(f32[3,8192]{1,0:T(4,128)} %vertices_ref) | copy-start | bytes 294916
  0.6 8.1 %copy-start.2 = (s32[16384]{0:T(1024)S(1)}, s32[16384]{0:T(1024)}, u32[]{:S(2)}) copy-start(s32[16384]{0:T(1024)} %param.9) | copy-start | bytes 196612
  0.7 8.1 %copy-start = (s32[3,16384]{1,0:T(4,128)S(1)}, s32[3,16384]{1,0:T(4,128)}, u32[]{:S(2)}) copy-start(s32[3,16384]{1,0:T(4,128)} %corners_ref.1) | copy-start | bytes 589828
  1.9 18.2 %collective-permute-start.2 = (f32[128,1024]{1,0:T(8,128)S(1)}, f32[128,1024]{1,0:T(8,128)S(1)}, u32[]{:S(2)}, u32[]{:S(2)}) collective-permute-start(f32[128,1024]{1,0:T(8,128)S(1)} %get-tuple-element.90.refs_0_), channel_id=1, source_target_pairs={{0,2},{2,0},{1,3},{3,1},{4,6},{6,4},{5,7},{7,5},{8,10},{10,8},{9,1... | collective-permute-start | bytes 1572872 | tf_op jit(solution)/shard_map/ppermute | solution.py:565
  5.0 11.2 %collective-permute-start.4 = (bf16[128,1024]{1,0:T(8,128)(2,1)S(1)}, bf16[128,1024]{1,0:T(8,128)(2,1)S(1)}, u32[]{:S(2)}, u32[]{:S(2)}) collective-permute-start(bf16[128,1024]{1,0:T(8,128)(2,1)S(1)} %get-tuple-element.83.refs_0_), channel_id=1, source_target_pairs={{0,4},{4,0},{8,12},{12,8},{16,20},{20,16},{24,28},{28,24},{1,5},{5... | collective-permute-start | bytes 786440 | tf_op jit(solution)/shard_map/ppermute | solution.py:565
  6.4 11.7 %collective-permute-start.3 = (bf16[128,1024]{1,0:T(8,128)(2,1)S(1)}, bf16[128,1024]{1,0:T(8,128)(2,1)S(1)}, u32[]{:S(2)}, u32[]{:S(2)}) collective-permute-start(bf16[128,1024]{1,0:T(8,128)(2,1)S(1)} %get-tuple-element.83.refs_0_), channel_id=1, source_target_pairs={{0,8},{4,12},{8,0},{12,4},{16,24},{20,28},{24,16},{28,20},{1,9},{5... | collective-permute-start | bytes 786440 | tf_op jit(solution)/shard_map/ppermute | solution.py:565
  8.0 12.1 %collective-permute-start = (bf16[128,1024]{1,0:T(8,128)(2,1)S(1)}, bf16[128,1024]{1,0:T(8,128)(2,1)S(1)}, u32[]{:S(2)}, u32[]{:S(2)}) collective-permute-start(bf16[128,1024]{1,0:T(8,128)(2,1)S(1)} %get-tuple-element.83.refs_0_), channel_id=1, source_target_pairs={{0,12},{4,8},{8,4},{12,0},{16,28},{20,24},{24,20},{28,16},{1,13},{... | collective-permute-start | bytes 786440 | tf_op jit(solution)/shard_map/ppermute | solution.py:565
  13.7 1.4 %collective-permute-start.1 = (bf16[2,32,1024]{2,1,0:T(8,128)(2,1)S(1)}, bf16[2,32,1024]{2,1,0:T(8,128)(2,1)S(1)}, u32[]{:S(2)}, u32[]{:S(2)}) collective-permute-start(bf16[2,32,1024]{2,1,0:T(8,128)(2,1)S(1)} %get-tuple-element.81.refs_2_.b_ref), channel_id=1, source_target_pairs={{0,1},{1,0},{2,3},{3,2},{4,5},{5,4},{6,7},{7,6},{8,9},{9,8},{10,11... | collective-permute-start | bytes 393224 | tf_op jit(solution)/shard_map/ppermute | solution.py:565
  20.7 1.4 %collective-permute-start.5 = (bf16[128,512]{1,0:T(8,128)(2,1)S(1)}, bf16[128,512]{1,0:T(8,128)(2,1)S(1)}, u32[]{:S(2)}, u32[]{:S(2)}) collective-permute-start(bf16[128,512]{1,0:T(8,128)(2,1)S(1)} %image_part.12), channel_id=1, source_target_pairs={{0,1},{1,0},{2,3},{3,2},{4,5},{5,4},{6,7},{7,6},{8,9},{9,8},{10,11... | collective-permute-start | bytes 393224 | tf_op jit(solution)/shard_map/ppermute | solution.py:565
  22.9 6.6 %collective-permute-start.7 = (bf16[640,1024]{1,0:T(8,128)(2,1)S(1)}, bf16[640,1024]{1,0:T(8,128)(2,1)S(1)}, u32[]{:S(2)}, u32[]{:S(2)}) collective-permute-start(bf16[640,1024]{1,0:T(8,128)(2,1)S(1)} %stack_rows.1.refs_0_), channel_id=1, source_target_pairs={{0,1},{1,0},{2,3},{3,2},{4,5},{5,4},{6,7},{7,6},{8,9},{9,8},{10,11... | collective-permute-start | bytes 3932168 | tf_op jit(solution)/shard_map/ppermute | solution.py:565
  23.2 3.0 %collective-permute-start.6 = (bf16[128,512]{1,0:T(8,128)(2,1)S(1)}, bf16[128,512]{1,0:T(8,128)(2,1)S(1)}, u32[]{:S(2)}, u32[]{:S(2)}) collective-permute-start(bf16[128,512]{1,0:T(8,128)(2,1)S(1)} %image_part.13), channel_id=1, source_target_pairs={{0,1},{1,0},{2,3},{3,2},{4,5},{5,4},{6,7},{7,6},{8,9},{9,8},{10,11... | collective-permute-start | bytes 393224 | tf_op jit(solution)/shard_map/ppermute | solution.py:565
  23.4 12.8 %collective-permute-start.8 = (bf16[128,512]{1,0:T(8,128)(2,1)S(1)}, bf16[128,512]{1,0:T(8,128)(2,1)S(1)}, u32[]{:S(2)}, u32[]{:S(2)}) collective-permute-start(bf16[128,512]{1,0:T(8,128)(2,1)S(1)} %image_part.14), channel_id=1, source_target_pairs={{0,16},{4,20},{8,24},{12,28},{16,0},{20,4},{24,8},{28,12},{1,17},{... | collective-permute-start | bytes 393224 | tf_op jit(solution)/shard_map/ppermute | solution.py:565
  26.8 12.0 %collective-permute-start.9 = (bf16[128,512]{1,0:T(8,128)(2,1)S(1)}, bf16[128,512]{1,0:T(8,128)(2,1)S(1)}, u32[]{:S(2)}, u32[]{:S(2)}) collective-permute-start(bf16[128,512]{1,0:T(8,128)(2,1)S(1)} %image_part.15), channel_id=1, source_target_pairs={{0,16},{4,20},{8,24},{12,28},{16,0},{20,4},{24,8},{28,12},{1,17},{... | collective-permute-start | bytes 393224 | tf_op jit(solution)/shard_map/ppermute | solution.py:565
  36.3 5.0 %collective-permute-start.10 = (bf16[128,512]{1,0:T(8,128)(2,1)S(1)}, bf16[128,512]{1,0:T(8,128)(2,1)S(1)}, u32[]{:S(2)}, u32[]{:S(2)}) collective-permute-start(bf16[128,512]{1,0:T(8,128)(2,1)S(1)} %get-tuple-element.92), channel_id=1, source_target_pairs={{0,2},{2,0},{1,3},{3,1},{4,6},{6,4},{5,7},{7,5},{8,10},{10,8},{9,1... | collective-permute-start | bytes 393224 | tf_op jit(solution)/shard_map/ppermute | solution.py:565
  42.3 1.5 %collective-permute-start.11 = (f32[192,256]{1,0:T(8,128)S(1)}, f32[192,256]{1,0:T(8,128)S(1)}, u32[]{:S(2)}, u32[]{:S(2)}) collective-permute-start(f32[192,256]{1,0:T(8,128)S(1)} %get-tuple-element.98), channel_id=1, source_target_pairs={{0,1},{1,0},{2,3},{3,2},{4,5},{5,4},{6,7},{7,6},{8,9},{9,8},{10,11... | collective-permute-start | bytes 589832 | tf_op jit(solution)/shard_map/ppermute | solution.py:565
  43.8 4.9 %collective-permute-start.12 = (f32[96,256]{1,0:T(8,128)S(1)}, f32[96,256]{1,0:T(8,128)S(1)}, u32[]{:S(2)}, u32[]{:S(2)}) collective-permute-start(f32[96,256]{1,0:T(8,128)S(1)} %split.9), channel_id=1, source_target_pairs={{0,4},{4,0},{8,12},{12,8},{16,20},{20,16},{24,28},{28,24},{1,5},{5... | collective-permute-start | bytes 294920 | tf_op jit(solution)/shard_map/ppermute | solution.py:565
  45.4 7.8 %collective-permute-start.16 = (bf16[128,512]{1,0:T(8,128)(2,1)S(1)}, bf16[128,512]{1,0:T(8,128)(2,1)S(1)}, u32[]{:S(2)}, u32[]{:S(2)}) collective-permute-start(bf16[128,512]{1,0:T(8,128)(2,1)S(1)} %get-tuple-element.100), channel_id=1, source_target_pairs={{0,2},{2,0},{1,3},{3,1},{4,6},{6,4},{5,7},{7,5},{8,10},{10,8},{9,1... | collective-permute-start | bytes 393224 | tf_op jit(solution)/shard_map/ppermute | solution.py:565
  48.8 7.1 %collective-permute-start.15 = (f32[96,256]{1,0:T(8,128)S(1)}, f32[96,256]{1,0:T(8,128)S(1)}, u32[]{:S(2)}, u32[]{:S(2)}) collective-permute-start(f32[96,256]{1,0:T(8,128)S(1)} %slice_add_fusion), channel_id=1, source_target_pairs={{0,24},{4,28},{8,16},{12,20},{16,8},{20,12},{24,0},{28,4},{1,25},{... | collective-permute-start | bytes 294920 | tf_op jit(solution)/shard_map/ppermute | solution.py:565
  52.1 7.8 %collective-permute-start.14 = (f32[96,256]{1,0:T(8,128)S(1)}, f32[96,256]{1,0:T(8,128)S(1)}, u32[]{:S(2)}, u32[]{:S(2)}) collective-permute-start(f32[96,256]{1,0:T(8,128)S(1)} %slice_add_fusion), channel_id=1, source_target_pairs={{0,16},{4,20},{8,24},{12,28},{16,0},{20,4},{24,8},{28,12},{1,17},{... | collective-permute-start | bytes 294920 | tf_op jit(solution)/shard_map/ppermute | solution.py:565
  52.1 7.8 %collective-permute-start.13 = (f32[96,256]{1,0:T(8,128)S(1)}, f32[96,256]{1,0:T(8,128)S(1)}, u32[]{:S(2)}, u32[]{:S(2)}) collective-permute-start(f32[96,256]{1,0:T(8,128)S(1)} %slice_add_fusion), channel_id=1, source_target_pairs={{0,8},{4,12},{8,0},{12,4},{16,24},{20,28},{24,16},{28,20},{1,9},{5... | collective-permute-start | bytes 294920 | tf_op jit(solution)/shard_map/ppermute | solution.py:565
  59.9 6.1 %collective-permute-start.19 = (f32[96,256]{1,0:T(8,128)S(1)}, f32[96,256]{1,0:T(8,128)S(1)}, u32[]{:S(2)}, u32[]{:S(2)}) collective-permute-start(f32[96,256]{1,0:T(8,128)S(1)} %add_add_fusion.refs_0_), channel_id=1, source_target_pairs={{0,6},{2,4},{4,2},{6,0},{8,14},{10,12},{12,10},{14,8},{16,22},{18,... | collective-permute-start | bytes 294920 | tf_op jit(solution)/shard_map/ppermute | solution.py:578
  61.6 4.6 %collective-permute-start.18 = (f32[96,256]{1,0:T(8,128)S(1)}, f32[96,256]{1,0:T(8,128)S(1)}, u32[]{:S(2)}, u32[]{:S(2)}) collective-permute-start(f32[96,256]{1,0:T(8,128)S(1)} %add_add_fusion.refs_0_), channel_id=1, source_target_pairs={{0,4},{4,0},{8,12},{12,8},{16,20},{20,16},{24,28},{28,24},{1,5},{5... | collective-permute-start | bytes 294920 | tf_op jit(solution)/shard_map/ppermute | solution.py:565
  62.1 4.9 %collective-permute-start.17 = (f32[96,256]{1,0:T(8,128)S(1)}, f32[96,256]{1,0:T(8,128)S(1)}, u32[]{:S(2)}, u32[]{:S(2)}) collective-permute-start(f32[96,256]{1,0:T(8,128)S(1)} %add_add_fusion.refs_0_), channel_id=1, source_target_pairs={{0,2},{2,0},{1,3},{3,1},{4,6},{6,4},{5,7},{7,5},{8,10},{10,8},{9,1... | collective-permute-start | bytes 294920 | tf_op jit(solution)/shard_map/ppermute | solution.py:565
  63.5 3.5 %collective-permute-start.20 = (f32[96,256]{1,0:T(8,128)S(1)}, f32[96,256]{1,0:T(8,128)S(1)}, u32[]{:S(2)}, u32[]{:S(2)}) collective-permute-start(f32[96,256]{1,0:T(8,128)S(1)} %add_add_fusion.refs_0_), channel_id=1, source_target_pairs={{0,1},{1,0},{2,3},{3,2},{4,5},{5,4},{6,7},{7,6},{8,9},{9,8},{10,11... | collective-permute-start | bytes 294920 | tf_op jit(solution)/shard_map/ppermute | solution.py:565
  66.0 1.3 %collective-permute-start.23 = (f32[96,256]{1,0:T(8,128)S(1)}, f32[96,256]{1,0:T(8,128)S(1)}, u32[]{:S(2)}, u32[]{:S(2)}) collective-permute-start(f32[96,256]{1,0:T(8,128)S(1)} %collective-permute-done.19.refs_3_), channel_id=1, source_target_pairs={{0,1},{1,0},{2,3},{3,2},{4,5},{5,4},{6,7},{7,6},{8,9},{9,8},{10,11... | collective-permute-start | bytes 294920 | tf_op jit(solution)/shard_map/ppermute | solution.py:565
  66.2 1.3 %collective-permute-start.22 = (f32[96,256]{1,0:T(8,128)S(1)}, f32[96,256]{1,0:T(8,128)S(1)}, u32[]{:S(2)}, u32[]{:S(2)}) collective-permute-start(f32[96,256]{1,0:T(8,128)S(1)} %collective-permute-done.18.refs_2_), channel_id=1, source_target_pairs={{0,1},{1,0},{2,3},{3,2},{4,5},{5,4},{6,7},{7,6},{8,9},{9,8},{10,11... | collective-permute-start | bytes 294920 | tf_op jit(solution)/shard_map/ppermute | solution.py:565
  67.0 1.3 %collective-permute-start.21 = (f32[96,256]{1,0:T(8,128)S(1)}, f32[96,256]{1,0:T(8,128)S(1)}, u32[]{:S(2)}, u32[]{:S(2)}) collective-permute-start(f32[96,256]{1,0:T(8,128)S(1)} %collective-permute-done.17.refs_1_), channel_id=1, source_target_pairs={{0,1},{1,0},{2,3},{3,2},{4,5},{5,4},{6,7},{7,6},{8,9},{9,8},{10,11... | collective-permute-start | bytes 294920 | tf_op jit(solution)/shard_map/ppermute | solution.py:565

commit v6 on v5

--- a/solution.py
+++ b/solution.py
@@ -304,35 +304,52 @@
         image_ref[:, lanes] = smooth + fixed
 
 
-def gram_kernel(ranks, first_ref, diag_ref, first_half, *refs):
+def gram_kernel(ranks, place_ref, first_ref, diag_ref, first_half, *refs):
     currents, parts, (block, image, low) = refs[:ranks], refs[ranks:-3], refs[-3:]
     columns = currents[0].shape[0]
     second_half = add_parts(parts)
     low[...] = second_half.astype(bf16)
     full_image(first_ref, diag_ref, currents[0], (first_half[...], second_half), image)
+    mine = currents[0][...]
+    half = columns // 2
     for rank in range(ranks):
         current = currents[rank][...]
         block[rank, :columns] = close_dot(image[...], current, 1, 1)
-        block[rank, columns : 2 * columns] = close_dot(currents[0][...], current, 1, 1)
-    block[0, 2 * columns :] = close_dot(image[...], image[...], 1, 1)
-
-
-def gram_sums(first, diag, smooth, parts, currents):
+        if rank > 0:
+            ahead = place_ref[0] < place_ref[rank]
+            left = jnp.where(ahead, mine[:half], current[half:])
+            block[rank, 2 * columns : 2 * columns + half] = close_dot(left, jnp.where(ahead, current, mine), 1, 1)
+    square = close_dot(mine, mine, 1, 1)
+    row_at = lax.broadcasted_iota(jnp.int32, square.shape, 0)
+    col_at = lax.broadcasted_iota(jnp.int32, square.shape, 1)
+    block[0, columns : 2 * columns] = jnp.where(row_at > col_at, square, close_dot(image[...], image[...], 1, 1))
+    diagonal = jnp.sum(jnp.where(row_at == col_at, square, 0.0), axis=0, keepdims=True)
+    block[0, 2 * columns : 2 * columns + half] = jnp.broadcast_to(diagonal, (half, columns))
+    spare = block.shape[1] - 2 * columns - half
+    if spare > 0:
+        block[:, 2 * columns + half :] = jnp.zeros((ranks, spare, columns), f32)
+
+
+def sum_rows(columns):
+    return -(-5 * columns // 64) * 32
+
+
+def gram_sums(places, first, diag, smooth, parts, currents):
     ranks = len(currents)
     columns, count = currents[0].shape
     return pl.pallas_call(
         functools.partial(gram_kernel, ranks),
-        in_specs=[SMEM] + [VMEM] * (ranks + len(parts) + 2),
+        in_specs=[SMEM] * 2 + [VMEM] * (ranks + len(parts) + 2),
         out_specs=[VMEM] * 3,
         out_shape=(
-            jax.ShapeDtypeStruct((ranks, 3 * columns, columns), f32),
+            jax.ShapeDtypeStruct((ranks, sum_rows(columns), columns), f32),
             jax.ShapeDtypeStruct((columns, count), f32),
             jax.ShapeDtypeStruct((columns, count // 2), bf16),
         ),
         compiler_params=params(),
         cost_estimate=SMALL,
         name="gram",
-    )(first, diag, smooth, *currents, *parts)
+    )(places, first, diag, smooth, *currents, *parts)
 
 
 def cross_kernel(ranks, place_ref, cut_ref, block_ref, image_ref, diag_ref, *refs):
@@ -346,7 +363,7 @@
         lanes = pl.ds(pl.multiple_of(which * half, half), half)
         current = currents[rank - 1][:, lanes].astype(bf16).astype(f32)
         other = gots[rank - 1][...].astype(f32) + diag_ref[:, lanes].astype(bf16).astype(f32) * current
-        block[rank, 2 * columns :] = close_dot(image_ref[:, lanes], other, 1, 1)
+        block[rank, columns : 2 * columns] = close_dot(image_ref[:, lanes], other, 1, 1)
     for place in range(ranks):
         rank = jnp.bitwise_xor(place_ref[0], place)
         sums[:, place * columns : (place + 1) * columns] = block[rank]
@@ -360,15 +377,16 @@
     ranks = len(currents)
     columns, count = image.shape
     total = ranks * columns
-    half = jax.ShapeDtypeStruct((3 * columns // 2, total), f32)
+    rows = sum_rows(columns)
+    half = jax.ShapeDtypeStruct((rows // 2, total), f32)
     return pl.pallas_call(
         functools.partial(cross_kernel, ranks),
         in_specs=[SMEM, SMEM] + [VMEM] * (2 * ranks + 1),
         out_specs=[VMEM] * 2,
         out_shape=(half, half),
         scratch_shapes=[
-            pltpu.VMEM((3 * columns, total), f32),
-            pltpu.VMEM((ranks, 3 * columns, columns), f32),
+            pltpu.VMEM((rows, total), f32),
+            pltpu.VMEM((ranks, rows, columns), f32),
         ],
         compiler_params=params(),
         cost_estimate=SMALL,
@@ -431,10 +449,34 @@
     rows, total = shares[0].shape
     for at, share in enumerate(shares):
         sums[pl.ds(pl.multiple_of(share_ref[at] * rows, rows), rows), :] = share[...]
-    for rank in range(total // columns):
-        for which in range(3):
-            begin = (rank * 3 + which) * columns
-            grams[which, rank * columns : (rank + 1) * columns, :] = sums[begin : begin + columns, :]
+    ranks = total // columns
+    height = sums.shape[0] // ranks
+    half = columns // 2
+    row_at = lax.broadcasted_iota(jnp.int32, (total, total), 0)
+    col_at = lax.broadcasted_iota(jnp.int32, (total, total), 1)
+    same = row_at // columns == col_at // columns
+    lanes = col_at[:1] // columns
+    diagonal = jnp.zeros((1, total), f32)
+    grams[1] = jnp.zeros((total, total), f32)
+    for rank in range(ranks):
+        mine = slice(rank * columns, (rank + 1) * columns)
+        base = rank * height
+        grams[0, mine, :] = sums[base : base + columns, :]
+        grams[2, mine, :] = sums[base + columns : base + 2 * columns, :]
+        base += 2 * columns
+        diagonal = jnp.where(lanes == rank, sums[base : base + 1, :], diagonal)
+        for other in range(ranks):
+            block = sums[base : base + half, other * columns : (other + 1) * columns]
+            if other > rank:
+                grams[1, rank * columns : rank * columns + half, other * columns : (other + 1) * columns] = block
+            if other < rank:
+                grams[1, other * columns + half : (other + 1) * columns, mine] = block
+    pairs = grams[2]
+    flipped = pairs.T
+    across = grams[1]
+    own = jnp.where(row_at > col_at, pairs, jnp.where(row_at < col_at, flipped, diagonal))
+    grams[1] = jnp.where(same, own, across + across.T)
+    grams[2] = jnp.where(same, jnp.where(row_at > col_at, flipped, pairs), pairs + flipped)
     cross = grams[0]
     gram = 0.5 * (cross + cross.T)
     gram_scale = 1.0 / jnp.max(gram, keepdims=True)
@@ -448,11 +490,7 @@
     step_all[...] = close_dot(grams[1], gram_inv[...] * gram_scale, 1, 0)
     step = step_all[mine, :]
     step_ref[...] = step
-    row_at = lax.broadcasted_iota(jnp.int32, (total, total), 0) // columns
-    col_at = lax.broadcasted_iota(jnp.int32, (total, total), 1) // columns
-    pairs = grams[2]
-    images = pairs + jnp.where(row_at == col_at, 0.0, pairs.T)
-    left = close_dot(step, images, 1, 0)
+    left = close_dot(step, grams[2], 1, 0)
     across = close_dot(step, grams[0], 1, 0)
     grams[0] = grams[0].T
     left = left - grams[0, mine, :]
@@ -470,7 +508,7 @@
         out_specs=[VMEM] * 2,
         out_shape=(rows, rows),
         scratch_shapes=[
-            pltpu.VMEM((3 * total, total), f32),
+            pltpu.VMEM((total // columns * sum_rows(columns), total), f32),
             pltpu.VMEM((3, total, total), f32),
             square,
             square,
@@ -670,7 +708,7 @@
     smooth, low_first = combine([own_first, *arrived[0]])
     after, _ = lax.optimization_barrier((first, low_first))
     own_second = own_image(1, after, [theirs], b_side, near, False, [own_second])
-    blocks, image, low_second = gram_sums(first, diag, smooth, [own_second, *arrived[1]], currents)
+    blocks, image, low_second = gram_sums(places, first, diag, smooth, [own_second, *arrived[1]], currents)
     gots, rests = [], []
     for bits in range(1, ranks):
         if bits == 1:

time: 82.5 us -> 80.9 us (0.981)
  waiting for transfers between devices: 17.8 us -> 15.3 us
    ppermute x23, waiting for transfers between devices: 15.3 us -> 12.9 us  [swap(): return lax.ppermute(value, axis, [(at, at ^ bits) for at in range(size)])]
  transfers between devices with their start and end apart: 24 -> 24, of which waited for: 15 -> 14; matrix products, arithmetic and copies ran while one was open for 0% -> 0% of each run, Pallas kernels for 27% -> 28%
where the time goes in v6:
time: 80.9 us; the launch traced here: 80.8 us
  Pallas kernels  38.9 us (48%)
  starting transfers between devices  23.8 us (29%)
  waiting for transfers between devices  15.3 us (19%)
  other arithmetic  1.44 us (2%)
  between operations  1.08 us (1%)
    ppermute x23, starting transfers between devices, swap(): return lax.ppermute(value, axis, [(at, at ^ bits) for at in range(size)])  21.7 us
    ppermute x23, waiting for transfers between devices, swap(): return lax.ppermute(value, axis, [(at, at ^ bits) for at in range(size)])  12.9 us
    pallas_call x1, Pallas kernels, solve(): pl.pallas_call(functools.partial(solve_kernel, columns, 32), in_specs=[SM...  11.6 us
    pallas_call x8, Pallas kernels, image_part(): pl.pallas_call(functools.partial(image_kernel, range(len(densities)), slo...  8.5 us
    pallas_call x3, Pallas kernels, own_image(): pl.pallas_call(functools.partial(own_kernel, near, part, diagonal, len(st...  8.05 us
    pallas_call x1, Pallas kernels, geometry(): pl.pallas_call(functools.partial(geometry_kernel, scale, near), grid_spec...  4.88 us
    ppermute x1, waiting for transfers between devices, pair_swap(): return lax.ppermute(value, ('tri', 'rhs'), perm)  2.33 us
    pallas_call x1, Pallas kernels, finish(): pl.pallas_call(functools.partial(finish_kernel, ranks, chunks), in_specs=...  2.28 us
  transfers between devices with their start and end apart: 24, of which 14 were waited for; matrix products, arithmetic and copies ran while one was open for 0% of the time, Pallas kernels for 28%

profile of v6, /device:TPU:0, one launch (start us, length us, event | category | flops | bytes accessed | tf_op | source)
XLA Modules:
  0.0 80.8 jit_solution(4522679604309048461)
XLA Ops:
  0.7 1.2 %fusion = (bf16[128,1024]{1,0:T(8,128)(2,1)S(1)}, f32[128,1024]{1,0:T(8,128)S(1)}) fusion(f32[128,1024]{1,0:T(8,128)} %param.5, s32[1024]{0:T(1024)S(1)} %iota_add_fusion, s32[128]{0:T(128)} %param.6), kind=kLoop, calls=%fused_computation.6 | loop fusion | flops 524288 | bytes 1315328 | tf_op jit(solution)/shard_map/convert_element_type | solution.py:645
  1.9 3.0 %collective-permute-start.2 = (f32[128,1024]{1,0:T(8,128)S(1)}, f32[128,1024]{1,0:T(8,128)S(1)}, u32[]{:S(2)}, u32[]{:S(2)}) collective-permute-start(f32[128,1024]{1,0:T(8,128)S(1)} %get-tuple-element.90.refs_0_), channel_id=1, source_target_pairs={{0,2},{2,0},{1,3},{3,1},{4,6},{6,4},{5,7},{7,5},{8,10},{10,8},{9,1... | collective-permute-start | bytes 1572872 | tf_op jit(solution)/shard_map/ppermute | solution.py:603
  5.0 1.5 %collective-permute-start.4 = (bf16[128,1024]{1,0:T(8,128)(2,1)S(1)}, bf16[128,1024]{1,0:T(8,128)(2,1)S(1)}, u32[]{:S(2)}, u32[]{:S(2)}) collective-permute-start(bf16[128,1024]{1,0:T(8,128)(2,1)S(1)} %get-tuple-element.83.refs_0_), channel_id=1, source_target_pairs={{0,4},{4,0},{8,12},{12,8},{16,20},{20,16},{24,28},{28,24},{1,5},{5... | collective-permute-start | bytes 786440 | tf_op jit(solution)/shard_map/ppermute | solution.py:603
  6.4 1.6 %collective-permute-start.3 = (bf16[128,1024]{1,0:T(8,128)(2,1)S(1)}, bf16[128,1024]{1,0:T(8,128)(2,1)S(1)}, u32[]{:S(2)}, u32[]{:S(2)}) collective-permute-start(bf16[128,1024]{1,0:T(8,128)(2,1)S(1)} %get-tuple-element.83.refs_0_), channel_id=1, source_target_pairs={{0,8},{4,12},{8,0},{12,4},{16,24},{20,28},{24,16},{28,20},{1,9},{5... | collective-permute-start | bytes 786440 | tf_op jit(solution)/shard_map/ppermute | solution.py:603
  8.0 0.4 collective-permute-start
  8.8 4.9 %geometry.1 = (bf16[4,32,1024]{2,1,0:T(8,128)(2,1)S(1)}, bf16[2,32,1024]{2,1,0:T(8,128)(2,1)S(1)}, f32[1,1024]{1,0:T(1,128)S(1)}) custom-call(s32[5]{0:T(128)S(1)} %stack.80.blocks_ref, f32[3,8192]{1,0:T(4,128)S(1)} %copy-done.1, s32[3,16384]{1,0:T(4,128)S(1)} %copy-done, s32[1,16384]{1,0:T(1,128)S(1)} %bitcast.21), custom_call_target="tpu_custom_call" | custom-call | tf_op jit(solution)/shard_map/geometry/pallas_call | solution.py:136
  13.7 1.1 %image_part.8.refs_5_ = f32[128,1024]{1,0:T(8,128)S(1)} custom-call(s32[1]{0:T(128)} %bitcast.5.first_ref, bf16[128,1024]{1,0:T(8,128)(2,1)S(1)} %get-tuple-element.83.refs_0_, bf16[4,32,1024]{2,1,0:T(8,128)(2,1)S(1)} %get-tuple-element.80.refs_1_.refs_4_, bf16[2,32,1024]{2,1,0:T(8,128)(2,1)S(1)} %get-tuple-element.81.refs_2_.b_ref), custom_call_target="tpu_custom_call" | custom-call | flops 1024 | bytes 1024 | tf_op jit(solution)/shard_map/image_part/pallas_call | solution.py:200
  14.8 0.3 collective-permute-done.1.refs_3_
  15.1 1.0 %image_part.9.refs_4_ = f32[128,1024]{1,0:T(8,128)S(1)} custom-call(s32[1]{0:T(128)} %bitcast.5.first_ref, bf16[128,1024]{1,0:T(8,128)(2,1)S(1)} %get-tuple-element.83.refs_0_, bf16[4,32,1024]{2,1,0:T(8,128)(2,1)S(1)} %get-tuple-element.80.refs_1_.refs_4_, bf16[2,32,1024]{2,1,0:T(8,128)(2,1)S(1)} %get-tuple-element.81.refs_2_.b_ref, ...), custom_call_target="tpu_custom_call" | custom-call | flops 1024 | bytes 1024 | tf_op jit(solution)/shard_map/image_part/pallas_call | solution.py:200
  16.1 2.0 %image_part.10 = (f32[128,1024]{1,0:T(8,128)S(1)}, f32[128,1024]{1,0:T(8,128)S(1)}) custom-call(s32[1]{0:T(128)} %bitcast.5.first_ref, bf16[128,1024]{1,0:T(8,128)(2,1)S(1)} %collective-permute-done.4.refs_0_.refs_1_, bf16[4,32,1024]{2,1,0:T(8,128)(2,1)S(1)} %get-tuple-element.80.refs_1_.refs_4_, bf16[2,32,1024]{2,1,0:T(8,128)(2,1)S(1)} %get-tuple-element.81.refs_2_.b_ref, ...), custom_call_target="tpu_custom_call" | custom-call | flops 1024 | bytes 1024 | tf_op jit(solution)/shard_map/image_part/pallas_call | solution.py:200
  18.1 1.9 %image_part.11 = (f32[128,1024]{1,0:T(8,128)S(1)}, f32[128,1024]{1,0:T(8,128)S(1)}) custom-call(s32[1]{0:T(128)} %bitcast.5.first_ref, bf16[128,1024]{1,0:T(8,128)(2,1)S(1)} %collective-permute-done.3.refs_0_.refs_2_, bf16[4,32,1024]{2,1,0:T(8,128)(2,1)S(1)} %get-tuple-element.80.refs_1_.refs_4_, bf16[2,32,1024]{2,1,0:T(8,128)(2,1)S(1)} %get-tuple-element.81.refs_2_.b_ref, ...), custom_call_target="tpu_custom_call" | custom-call | flops 1024 | bytes 1024 | tf_op jit(solution)/shard_map/image_part/pallas_call | solution.py:200
  20.1 0.6 image_part.12
  20.7 0.3 collective-permute-start.5
  21.0 0.6 image_part.13
  21.7 0.5 collective-permute-done.5.refs_4_
  22.1 0.6 image_part.14
  22.9 0.3 collective-permute-start.7
  23.2 0.3 collective-permute-start.6
  23.4 2.6 %collective-permute-start.8 = (bf16[128,512]{1,0:T(8,128)(2,1)S(1)}, bf16[128,512]{1,0:T(8,128)(2,1)S(1)}, u32[]{:S(2)}, u32[]{:S(2)}) collective-permute-start(bf16[128,512]{1,0:T(8,128)(2,1)S(1)} %image_part.14), channel_id=1, source_target_pairs={{0,16},{4,20},{8,24},{12,28},{16,0},{20,4},{24,8},{28,12},{1,17},{... | collective-permute-start | bytes 393224 | tf_op jit(solution)/shard_map/ppermute | solution.py:603
  26.2 0.6 image_part.15
  26.8 2.7 %collective-permute-start.9 = (bf16[128,512]{1,0:T(8,128)(2,1)S(1)}, bf16[128,512]{1,0:T(8,128)(2,1)S(1)}, u32[]{:S(2)}, u32[]{:S(2)}) collective-permute-start(bf16[128,512]{1,0:T(8,128)(2,1)S(1)} %image_part.15), channel_id=1, source_target_pairs={{0,16},{4,20},{8,24},{12,28},{16,0},{20,4},{24,8},{28,12},{1,17},{... | collective-permute-start | bytes 393224 | tf_op jit(solution)/shard_map/ppermute | solution.py:603
  29.5 3.8 %own_image.3.refs_0_ = f32[128,512]{1,0:T(8,128)S(1)} custom-call(s32[1]{0:T(128)} %bitcast.5.first_ref, bf16[2,32,1024]{2,1,0:T(8,128)(2,1)S(1)} %get-tuple-element.81.refs_2_.b_ref, bf16[640,1024]{1,0:T(8,128)(2,1)S(1)} %stack_rows.1.refs_0_, bf16[640,1024]{1,0:T(8,128)(2,1)S(1)} %collective-permute-done.7.refs_1_.refs_0_), custom_call_target="tpu_custom_call" | custom-call | flops 1024 | bytes 1024 | tf_op jit(solution)/shard_map/own_image/pallas_call | solution.py:263
  33.3 2.0 %own_image.4.refs_1_ = f32[128,512]{1,0:T(8,128)S(1)} custom-call(s32[1]{0:T(128)} %bitcast.5.first_ref, bf16[2,32,1024]{2,1,0:T(8,128)(2,1)S(1)} %get-tuple-element.81.refs_2_.b_ref, bf16[640,1024]{1,0:T(8,128)(2,1)S(1)} %stack_rows.1.refs_0_), custom_call_target="tpu_custom_call" | custom-call | flops 1024 | bytes 1024 | tf_op jit(solution)/shard_map/own_image/pallas_call | solution.py:263
  35.3 1.0 %collective-permute-done.8.refs_1_ = bf16[128,512]{1,0:T(8,128)(2,1)S(1)} collective-permute-done((bf16[128,512]{1,0:T(8,128)(2,1)S(1)}, bf16[128,512]{1,0:T(8,128)(2,1)S(1)}, u32[]{:S(2)}, u32[]{:S(2)}) %collective-permute-start.8) | collective-permute-done | bytes 131104 | tf_op jit(solution)/shard_map/ppermute | solution.py:603
  36.3 0.2 collective-permute-start.10
  36.5 2.2 %own_image.5.refs_2_ = f32[128,512]{1,0:T(8,128)S(1)} custom-call(s32[1]{0:T(128)} %bitcast.5.first_ref, bf16[2,32,1024]{2,1,0:T(8,128)(2,1)S(1)} %get-tuple-element.81.refs_2_.b_ref, bf16[640,1024]{1,0:T(8,128)(2,1)S(1)} %collective-permute-done.7.refs_1_.refs_0_, f32[128,512]{1,0:T(8,128)S(1)} %own_image.4.refs_1_), custom_call_target="tpu_custom_call" | custom-call | flops 1024 | bytes 1024 | tf_op jit(solution)/shard_map/own_image/pallas_call | solution.py:263
  38.8 2.0 %gram.1 = (f32[2,320,128]{2,1,0:T(8,128)S(1)}, f32[128,1024]{1,0:T(8,128)S(1)}, bf16[128,512]{1,0:T(8,128)(2,1)S(1)}) custom-call(s32[2]{0:T(128)S(1)} %pad_add_fusion.place_ref, s32[1]{0:T(128)} %bitcast.5.first_ref, f32[1,1024]{1,0:T(1,128)S(1)} %get-tuple-element.61.diag_ref, f32[128,512]{1,0:T(8,128)S(1)} %get-tuple-element.89.first_half, ...), custom_call_target="tpu_custom_call" | custom-call | flops 1024 | bytes 1024 | tf_op jit(solution)/shard_map/gram/pallas_call | solution.py:340
  40.7 0.6 collective-permute-done.10.refs_1_
  41.4 0.9 %cross.1 = (f32[160,256]{1,0:T(8,128)S(1)}, f32[160,256]{1,0:T(8,128)S(1)}) custom-call(s32[2]{0:T(128)S(1)} %pad_add_fusion.place_ref, s32[4]{0:T(128)S(1)} %pad_add_fusion.1.cut_ref, f32[2,320,128]{2,1,0:T(8,128)S(1)} %get-tuple-element.95.block_ref, f32[128,1024]{1,0:T(8,128)S(1)} %get-tuple-element.96.image_ref.refs_2_, ...), custom_call_target="tpu_custom_call" | custom-call | flops 1024 | bytes 1024 | tf_op jit(solution)/shard_map/cross/pallas_call | solution.py:382
  42.4 1.4 %collective-permute-done.11 = f32[160,256]{1,0:T(8,128)S(1)} collective-permute-done((f32[160,256]{1,0:T(8,128)S(1)}, f32[160,256]{1,0:T(8,128)S(1)}, u32[]{:S(2)}, u32[]{:S(2)}) %collective-permute-start.11) | collective-permute-done | bytes 163872 | tf_op jit(solution)/shard_map/ppermute | solution.py:603
  43.8 1.6 %collective-permute-start.12 = (f32[80,256]{1,0:T(8,128)S(1)}, f32[80,256]{1,0:T(8,128)S(1)}, u32[]{:S(2)}, u32[]{:S(2)}) collective-permute-start(f32[80,256]{1,0:T(8,128)S(1)} %split.9), channel_id=1, source_target_pairs={{0,4},{4,0},{8,12},{12,8},{16,20},{20,16},{24,28},{28,24},{1,5},{5... | collective-permute-start | bytes 245768 | tf_op jit(solution)/shard_map/ppermute | solution.py:603
  45.3 1.3 %collective-permute-start.16 = (bf16[128,512]{1,0:T(8,128)(2,1)S(1)}, bf16[128,512]{1,0:T(8,128)(2,1)S(1)}, u32[]{:S(2)}, u32[]{:S(2)}) collective-permute-start(bf16[128,512]{1,0:T(8,128)(2,1)S(1)} %get-tuple-element.100), channel_id=1, source_target_pairs={{0,2},{2,0},{1,3},{3,1},{4,6},{6,4},{5,7},{7,5},{8,10},{10,8},{9,1... | collective-permute-start | bytes 393224 | tf_op jit(solution)/shard_map/ppermute | solution.py:603
  46.6 1.7 %collective-permute-done.12 = f32[80,256]{1,0:T(8,128)S(1)} collective-permute-done((f32[80,256]{1,0:T(8,128)S(1)}, f32[80,256]{1,0:T(8,128)S(1)}, u32[]{:S(2)}, u32[]{:S(2)}) %collective-permute-start.12) | collective-permute-done | bytes 81952 | tf_op jit(solution)/shard_map/ppermute | solution.py:603
  48.3 3.3 %collective-permute-start.15 = (f32[80,256]{1,0:T(8,128)S(1)}, f32[80,256]{1,0:T(8,128)S(1)}, u32[]{:S(2)}, u32[]{:S(2)}) collective-permute-start(f32[80,256]{1,0:T(8,128)S(1)} %slice_add_fusion), channel_id=1, source_target_pairs={{0,24},{4,28},{8,16},{12,20},{16,8},{20,12},{24,0},{28,4},{1,25},{... | collective-permute-start | bytes 245768 | tf_op jit(solution)/shard_map/ppermute | solution.py:603
  51.7 1.1 %collective-permute-start.13 = (f32[80,256]{1,0:T(8,128)S(1)}, f32[80,256]{1,0:T(8,128)S(1)}, u32[]{:S(2)}, u32[]{:S(2)}) collective-permute-start(f32[80,256]{1,0:T(8,128)S(1)} %slice_add_fusion), channel_id=1, source_target_pairs={{0,8},{4,12},{8,0},{12,4},{16,24},{20,28},{24,16},{28,20},{1,9},{5... | collective-permute-start | bytes 245768 | tf_op jit(solution)/shard_map/ppermute | solution.py:603
  52.8 0.6 other_images.1.refs_3_
  53.4 1.5 %collective-permute-done.15 = f32[80,256]{1,0:T(8,128)S(1)} collective-permute-done((f32[80,256]{1,0:T(8,128)S(1)}, f32[80,256]{1,0:T(8,128)S(1)}, u32[]{:S(2)}, u32[]{:S(2)}) %collective-permute-start.15) | collective-permute-done | bytes 81952 | tf_op jit(solution)/shard_map/ppermute | solution.py:603
  55.0 3.3 %collective-permute-done.14 = f32[80,256]{1,0:T(8,128)S(1)} collective-permute-done((f32[80,256]{1,0:T(8,128)S(1)}, f32[80,256]{1,0:T(8,128)S(1)}, u32[]{:S(2)}, u32[]{:S(2)}) %collective-permute-start.14) | collective-permute-done | bytes 81952 | tf_op jit(solution)/shard_map/ppermute | solution.py:603
  58.3 2.2 %collective-permute-start.19 = (f32[80,256]{1,0:T(8,128)S(1)}, f32[80,256]{1,0:T(8,128)S(1)}, u32[]{:S(2)}, u32[]{:S(2)}) collective-permute-start(f32[80,256]{1,0:T(8,128)S(1)} %add_add_fusion.refs_0_), channel_id=1, source_target_pairs={{0,6},{2,4},{4,2},{6,0},{8,14},{10,12},{12,10},{14,8},{16,22},{18,... | collective-permute-start | bytes 245768 | tf_op jit(solution)/shard_map/ppermute | solution.py:616
  60.5 0.5 collective-permute-start.18
  61.0 0.9 %collective-permute-start.17 = (f32[80,256]{1,0:T(8,128)S(1)}, f32[80,256]{1,0:T(8,128)S(1)}, u32[]{:S(2)}, u32[]{:S(2)}) collective-permute-start(f32[80,256]{1,0:T(8,128)S(1)} %add_add_fusion.refs_0_), channel_id=1, source_target_pairs={{0,2},{2,0},{1,3},{3,1},{4,6},{6,4},{5,7},{7,5},{8,10},{10,8},{9,1... | collective-permute-start | bytes 245768 | tf_op jit(solution)/shard_map/ppermute | solution.py:603
  61.8 2.3 %collective-permute-done.19.refs_3_ = f32[80,256]{1,0:T(8,128)S(1)} collective-permute-done((f32[80,256]{1,0:T(8,128)S(1)}, f32[80,256]{1,0:T(8,128)S(1)}, u32[]{:S(2)}, u32[]{:S(2)}) %collective-permute-start.19) | collective-permute-done | bytes 81952 | tf_op jit(solution)/shard_map/ppermute | solution.py:616
  64.2 0.7 collective-permute-done.18.refs_2_
  64.9 0.5 collective-permute-done.17.refs_1_
  65.5 0.7 collective-permute-done.22.refs_6_
  66.2 0.5 collective-permute-done.21.refs_5_
  66.7 11.6 %solve.1 = (f32[128,256]{1,0:T(8,128)S(1)}, f32[128,256]{1,0:T(8,128)S(1)}) custom-call(s32[2]{0:T(128)S(1)} %pad_add_fusion.place_ref, s32[8]{0:T(128)S(1)} %stack.99.share_ref, f32[80,256]{1,0:T(8,128)S(1)} %add_add_fusion.refs_0_, f32[80,256]{1,0:T(8,128)S(1)} %collective-permute-done.17.refs_1_, f32[80,256]{1,0:T(8,128)S(1)} %collective-permute-done.18.refs_2_, ...), custom_call_target="tpu_custom_call" | custom-call | tf_op jit(solution)/shard_map/solve/pallas_call | solution.py:505
  78.3 2.3 %finish.1 = (f32[128,1024]{1,0:T(8,128)}, f32[128,1024]{1,0:T(8,128)}, f32[128,1024]{1,0:T(8,128)}) custom-call(s32[2]{0:T(128)S(1)} %pad_add_fusion.place_ref, f32[128,256]{1,0:T(8,128)S(1)} %get-tuple-element.104.step_ref, f32[128,256]{1,0:T(8,128)S(1)} %get-tuple-element.105.turn_ref, f32[128,1024]{1,0:T(8,128)S(1)} %get-tuple-element.90.refs_0_, ...), custom_call_target="tpu_custom_call" | custom-call | flops 1024 | bytes 1024 | tf_op jit(solution)/shard_map/finish/pallas_call | solution.py:587
  (35 shorter events, 0.8 us)
Async XLA Ops:
  0.6 8.1 %copy-start.1 = (f32[3,8192]{1,0:T(4,128)S(1)}, f32[3,8192]{1,0:T(4,128)}, u32[]{:S(2)}) copy-start(f32[3,8192]{1,0:T(4,128)} %vertices_ref) | copy-start | bytes 294916
  0.6 8.1 %copy-start.2 = (s32[16384]{0:T(1024)S(1)}, s32[16384]{0:T(1024)}, u32[]{:S(2)}) copy-start(s32[16384]{0:T(1024)} %param.9) | copy-start | bytes 196612
  0.7 8.1 %copy-start = (s32[3,16384]{1,0:T(4,128)S(1)}, s32[3,16384]{1,0:T(4,128)}, u32[]{:S(2)}) copy-start(s32[3,16384]{1,0:T(4,128)} %corners_ref.1) | copy-start | bytes 589828
  1.9 18.2 %collective-permute-start.2 = (f32[128,1024]{1,0:T(8,128)S(1)}, f32[128,1024]{1,0:T(8,128)S(1)}, u32[]{:S(2)}, u32[]{:S(2)}) collective-permute-start(f32[128,1024]{1,0:T(8,128)S(1)} %get-tuple-element.90.refs_0_), channel_id=1, source_target_pairs={{0,2},{2,0},{1,3},{3,1},{4,6},{6,4},{5,7},{7,5},{8,10},{10,8},{9,1... | collective-permute-start | bytes 1572872 | tf_op jit(solution)/shard_map/ppermute | solution.py:603
  5.0 11.2 %collective-permute-start.4 = (bf16[128,1024]{1,0:T(8,128)(2,1)S(1)}, bf16[128,1024]{1,0:T(8,128)(2,1)S(1)}, u32[]{:S(2)}, u32[]{:S(2)}) collective-permute-start(bf16[128,1024]{1,0:T(8,128)(2,1)S(1)} %get-tuple-element.83.refs_0_), channel_id=1, source_target_pairs={{0,4},{4,0},{8,12},{12,8},{16,20},{20,16},{24,28},{28,24},{1,5},{5... | collective-permute-start | bytes 786440 | tf_op jit(solution)/shard_map/ppermute | solution.py:603
  6.4 11.7 %collective-permute-start.3 = (bf16[128,1024]{1,0:T(8,128)(2,1)S(1)}, bf16[128,1024]{1,0:T(8,128)(2,1)S(1)}, u32[]{:S(2)}, u32[]{:S(2)}) collective-permute-start(bf16[128,1024]{1,0:T(8,128)(2,1)S(1)} %get-tuple-element.83.refs_0_), channel_id=1, source_target_pairs={{0,8},{4,12},{8,0},{12,4},{16,24},{20,28},{24,16},{28,20},{1,9},{5... | collective-permute-start | bytes 786440 | tf_op jit(solution)/shard_map/ppermute | solution.py:603
  8.0 12.1 %collective-permute-start = (bf16[128,1024]{1,0:T(8,128)(2,1)S(1)}, bf16[128,1024]{1,0:T(8,128)(2,1)S(1)}, u32[]{:S(2)}, u32[]{:S(2)}) collective-permute-start(bf16[128,1024]{1,0:T(8,128)(2,1)S(1)} %get-tuple-element.83.refs_0_), channel_id=1, source_target_pairs={{0,12},{4,8},{8,4},{12,0},{16,28},{20,24},{24,20},{28,16},{1,13},{... | collective-permute-start | bytes 786440 | tf_op jit(solution)/shard_map/ppermute | solution.py:603
  13.7 1.4 %collective-permute-start.1 = (bf16[2,32,1024]{2,1,0:T(8,128)(2,1)S(1)}, bf16[2,32,1024]{2,1,0:T(8,128)(2,1)S(1)}, u32[]{:S(2)}, u32[]{:S(2)}) collective-permute-start(bf16[2,32,1024]{2,1,0:T(8,128)(2,1)S(1)} %get-tuple-element.81.refs_2_.b_ref), channel_id=1, source_target_pairs={{0,1},{1,0},{2,3},{3,2},{4,5},{5,4},{6,7},{7,6},{8,9},{9,8},{10,11... | collective-permute-start | bytes 393224 | tf_op jit(solution)/shard_map/ppermute | solution.py:603
  20.7 1.4 %collective-permute-start.5 = (bf16[128,512]{1,0:T(8,128)(2,1)S(1)}, bf16[128,512]{1,0:T(8,128)(2,1)S(1)}, u32[]{:S(2)}, u32[]{:S(2)}) collective-permute-start(bf16[128,512]{1,0:T(8,128)(2,1)S(1)} %image_part.12), channel_id=1, source_target_pairs={{0,1},{1,0},{2,3},{3,2},{4,5},{5,4},{6,7},{7,6},{8,9},{9,8},{10,11... | collective-permute-start | bytes 393224 | tf_op jit(solution)/shard_map/ppermute | solution.py:603
  22.9 6.6 %collective-permute-start.7 = (bf16[640,1024]{1,0:T(8,128)(2,1)S(1)}, bf16[640,1024]{1,0:T(8,128)(2,1)S(1)}, u32[]{:S(2)}, u32[]{:S(2)}) collective-permute-start(bf16[640,1024]{1,0:T(8,128)(2,1)S(1)} %stack_rows.1.refs_0_), channel_id=1, source_target_pairs={{0,1},{1,0},{2,3},{3,2},{4,5},{5,4},{6,7},{7,6},{8,9},{9,8},{10,11... | collective-permute-start | bytes 3932168 | tf_op jit(solution)/shard_map/ppermute | solution.py:603
  23.2 3.0 %collective-permute-start.6 = (bf16[128,512]{1,0:T(8,128)(2,1)S(1)}, bf16[128,512]{1,0:T(8,128)(2,1)S(1)}, u32[]{:S(2)}, u32[]{:S(2)}) collective-permute-start(bf16[128,512]{1,0:T(8,128)(2,1)S(1)} %image_part.13), channel_id=1, source_target_pairs={{0,1},{1,0},{2,3},{3,2},{4,5},{5,4},{6,7},{7,6},{8,9},{9,8},{10,11... | collective-permute-start | bytes 393224 | tf_op jit(solution)/shard_map/ppermute | solution.py:603
  23.4 12.8 %collective-permute-start.8 = (bf16[128,512]{1,0:T(8,128)(2,1)S(1)}, bf16[128,512]{1,0:T(8,128)(2,1)S(1)}, u32[]{:S(2)}, u32[]{:S(2)}) collective-permute-start(bf16[128,512]{1,0:T(8,128)(2,1)S(1)} %image_part.14), channel_id=1, source_target_pairs={{0,16},{4,20},{8,24},{12,28},{16,0},{20,4},{24,8},{28,12},{1,17},{... | collective-permute-start | bytes 393224 | tf_op jit(solution)/shard_map/ppermute | solution.py:603
  26.8 12.0 %collective-permute-start.9 = (bf16[128,512]{1,0:T(8,128)(2,1)S(1)}, bf16[128,512]{1,0:T(8,128)(2,1)S(1)}, u32[]{:S(2)}, u32[]{:S(2)}) collective-permute-start(bf16[128,512]{1,0:T(8,128)(2,1)S(1)} %image_part.15), channel_id=1, source_target_pairs={{0,16},{4,20},{8,24},{12,28},{16,0},{20,4},{24,8},{28,12},{1,17},{... | collective-permute-start | bytes 393224 | tf_op jit(solution)/shard_map/ppermute | solution.py:603
  36.3 5.0 %collective-permute-start.10 = (bf16[128,512]{1,0:T(8,128)(2,1)S(1)}, bf16[128,512]{1,0:T(8,128)(2,1)S(1)}, u32[]{:S(2)}, u32[]{:S(2)}) collective-permute-start(bf16[128,512]{1,0:T(8,128)(2,1)S(1)} %get-tuple-element.92), channel_id=1, source_target_pairs={{0,2},{2,0},{1,3},{3,1},{4,6},{6,4},{5,7},{7,5},{8,10},{10,8},{9,1... | collective-permute-start | bytes 393224 | tf_op jit(solution)/shard_map/ppermute | solution.py:603
  42.3 1.5 %collective-permute-start.11 = (f32[160,256]{1,0:T(8,128)S(1)}, f32[160,256]{1,0:T(8,128)S(1)}, u32[]{:S(2)}, u32[]{:S(2)}) collective-permute-start(f32[160,256]{1,0:T(8,128)S(1)} %get-tuple-element.98), channel_id=1, source_target_pairs={{0,1},{1,0},{2,3},{3,2},{4,5},{5,4},{6,7},{7,6},{8,9},{9,8},{10,11... | collective-permute-start | bytes 491528 | tf_op jit(solution)/shard_map/ppermute | solution.py:603
  43.8 4.6 %collective-permute-start.12 = (f32[80,256]{1,0:T(8,128)S(1)}, f32[80,256]{1,0:T(8,128)S(1)}, u32[]{:S(2)}, u32[]{:S(2)}) collective-permute-start(f32[80,256]{1,0:T(8,128)S(1)} %split.9), channel_id=1, source_target_pairs={{0,4},{4,0},{8,12},{12,8},{16,20},{20,16},{24,28},{28,24},{1,5},{5... | collective-permute-start | bytes 245768 | tf_op jit(solution)/shard_map/ppermute | solution.py:603
  45.3 7.5 %collective-permute-start.16 = (bf16[128,512]{1,0:T(8,128)(2,1)S(1)}, bf16[128,512]{1,0:T(8,128)(2,1)S(1)}, u32[]{:S(2)}, u32[]{:S(2)}) collective-permute-start(bf16[128,512]{1,0:T(8,128)(2,1)S(1)} %get-tuple-element.100), channel_id=1, source_target_pairs={{0,2},{2,0},{1,3},{3,1},{4,6},{6,4},{5,7},{7,5},{8,10},{10,8},{9,1... | collective-permute-start | bytes 393224 | tf_op jit(solution)/shard_map/ppermute | solution.py:603
  48.3 6.6 %collective-permute-start.15 = (f32[80,256]{1,0:T(8,128)S(1)}, f32[80,256]{1,0:T(8,128)S(1)}, u32[]{:S(2)}, u32[]{:S(2)}) collective-permute-start(f32[80,256]{1,0:T(8,128)S(1)} %slice_add_fusion), channel_id=1, source_target_pairs={{0,24},{4,28},{8,16},{12,20},{16,8},{20,12},{24,0},{28,4},{1,25},{... | collective-permute-start | bytes 245768 | tf_op jit(solution)/shard_map/ppermute | solution.py:603
  51.7 6.6 %collective-permute-start.14 = (f32[80,256]{1,0:T(8,128)S(1)}, f32[80,256]{1,0:T(8,128)S(1)}, u32[]{:S(2)}, u32[]{:S(2)}) collective-permute-start(f32[80,256]{1,0:T(8,128)S(1)} %slice_add_fusion), channel_id=1, source_target_pairs={{0,16},{4,20},{8,24},{12,28},{16,0},{20,4},{24,8},{28,12},{1,17},{... | collective-permute-start | bytes 245768 | tf_op jit(solution)/shard_map/ppermute | solution.py:603
  51.7 6.6 %collective-permute-start.13 = (f32[80,256]{1,0:T(8,128)S(1)}, f32[80,256]{1,0:T(8,128)S(1)}, u32[]{:S(2)}, u32[]{:S(2)}) collective-permute-start(f32[80,256]{1,0:T(8,128)S(1)} %slice_add_fusion), channel_id=1, source_target_pairs={{0,8},{4,12},{8,0},{12,4},{16,24},{20,28},{24,16},{28,20},{1,9},{5... | collective-permute-start | bytes 245768 | tf_op jit(solution)/shard_map/ppermute | solution.py:603
  58.3 5.9 %collective-permute-start.19 = (f32[80,256]{1,0:T(8,128)S(1)}, f32[80,256]{1,0:T(8,128)S(1)}, u32[]{:S(2)}, u32[]{:S(2)}) collective-permute-start(f32[80,256]{1,0:T(8,128)S(1)} %add_add_fusion.refs_0_), channel_id=1, source_target_pairs={{0,6},{2,4},{4,2},{6,0},{8,14},{10,12},{12,10},{14,8},{16,22},{18,... | collective-permute-start | bytes 245768 | tf_op jit(solution)/shard_map/ppermute | solution.py:616
  60.5 4.4 %collective-permute-start.18 = (f32[80,256]{1,0:T(8,128)S(1)}, f32[80,256]{1,0:T(8,128)S(1)}, u32[]{:S(2)}, u32[]{:S(2)}) collective-permute-start(f32[80,256]{1,0:T(8,128)S(1)} %add_add_fusion.refs_0_), channel_id=1, source_target_pairs={{0,4},{4,0},{8,12},{12,8},{16,20},{20,16},{24,28},{28,24},{1,5},{5... | collective-permute-start | bytes 245768 | tf_op jit(solution)/shard_map/ppermute | solution.py:603
  61.0 4.4 %collective-permute-start.17 = (f32[80,256]{1,0:T(8,128)S(1)}, f32[80,256]{1,0:T(8,128)S(1)}, u32[]{:S(2)}, u32[]{:S(2)}) collective-permute-start(f32[80,256]{1,0:T(8,128)S(1)} %add_add_fusion.refs_0_), channel_id=1, source_target_pairs={{0,2},{2,0},{1,3},{3,1},{4,6},{6,4},{5,7},{7,5},{8,10},{10,8},{9,1... | collective-permute-start | bytes 245768 | tf_op jit(solution)/shard_map/ppermute | solution.py:603
  61.8 3.6 %collective-permute-start.20 = (f32[80,256]{1,0:T(8,128)S(1)}, f32[80,256]{1,0:T(8,128)S(1)}, u32[]{:S(2)}, u32[]{:S(2)}) collective-permute-start(f32[80,256]{1,0:T(8,128)S(1)} %add_add_fusion.refs_0_), channel_id=1, source_target_pairs={{0,1},{1,0},{2,3},{3,2},{4,5},{5,4},{6,7},{7,6},{8,9},{9,8},{10,11... | collective-permute-start | bytes 245768 | tf_op jit(solution)/shard_map/ppermute | solution.py:603
  64.2 1.3 %collective-permute-start.23 = (f32[80,256]{1,0:T(8,128)S(1)}, f32[80,256]{1,0:T(8,128)S(1)}, u32[]{:S(2)}, u32[]{:S(2)}) collective-permute-start(f32[80,256]{1,0:T(8,128)S(1)} %collective-permute-done.19.refs_3_), channel_id=1, source_target_pairs={{0,1},{1,0},{2,3},{3,2},{4,5},{5,4},{6,7},{7,6},{8,9},{9,8},{10,11... | collective-permute-start | bytes 245768 | tf_op jit(solution)/shard_map/ppermute | solution.py:603
  64.9 1.3 %collective-permute-start.22 = (f32[80,256]{1,0:T(8,128)S(1)}, f32[80,256]{1,0:T(8,128)S(1)}, u32[]{:S(2)}, u32[]{:S(2)}) collective-permute-start(f32[80,256]{1,0:T(8,128)S(1)} %collective-permute-done.18.refs_2_), channel_id=1, source_target_pairs={{0,1},{1,0},{2,3},{3,2},{4,5},{5,4},{6,7},{7,6},{8,9},{9,8},{10,11... | collective-permute-start | bytes 245768 | tf_op jit(solution)/shard_map/ppermute | solution.py:603
  65.4 1.3 %collective-permute-start.21 = (f32[80,256]{1,0:T(8,128)S(1)}, f32[80,256]{1,0:T(8,128)S(1)}, u32[]{:S(2)}, u32[]{:S(2)}) collective-permute-start(f32[80,256]{1,0:T(8,128)S(1)} %collective-permute-done.17.refs_1_), channel_id=1, source_target_pairs={{0,1},{1,0},{2,3},{3,2},{4,5},{5,4},{6,7},{7,6},{8,9},{9,8},{10,11... | collective-permute-start | bytes 245768 | tf_op jit(solution)/shard_map/ppermute | solution.py:603

commit v7 on v6

--- a/solution.py
+++ b/solution.py
@@ -696,12 +696,19 @@
                 part(last, [(*at[:2], half) for at in own_at], far_own, extras=sent[half], kind=bf16)
             )
             arrived[half] = [swap(value, "tri", near * far) for far, value in zip(fars, far_sum[half])]
-            sides, _ = lax.optimization_barrier((sides, far_sum))
-        sources, _ = lax.optimization_barrier((sources, far_sum[0]))
-    mine = stack_rows(sources, a_side, near)
-    theirs = swap(mine, "split", 1)
-    after, _ = lax.optimization_barrier((first, far_sum))
-    own_first = own_image(0, after, [mine, theirs], b_side, near, True)
+            if half == 0:
+                sources, _ = lax.optimization_barrier((sources, far_sum[0]))
+                mine = stack_rows(sources, a_side, near)
+                theirs = swap(mine, "split", 1)
+                after, _ = lax.optimization_barrier((first, far_sum[0]))
+                own_first = own_image(0, after, [mine], b_side, near, True)
+                sides, _ = lax.optimization_barrier((sides, own_first))
+    else:
+        mine = stack_rows(sources, a_side, near)
+        theirs = swap(mine, "split", 1)
+        own_first = own_image(0, first, [mine], b_side, near, True)
+    after, _, _ = lax.optimization_barrier((first, far_sum, own_first))
+    own_first = own_image(0, after, [theirs], b_side, near, False, [own_first])
     after, _ = lax.optimization_barrier((first, own_first))
     own_second = own_image(1, after, [mine], b_side, near, True)
     own_first, own_second = lax.optimization_barrier((own_first, own_second))

time: 80.9 us -> 80.3 us (level)
  starting transfers between devices: 23.8 us -> 22.2 us
  waiting for transfers between devices: 15.3 us -> 16.2 us
    ppermute x23, starting transfers between devices: 21.7 us -> 20.3 us  [swap(): return lax.ppermute(value, axis, [(at, at ^ bits) for at in range(size)])]
    ppermute x23, waiting for transfers between devices: 12.9 us -> 13.9 us  [swap(): return lax.ppermute(value, axis, [(at, at ^ bits) for at in range(size)])]
    pallas_call x3 -> x4, Pallas kernels: 8.05 us -> 8.19 us  [own_image(): pl.pallas_call(functools.partial(own_kernel, near, part, diagonal, len(st...]
  transfers between devices with their start and end apart: 24 -> 24, of which waited for: 14 -> 13; matrix products, arithmetic and copies ran while one was open for 0% -> 0% of each run, Pallas kernels for 28% -> 29%
where the time goes in v7:
time: 80.3 us; the launch traced here: 80.1 us
  Pallas kernels  39.1 us (49%)
  starting transfers between devices  22.2 us (28%)
  waiting for transfers between devices  16.2 us (20%)
  other arithmetic  1.44 us (2%)
  between operations  1.1 us (1%)
    ppermute x23, starting transfers between devices, swap(): return lax.ppermute(value, axis, [(at, at ^ bits) for at in range(size)])  20.3 us
    ppermute x23, waiting for transfers between devices, swap(): return lax.ppermute(value, axis, [(at, at ^ bits) for at in range(size)])  13.9 us
    pallas_call x1, Pallas kernels, solve(): pl.pallas_call(functools.partial(solve_kernel, columns, 32), in_specs=[SM...  11.6 us
    pallas_call x8, Pallas kernels, image_part(): pl.pallas_call(functools.partial(image_kernel, range(len(densities)), slo...  8.52 us
    pallas_call x4, Pallas kernels, own_image(): pl.pallas_call(functools.partial(own_kernel, near, part, diagonal, len(st...  8.19 us
    pallas_call x1, Pallas kernels, geometry(): pl.pallas_call(functools.partial(geometry_kernel, scale, near), grid_spec...  4.88 us
    ppermute x1, waiting for transfers between devices, pair_swap(): return lax.ppermute(value, ('tri', 'rhs'), perm)  2.29 us
    pallas_call x1, Pallas kernels, finish(): pl.pallas_call(functools.partial(finish_kernel, ranks, chunks), in_specs=...  2.28 us
  transfers between devices with their start and end apart: 24, of which 13 were waited for; matrix products, arithmetic and copies ran while one was open for 0% of the time, Pallas kernels for 29%

profile of v7, /device:TPU:0, one launch (start us, length us, event | category | flops | bytes accessed | tf_op | source)
XLA Modules:
  0.0 80.1 jit_solution(13881603479811989292)
XLA Ops:
  0.7 1.2 %fusion = (bf16[128,1024]{1,0:T(8,128)(2,1)S(1)}, f32[128,1024]{1,0:T(8,128)S(1)}) fusion(f32[128,1024]{1,0:T(8,128)} %param.5, s32[1024]{0:T(1024)S(1)} %iota_add_fusion, s32[128]{0:T(128)} %param.6), kind=kLoop, calls=%fused_computation.6 | loop fusion | flops 524288 | bytes 1315328 | tf_op jit(solution)/shard_map/convert_element_type | solution.py:645
  1.9 3.0 %collective-permute-start.2 = (f32[128,1024]{1,0:T(8,128)S(1)}, f32[128,1024]{1,0:T(8,128)S(1)}, u32[]{:S(2)}, u32[]{:S(2)}) collective-permute-start(f32[128,1024]{1,0:T(8,128)S(1)} %get-tuple-element.92.refs_0_), channel_id=1, source_target_pairs={{0,2},{2,0},{1,3},{3,1},{4,6},{6,4},{5,7},{7,5},{8,10},{10,8},{9,1... | collective-permute-start | bytes 1572872 | tf_op jit(solution)/shard_map/ppermute | solution.py:603
  5.0 1.5 %collective-permute-start.4 = (bf16[128,1024]{1,0:T(8,128)(2,1)S(1)}, bf16[128,1024]{1,0:T(8,128)(2,1)S(1)}, u32[]{:S(2)}, u32[]{:S(2)}) collective-permute-start(bf16[128,1024]{1,0:T(8,128)(2,1)S(1)} %get-tuple-element.83.refs_0_), channel_id=1, source_target_pairs={{0,4},{4,0},{8,12},{12,8},{16,20},{20,16},{24,28},{28,24},{1,5},{5... | collective-permute-start | bytes 786440 | tf_op jit(solution)/shard_map/ppermute | solution.py:603
  6.4 1.6 %collective-permute-start.3 = (bf16[128,1024]{1,0:T(8,128)(2,1)S(1)}, bf16[128,1024]{1,0:T(8,128)(2,1)S(1)}, u32[]{:S(2)}, u32[]{:S(2)}) collective-permute-start(bf16[128,1024]{1,0:T(8,128)(2,1)S(1)} %get-tuple-element.83.refs_0_), channel_id=1, source_target_pairs={{0,8},{4,12},{8,0},{12,4},{16,24},{20,28},{24,16},{28,20},{1,9},{5... | collective-permute-start | bytes 786440 | tf_op jit(solution)/shard_map/ppermute | solution.py:603
  8.0 0.4 collective-permute-start
  8.8 4.9 %geometry.1 = (bf16[4,32,1024]{2,1,0:T(8,128)(2,1)S(1)}, bf16[2,32,1024]{2,1,0:T(8,128)(2,1)S(1)}, f32[1,1024]{1,0:T(1,128)S(1)}) custom-call(s32[5]{0:T(128)S(1)} %stack.80.blocks_ref, f32[3,8192]{1,0:T(4,128)S(1)} %copy-done.1, s32[3,16384]{1,0:T(4,128)S(1)} %copy-done, s32[1,16384]{1,0:T(1,128)S(1)} %bitcast.21), custom_call_target="tpu_custom_call" | custom-call | tf_op jit(solution)/shard_map/geometry/pallas_call | solution.py:136
  13.7 1.1 %image_part.8.refs_5_ = f32[128,1024]{1,0:T(8,128)S(1)} custom-call(s32[1]{0:T(128)} %bitcast.5.first_ref, bf16[128,1024]{1,0:T(8,128)(2,1)S(1)} %get-tuple-element.83.refs_0_, bf16[4,32,1024]{2,1,0:T(8,128)(2,1)S(1)} %get-tuple-element.86.refs_1_.refs_4_, bf16[2,32,1024]{2,1,0:T(8,128)(2,1)S(1)} %get-tuple-element.87.refs_2_.b_ref), custom_call_target="tpu_custom_call" | custom-call | flops 1024 | bytes 1024 | tf_op jit(solution)/shard_map/image_part/pallas_call | solution.py:200
  15.1 1.0 %image_part.9.refs_4_ = f32[128,1024]{1,0:T(8,128)S(1)} custom-call(s32[1]{0:T(128)} %bitcast.5.first_ref, bf16[128,1024]{1,0:T(8,128)(2,1)S(1)} %get-tuple-element.83.refs_0_, bf16[4,32,1024]{2,1,0:T(8,128)(2,1)S(1)} %get-tuple-element.86.refs_1_.refs_4_, bf16[2,32,1024]{2,1,0:T(8,128)(2,1)S(1)} %get-tuple-element.87.refs_2_.b_ref, ...), custom_call_target="tpu_custom_call" | custom-call | flops 1024 | bytes 1024 | tf_op jit(solution)/shard_map/image_part/pallas_call | solution.py:200
  16.1 2.0 %image_part.10 = (f32[128,1024]{1,0:T(8,128)S(1)}, f32[128,1024]{1,0:T(8,128)S(1)}) custom-call(s32[1]{0:T(128)} %bitcast.5.first_ref, bf16[128,1024]{1,0:T(8,128)(2,1)S(1)} %collective-permute-done.4.refs_0_.refs_1_, bf16[4,32,1024]{2,1,0:T(8,128)(2,1)S(1)} %get-tuple-element.86.refs_1_.refs_4_, bf16[2,32,1024]{2,1,0:T(8,128)(2,1)S(1)} %get-tuple-element.87.refs_2_.b_ref, ...), custom_call_target="tpu_custom_call" | custom-call | flops 1024 | bytes 1024 | tf_op jit(solution)/shard_map/image_part/pallas_call | solution.py:200
  18.1 1.9 %image_part.11 = (f32[128,1024]{1,0:T(8,128)S(1)}, f32[128,1024]{1,0:T(8,128)S(1)}) custom-call(s32[1]{0:T(128)} %bitcast.5.first_ref, bf16[128,1024]{1,0:T(8,128)(2,1)S(1)} %collective-permute-done.3.refs_0_.refs_2_, bf16[4,32,1024]{2,1,0:T(8,128)(2,1)S(1)} %get-tuple-element.86.refs_1_.refs_4_, bf16[2,32,1024]{2,1,0:T(8,128)(2,1)S(1)} %get-tuple-element.87.refs_2_.b_ref, ...), custom_call_target="tpu_custom_call" | custom-call | flops 1024 | bytes 1024 | tf_op jit(solution)/shard_map/image_part/pallas_call | solution.py:200
  20.1 0.6 image_part.12
  20.7 0.3 collective-permute-start.5
  21.0 0.6 image_part.13
  21.7 0.5 collective-permute-done.5.refs_4_
  22.1 0.6 image_part.14
  22.9 0.3 collective-permute-start.7
  23.2 0.3 collective-permute-start.6
  23.4 2.6 %collective-permute-start.8 = (bf16[128,512]{1,0:T(8,128)(2,1)S(1)}, bf16[128,512]{1,0:T(8,128)(2,1)S(1)}, u32[]{:S(2)}, u32[]{:S(2)}) collective-permute-start(bf16[128,512]{1,0:T(8,128)(2,1)S(1)} %image_part.14), channel_id=1, source_target_pairs={{0,16},{4,20},{8,24},{12,28},{16,0},{20,4},{24,8},{28,12},{1,17},{... | collective-permute-start | bytes 393224 | tf_op jit(solution)/shard_map/ppermute | solution.py:603
  26.0 2.0 %own_image.4.refs_1_ = f32[128,512]{1,0:T(8,128)S(1)} custom-call(s32[1]{0:T(128)} %bitcast.5.first_ref, bf16[2,32,1024]{2,1,0:T(8,128)(2,1)S(1)} %get-tuple-element.87.refs_2_.b_ref, bf16[640,1024]{1,0:T(8,128)(2,1)S(1)} %stack_rows.1.refs_0_), custom_call_target="tpu_custom_call" | custom-call | flops 1024 | bytes 1024 | tf_op jit(solution)/shard_map/own_image/pallas_call | solution.py:263
  28.1 0.6 image_part.15
  28.7 0.7 collective-permute-start.9
  29.5 2.0 %own_image.5.refs_0_ = f32[128,512]{1,0:T(8,128)S(1)} custom-call(s32[1]{0:T(128)} %bitcast.5.first_ref, bf16[2,32,1024]{2,1,0:T(8,128)(2,1)S(1)} %get-tuple-element.87.refs_2_.b_ref, bf16[640,1024]{1,0:T(8,128)(2,1)S(1)} %collective-permute-done.7.refs_0_, f32[128,512]{1,0:T(8,128)S(1)} %own_image.4.refs_1_), custom_call_target="tpu_custom_call" | custom-call | flops 1024 | bytes 1024 | tf_op jit(solution)/shard_map/own_image/pallas_call | solution.py:263
  31.5 2.0 %own_image.6.refs_1_ = f32[128,512]{1,0:T(8,128)S(1)} custom-call(s32[1]{0:T(128)} %bitcast.5.first_ref, bf16[2,32,1024]{2,1,0:T(8,128)(2,1)S(1)} %get-tuple-element.87.refs_2_.b_ref, bf16[640,1024]{1,0:T(8,128)(2,1)S(1)} %stack_rows.1.refs_0_), custom_call_target="tpu_custom_call" | custom-call | flops 1024 | bytes 1024 | tf_op jit(solution)/shard_map/own_image/pallas_call | solution.py:263
  33.5 0.6 collective-permute-start.10
  34.1 2.2 %own_image.7.refs_2_ = f32[128,512]{1,0:T(8,128)S(1)} custom-call(s32[1]{0:T(128)} %bitcast.5.first_ref, bf16[2,32,1024]{2,1,0:T(8,128)(2,1)S(1)} %get-tuple-element.87.refs_2_.b_ref, bf16[640,1024]{1,0:T(8,128)(2,1)S(1)} %collective-permute-done.7.refs_0_, f32[128,512]{1,0:T(8,128)S(1)} %own_image.6.refs_1_), custom_call_target="tpu_custom_call" | custom-call | flops 1024 | bytes 1024 | tf_op jit(solution)/shard_map/own_image/pallas_call | solution.py:263
  36.3 2.1 %collective-permute-done.9.refs_3_ = bf16[128,512]{1,0:T(8,128)(2,1)S(1)} collective-permute-done((bf16[128,512]{1,0:T(8,128)(2,1)S(1)}, bf16[128,512]{1,0:T(8,128)(2,1)S(1)}, u32[]{:S(2)}, u32[]{:S(2)}) %collective-permute-start.9) | collective-permute-done | bytes 131104 | tf_op jit(solution)/shard_map/ppermute | solution.py:603
  38.4 2.0 %gram.1 = (f32[2,320,128]{2,1,0:T(8,128)S(1)}, f32[128,1024]{1,0:T(8,128)S(1)}, bf16[128,512]{1,0:T(8,128)(2,1)S(1)}) custom-call(s32[2]{0:T(128)S(1)} %pad_add_fusion.place_ref, s32[1]{0:T(128)} %bitcast.5.first_ref, f32[1,1024]{1,0:T(1,128)S(1)} %get-tuple-element.62.diag_ref, f32[128,512]{1,0:T(8,128)S(1)} %get-tuple-element.91.first_half, ...), custom_call_target="tpu_custom_call" | custom-call | flops 1024 | bytes 1024 | tf_op jit(solution)/shard_map/gram/pallas_call | solution.py:340
  40.4 0.9 %cross.1 = (f32[160,256]{1,0:T(8,128)S(1)}, f32[160,256]{1,0:T(8,128)S(1)}) custom-call(s32[2]{0:T(128)S(1)} %pad_add_fusion.place_ref, s32[4]{0:T(128)S(1)} %pad_add_fusion.1.cut_ref, f32[2,320,128]{2,1,0:T(8,128)S(1)} %get-tuple-element.97.block_ref, f32[128,1024]{1,0:T(8,128)S(1)} %get-tuple-element.98.image_ref.refs_2_, ...), custom_call_target="tpu_custom_call" | custom-call | flops 1024 | bytes 1024 | tf_op jit(solution)/shard_map/cross/pallas_call | solution.py:382
  41.4 1.4 %collective-permute-done.11 = f32[160,256]{1,0:T(8,128)S(1)} collective-permute-done((f32[160,256]{1,0:T(8,128)S(1)}, f32[160,256]{1,0:T(8,128)S(1)}, u32[]{:S(2)}, u32[]{:S(2)}) %collective-permute-start.11) | collective-permute-done | bytes 163872 | tf_op jit(solution)/shard_map/ppermute | solution.py:603
  42.8 1.6 %collective-permute-start.12 = (f32[80,256]{1,0:T(8,128)S(1)}, f32[80,256]{1,0:T(8,128)S(1)}, u32[]{:S(2)}, u32[]{:S(2)}) collective-permute-start(f32[80,256]{1,0:T(8,128)S(1)} %split.9), channel_id=1, source_target_pairs={{0,4},{4,0},{8,12},{12,8},{16,20},{20,16},{24,28},{28,24},{1,5},{5... | collective-permute-start | bytes 245768 | tf_op jit(solution)/shard_map/ppermute | solution.py:603
  44.4 0.5 collective-permute-start.16
  44.9 2.5 %collective-permute-done.12 = f32[80,256]{1,0:T(8,128)S(1)} collective-permute-done((f32[80,256]{1,0:T(8,128)S(1)}, f32[80,256]{1,0:T(8,128)S(1)}, u32[]{:S(2)}, u32[]{:S(2)}) %collective-permute-start.12) | collective-permute-done | bytes 81952 | tf_op jit(solution)/shard_map/ppermute | solution.py:603
  47.4 4.3 %collective-permute-start.15 = (f32[80,256]{1,0:T(8,128)S(1)}, f32[80,256]{1,0:T(8,128)S(1)}, u32[]{:S(2)}, u32[]{:S(2)}) collective-permute-start(f32[80,256]{1,0:T(8,128)S(1)} %slice_add_fusion), channel_id=1, source_target_pairs={{0,24},{4,28},{8,16},{12,20},{16,8},{20,12},{24,0},{28,4},{1,25},{... | collective-permute-start | bytes 245768 | tf_op jit(solution)/shard_map/ppermute | solution.py:603
  51.7 0.6 collective-permute-start.13
  52.3 0.6 other_images.1.refs_3_
  53.0 1.7 %collective-permute-done.15 = f32[80,256]{1,0:T(8,128)S(1)} collective-permute-done((f32[80,256]{1,0:T(8,128)S(1)}, f32[80,256]{1,0:T(8,128)S(1)}, u32[]{:S(2)}, u32[]{:S(2)}) %collective-permute-start.15) | collective-permute-done | bytes 81952 | tf_op jit(solution)/shard_map/ppermute | solution.py:603
  54.7 3.3 %collective-permute-done.14 = f32[80,256]{1,0:T(8,128)S(1)} collective-permute-done((f32[80,256]{1,0:T(8,128)S(1)}, f32[80,256]{1,0:T(8,128)S(1)}, u32[]{:S(2)}, u32[]{:S(2)}) %collective-permute-start.14) | collective-permute-done | bytes 81952 | tf_op jit(solution)/shard_map/ppermute | solution.py:603
  58.0 1.8 %collective-permute-start.19 = (f32[80,256]{1,0:T(8,128)S(1)}, f32[80,256]{1,0:T(8,128)S(1)}, u32[]{:S(2)}, u32[]{:S(2)}) collective-permute-start(f32[80,256]{1,0:T(8,128)S(1)} %add_add_fusion.refs_0_), channel_id=1, source_target_pairs={{0,6},{2,4},{4,2},{6,0},{8,14},{10,12},{12,10},{14,8},{16,22},{18,... | collective-permute-start | bytes 245768 | tf_op jit(solution)/shard_map/ppermute | solution.py:616
  59.8 0.5 collective-permute-start.18
  60.4 1.2 %collective-permute-start.17 = (f32[80,256]{1,0:T(8,128)S(1)}, f32[80,256]{1,0:T(8,128)S(1)}, u32[]{:S(2)}, u32[]{:S(2)}) collective-permute-start(f32[80,256]{1,0:T(8,128)S(1)} %add_add_fusion.refs_0_), channel_id=1, source_target_pairs={{0,2},{2,0},{1,3},{3,1},{4,6},{6,4},{5,7},{7,5},{8,10},{10,8},{9,1... | collective-permute-start | bytes 245768 | tf_op jit(solution)/shard_map/ppermute | solution.py:603
  61.6 2.3 %collective-permute-done.19.refs_3_ = f32[80,256]{1,0:T(8,128)S(1)} collective-permute-done((f32[80,256]{1,0:T(8,128)S(1)}, f32[80,256]{1,0:T(8,128)S(1)}, u32[]{:S(2)}, u32[]{:S(2)}) %collective-permute-start.19) | collective-permute-done | bytes 81952 | tf_op jit(solution)/shard_map/ppermute | solution.py:616
  63.9 0.4 collective-permute-done.18.refs_2_
  64.4 0.4 collective-permute-done.17.refs_1_
  64.8 0.3 collective-permute-done.23.refs_7_
  65.2 0.4 collective-permute-done.22.refs_6_
  65.6 0.5 collective-permute-done.21.refs_5_
  66.1 11.6 %solve.1 = (f32[128,256]{1,0:T(8,128)S(1)}, f32[128,256]{1,0:T(8,128)S(1)}) custom-call(s32[2]{0:T(128)S(1)} %pad_add_fusion.place_ref, s32[8]{0:T(128)S(1)} %stack.99.share_ref, f32[80,256]{1,0:T(8,128)S(1)} %add_add_fusion.refs_0_, f32[80,256]{1,0:T(8,128)S(1)} %collective-permute-done.17.refs_1_, f32[80,256]{1,0:T(8,128)S(1)} %collective-permute-done.18.refs_2_, ...), custom_call_target="tpu_custom_call" | custom-call | tf_op jit(solution)/shard_map/solve/pallas_call | solution.py:505
  77.7 2.3 %finish.1 = (f32[128,1024]{1,0:T(8,128)}, f32[128,1024]{1,0:T(8,128)}, f32[128,1024]{1,0:T(8,128)}) custom-call(s32[2]{0:T(128)S(1)} %pad_add_fusion.place_ref, f32[128,256]{1,0:T(8,128)S(1)} %get-tuple-element.106.step_ref, f32[128,256]{1,0:T(8,128)S(1)} %get-tuple-element.107.turn_ref, f32[128,1024]{1,0:T(8,128)S(1)} %get-tuple-element.92.refs_0_, ...), custom_call_target="tpu_custom_call" | custom-call | flops 1024 | bytes 1024 | tf_op jit(solution)/shard_map/finish/pallas_call | solution.py:587
  (36 shorter events, 1.1 us)
Async XLA Ops:
  0.6 8.1 %copy-start.1 = (f32[3,8192]{1,0:T(4,128)S(1)}, f32[3,8192]{1,0:T(4,128)}, u32[]{:S(2)}) copy-start(f32[3,8192]{1,0:T(4,128)} %vertices_ref) | copy-start | bytes 294916
  0.6 8.1 %copy-start.2 = (s32[16384]{0:T(1024)S(1)}, s32[16384]{0:T(1024)}, u32[]{:S(2)}) copy-start(s32[16384]{0:T(1024)} %param.9) | copy-start | bytes 196612
  0.7 8.1 %copy-start = (s32[3,16384]{1,0:T(4,128)S(1)}, s32[3,16384]{1,0:T(4,128)}, u32[]{:S(2)}) copy-start(s32[3,16384]{1,0:T(4,128)} %corners_ref.1) | copy-start | bytes 589828
  1.9 18.2 %collective-permute-start.2 = (f32[128,1024]{1,0:T(8,128)S(1)}, f32[128,1024]{1,0:T(8,128)S(1)}, u32[]{:S(2)}, u32[]{:S(2)}) collective-permute-start(f32[128,1024]{1,0:T(8,128)S(1)} %get-tuple-element.92.refs_0_), channel_id=1, source_target_pairs={{0,2},{2,0},{1,3},{3,1},{4,6},{6,4},{5,7},{7,5},{8,10},{10,8},{9,1... | collective-permute-start | bytes 1572872 | tf_op jit(solution)/shard_map/ppermute | solution.py:603
  5.0 11.2 %collective-permute-start.4 = (bf16[128,1024]{1,0:T(8,128)(2,1)S(1)}, bf16[128,1024]{1,0:T(8,128)(2,1)S(1)}, u32[]{:S(2)}, u32[]{:S(2)}) collective-permute-start(bf16[128,1024]{1,0:T(8,128)(2,1)S(1)} %get-tuple-element.83.refs_0_), channel_id=1, source_target_pairs={{0,4},{4,0},{8,12},{12,8},{16,20},{20,16},{24,28},{28,24},{1,5},{5... | collective-permute-start | bytes 786440 | tf_op jit(solution)/shard_map/ppermute | solution.py:603
  6.4 11.7 %collective-permute-start.3 = (bf16[128,1024]{1,0:T(8,128)(2,1)S(1)}, bf16[128,1024]{1,0:T(8,128)(2,1)S(1)}, u32[]{:S(2)}, u32[]{:S(2)}) collective-permute-start(bf16[128,1024]{1,0:T(8,128)(2,1)S(1)} %get-tuple-element.83.refs_0_), channel_id=1, source_target_pairs={{0,8},{4,12},{8,0},{12,4},{16,24},{20,28},{24,16},{28,20},{1,9},{5... | collective-permute-start | bytes 786440 | tf_op jit(solution)/shard_map/ppermute | solution.py:603
  8.0 12.1 %collective-permute-start = (bf16[128,1024]{1,0:T(8,128)(2,1)S(1)}, bf16[128,1024]{1,0:T(8,128)(2,1)S(1)}, u32[]{:S(2)}, u32[]{:S(2)}) collective-permute-start(bf16[128,1024]{1,0:T(8,128)(2,1)S(1)} %get-tuple-element.83.refs_0_), channel_id=1, source_target_pairs={{0,12},{4,8},{8,4},{12,0},{16,28},{20,24},{24,20},{28,16},{1,13},{... | collective-permute-start | bytes 786440 | tf_op jit(solution)/shard_map/ppermute | solution.py:603
  13.7 1.4 %collective-permute-start.1 = (bf16[2,32,1024]{2,1,0:T(8,128)(2,1)S(1)}, bf16[2,32,1024]{2,1,0:T(8,128)(2,1)S(1)}, u32[]{:S(2)}, u32[]{:S(2)}) collective-permute-start(bf16[2,32,1024]{2,1,0:T(8,128)(2,1)S(1)} %get-tuple-element.87.refs_2_.b_ref), channel_id=1, source_target_pairs={{0,1},{1,0},{2,3},{3,2},{4,5},{5,4},{6,7},{7,6},{8,9},{9,8},{10,11... | collective-permute-start | bytes 393224 | tf_op jit(solution)/shard_map/ppermute | solution.py:603
  20.7 1.4 %collective-permute-start.5 = (bf16[128,512]{1,0:T(8,128)(2,1)S(1)}, bf16[128,512]{1,0:T(8,128)(2,1)S(1)}, u32[]{:S(2)}, u32[]{:S(2)}) collective-permute-start(bf16[128,512]{1,0:T(8,128)(2,1)S(1)} %image_part.12), channel_id=1, source_target_pairs={{0,1},{1,0},{2,3},{3,2},{4,5},{5,4},{6,7},{7,6},{8,9},{9,8},{10,11... | collective-permute-start | bytes 393224 | tf_op jit(solution)/shard_map/ppermute | solution.py:603
  22.9 6.6 %collective-permute-start.7 = (bf16[640,1024]{1,0:T(8,128)(2,1)S(1)}, bf16[640,1024]{1,0:T(8,128)(2,1)S(1)}, u32[]{:S(2)}, u32[]{:S(2)}) collective-permute-start(bf16[640,1024]{1,0:T(8,128)(2,1)S(1)} %stack_rows.1.refs_0_), channel_id=1, source_target_pairs={{0,1},{1,0},{2,3},{3,2},{4,5},{5,4},{6,7},{7,6},{8,9},{9,8},{10,11... | collective-permute-start | bytes 3932168 | tf_op jit(solution)/shard_map/ppermute | solution.py:603
  23.2 4.9 %collective-permute-start.6 = (bf16[128,512]{1,0:T(8,128)(2,1)S(1)}, bf16[128,512]{1,0:T(8,128)(2,1)S(1)}, u32[]{:S(2)}, u32[]{:S(2)}) collective-permute-start(bf16[128,512]{1,0:T(8,128)(2,1)S(1)} %image_part.13), channel_id=1, source_target_pairs={{0,1},{1,0},{2,3},{3,2},{4,5},{5,4},{6,7},{7,6},{8,9},{9,8},{10,11... | collective-permute-start | bytes 393224 | tf_op jit(solution)/shard_map/ppermute | solution.py:603
  23.4 10.0 %collective-permute-start.8 = (bf16[128,512]{1,0:T(8,128)(2,1)S(1)}, bf16[128,512]{1,0:T(8,128)(2,1)S(1)}, u32[]{:S(2)}, u32[]{:S(2)}) collective-permute-start(bf16[128,512]{1,0:T(8,128)(2,1)S(1)} %image_part.14), channel_id=1, source_target_pairs={{0,16},{4,20},{8,24},{12,28},{16,0},{20,4},{24,8},{28,12},{1,17},{... | collective-permute-start | bytes 393224 | tf_op jit(solution)/shard_map/ppermute | solution.py:603
  28.7 9.7 %collective-permute-start.9 = (bf16[128,512]{1,0:T(8,128)(2,1)S(1)}, bf16[128,512]{1,0:T(8,128)(2,1)S(1)}, u32[]{:S(2)}, u32[]{:S(2)}) collective-permute-start(bf16[128,512]{1,0:T(8,128)(2,1)S(1)} %image_part.15), channel_id=1, source_target_pairs={{0,16},{4,20},{8,24},{12,28},{16,0},{20,4},{24,8},{28,12},{1,17},{... | collective-permute-start | bytes 393224 | tf_op jit(solution)/shard_map/ppermute | solution.py:603
  33.5 6.8 %collective-permute-start.10 = (bf16[128,512]{1,0:T(8,128)(2,1)S(1)}, bf16[128,512]{1,0:T(8,128)(2,1)S(1)}, u32[]{:S(2)}, u32[]{:S(2)}) collective-permute-start(bf16[128,512]{1,0:T(8,128)(2,1)S(1)} %get-tuple-element.94), channel_id=1, source_target_pairs={{0,2},{2,0},{1,3},{3,1},{4,6},{6,4},{5,7},{7,5},{8,10},{10,8},{9,1... | collective-permute-start | bytes 393224 | tf_op jit(solution)/shard_map/ppermute | solution.py:603
  41.3 1.5 %collective-permute-start.11 = (f32[160,256]{1,0:T(8,128)S(1)}, f32[160,256]{1,0:T(8,128)S(1)}, u32[]{:S(2)}, u32[]{:S(2)}) collective-permute-start(f32[160,256]{1,0:T(8,128)S(1)} %get-tuple-element.100), channel_id=1, source_target_pairs={{0,1},{1,0},{2,3},{3,2},{4,5},{5,4},{6,7},{7,6},{8,9},{9,8},{10,11... | collective-permute-start | bytes 491528 | tf_op jit(solution)/shard_map/ppermute | solution.py:603
  42.8 4.6 %collective-permute-start.12 = (f32[80,256]{1,0:T(8,128)S(1)}, f32[80,256]{1,0:T(8,128)S(1)}, u32[]{:S(2)}, u32[]{:S(2)}) collective-permute-start(f32[80,256]{1,0:T(8,128)S(1)} %split.9), channel_id=1, source_target_pairs={{0,4},{4,0},{8,12},{12,8},{16,20},{20,16},{24,28},{28,24},{1,5},{5... | collective-permute-start | bytes 245768 | tf_op jit(solution)/shard_map/ppermute | solution.py:603
  44.4 8.0 %collective-permute-start.16 = (bf16[128,512]{1,0:T(8,128)(2,1)S(1)}, bf16[128,512]{1,0:T(8,128)(2,1)S(1)}, u32[]{:S(2)}, u32[]{:S(2)}) collective-permute-start(bf16[128,512]{1,0:T(8,128)(2,1)S(1)} %get-tuple-element.102), channel_id=1, source_target_pairs={{0,2},{2,0},{1,3},{3,1},{4,6},{6,4},{5,7},{7,5},{8,10},{10,8},{9,1... | collective-permute-start | bytes 393224 | tf_op jit(solution)/shard_map/ppermute | solution.py:603
  47.4 7.3 %collective-permute-start.15 = (f32[80,256]{1,0:T(8,128)S(1)}, f32[80,256]{1,0:T(8,128)S(1)}, u32[]{:S(2)}, u32[]{:S(2)}) collective-permute-start(f32[80,256]{1,0:T(8,128)S(1)} %slice_add_fusion), channel_id=1, source_target_pairs={{0,24},{4,28},{8,16},{12,20},{16,8},{20,12},{24,0},{28,4},{1,25},{... | collective-permute-start | bytes 245768 | tf_op jit(solution)/shard_map/ppermute | solution.py:603
  51.7 6.3 %collective-permute-start.14 = (f32[80,256]{1,0:T(8,128)S(1)}, f32[80,256]{1,0:T(8,128)S(1)}, u32[]{:S(2)}, u32[]{:S(2)}) collective-permute-start(f32[80,256]{1,0:T(8,128)S(1)} %slice_add_fusion), channel_id=1, source_target_pairs={{0,16},{4,20},{8,24},{12,28},{16,0},{20,4},{24,8},{28,12},{1,17},{... | collective-permute-start | bytes 245768 | tf_op jit(solution)/shard_map/ppermute | solution.py:603
  51.7 6.3 %collective-permute-start.13 = (f32[80,256]{1,0:T(8,128)S(1)}, f32[80,256]{1,0:T(8,128)S(1)}, u32[]{:S(2)}, u32[]{:S(2)}) collective-permute-start(f32[80,256]{1,0:T(8,128)S(1)} %slice_add_fusion), channel_id=1, source_target_pairs={{0,8},{4,12},{8,0},{12,4},{16,24},{20,28},{24,16},{28,20},{1,9},{5... | collective-permute-start | bytes 245768 | tf_op jit(solution)/shard_map/ppermute | solution.py:603
  58.0 5.9 %collective-permute-start.19 = (f32[80,256]{1,0:T(8,128)S(1)}, f32[80,256]{1,0:T(8,128)S(1)}, u32[]{:S(2)}, u32[]{:S(2)}) collective-permute-start(f32[80,256]{1,0:T(8,128)S(1)} %add_add_fusion.refs_0_), channel_id=1, source_target_pairs={{0,6},{2,4},{4,2},{6,0},{8,14},{10,12},{12,10},{14,8},{16,22},{18,... | collective-permute-start | bytes 245768 | tf_op jit(solution)/shard_map/ppermute | solution.py:616
  59.8 4.4 %collective-permute-start.18 = (f32[80,256]{1,0:T(8,128)S(1)}, f32[80,256]{1,0:T(8,128)S(1)}, u32[]{:S(2)}, u32[]{:S(2)}) collective-permute-start(f32[80,256]{1,0:T(8,128)S(1)} %add_add_fusion.refs_0_), channel_id=1, source_target_pairs={{0,4},{4,0},{8,12},{12,8},{16,20},{20,16},{24,28},{28,24},{1,5},{5... | collective-permute-start | bytes 245768 | tf_op jit(solution)/shard_map/ppermute | solution.py:603
  60.4 4.4 %collective-permute-start.17 = (f32[80,256]{1,0:T(8,128)S(1)}, f32[80,256]{1,0:T(8,128)S(1)}, u32[]{:S(2)}, u32[]{:S(2)}) collective-permute-start(f32[80,256]{1,0:T(8,128)S(1)} %add_add_fusion.refs_0_), channel_id=1, source_target_pairs={{0,2},{2,0},{1,3},{3,1},{4,6},{6,4},{5,7},{7,5},{8,10},{10,8},{9,1... | collective-permute-start | bytes 245768 | tf_op jit(solution)/shard_map/ppermute | solution.py:603
  61.6 3.2 %collective-permute-start.20 = (f32[80,256]{1,0:T(8,128)S(1)}, f32[80,256]{1,0:T(8,128)S(1)}, u32[]{:S(2)}, u32[]{:S(2)}) collective-permute-start(f32[80,256]{1,0:T(8,128)S(1)} %add_add_fusion.refs_0_), channel_id=1, source_target_pairs={{0,1},{1,0},{2,3},{3,2},{4,5},{5,4},{6,7},{7,6},{8,9},{9,8},{10,11... | collective-permute-start | bytes 245768 | tf_op jit(solution)/shard_map/ppermute | solution.py:603
  63.9 1.3 %collective-permute-start.23 = (f32[80,256]{1,0:T(8,128)S(1)}, f32[80,256]{1,0:T(8,128)S(1)}, u32[]{:S(2)}, u32[]{:S(2)}) collective-permute-start(f32[80,256]{1,0:T(8,128)S(1)} %collective-permute-done.19.refs_3_), channel_id=1, source_target_pairs={{0,1},{1,0},{2,3},{3,2},{4,5},{5,4},{6,7},{7,6},{8,9},{9,8},{10,11... | collective-permute-start | bytes 245768 | tf_op jit(solution)/shard_map/ppermute | solution.py:603
  64.3 1.3 %collective-permute-start.22 = (f32[80,256]{1,0:T(8,128)S(1)}, f32[80,256]{1,0:T(8,128)S(1)}, u32[]{:S(2)}, u32[]{:S(2)}) collective-permute-start(f32[80,256]{1,0:T(8,128)S(1)} %collective-permute-done.18.refs_2_), channel_id=1, source_target_pairs={{0,1},{1,0},{2,3},{3,2},{4,5},{5,4},{6,7},{7,6},{8,9},{9,8},{10,11... | collective-permute-start | bytes 245768 | tf_op jit(solution)/shard_map/ppermute | solution.py:603
  64.8 1.3 %collective-permute-start.21 = (f32[80,256]{1,0:T(8,128)S(1)}, f32[80,256]{1,0:T(8,128)S(1)}, u32[]{:S(2)}, u32[]{:S(2)}) collective-permute-start(f32[80,256]{1,0:T(8,128)S(1)} %collective-permute-done.17.refs_1_), channel_id=1, source_target_pairs={{0,1},{1,0},{2,3},{3,2},{4,5},{5,4},{6,7},{7,6},{8,9},{9,8},{10,11... | collective-permute-start | bytes 245768 | tf_op jit(solution)/shard_map/ppermute | solution.py:603
